TPU v7x, 512 devices: a whole 4x4x16 slice. The times are simulated.
512 devices in a mesh: gz: 64 (over z, x), strip: 8 (over y, core).
Axes of the slice: x: 4, y: 4, z: 16, core: 2. Of those that a mesh axis runs over, the one named last changes fastest.
Arguments:
- positions: float32 [64, 2, 256, 640], P('gz', None, 'strip'), may hold values from -3 to 3
- velocity: float32 [64, 2, 256, 640], P('gz', None, 'strip'), may hold values from -3.6 to 3.6
- flow_down: float32 [64, 2, 256, 640], P('gz', None, 'strip'), may hold values from 0 to 1
- flow_up: float32 [64, 2, 256, 640], P('gz', None, 'strip'), may hold values from 0 to 1
- flow_mask: int32 [2, 64, 256, 640], P(None, 'gz', 'strip'), may hold values 0 or 1
- resets: int32 [3, 64], P(None, 'gz'), may hold values 0 or 1
- dt_index: int32 [3], replicated, may hold values from 0 to 4
Outputs:
- final_positions: float32 [64, 2, 256, 640], P('gz', None, 'strip')
- final_velocity: float32 [64, 2, 256, 640], P('gz', None, 'strip')
All inputs are finite; a program needn't handle non-finite values. No bound on the sum of `flow_mask` or of `resets` on one device may be relied on, other than what follows from the above.
Results may differ from a plain program's by a relative error of at most 0.0003.
Values sent between devices are 32-bit elements; how exact they have to be, the bound alone decides.
No kernel may reach another device: no remote copies, remote signals or barrier semaphores. Data moves between devices by JAX's collectives and lax.ppermute only.
A program may use at most 64 MiB of HBM per device.

v0:
```python
import jax
import jax.numpy as jnp
from jax import lax
from jax.sharding import PartitionSpec as P

STEPS = 3


def extended(value, sides, width):
    for axis, dim in sides:
        peers, length = (lax.axis_size(axis), value.shape[dim])
        up = [(i, (i + 1) % peers) for i in range(peers - 1)]
        down = [(j, i) for i, j in up]
        last = lax.slice_in_dim(value, length - width, length, axis=dim)
        initial = lax.slice_in_dim(value, 0, width, axis=dim)
        before = lax.ppermute(last, axis, up)
        after = lax.ppermute(initial, axis, down)
        value = jnp.concatenate([before, value, after], axis=dim)
    return value


def shifted(value, axis, by):
    peers = lax.axis_size(axis)
    pairs = [(i, i + by) for i in range(peers) if 0 <= i + by < peers]
    return lax.ppermute(value, axis, pairs)


def shift_left(field):
    return jnp.concatenate([field[..., 1:], jnp.zeros_like(field[..., :1])], axis=-1)


def shift_right(field):
    return jnp.concatenate([jnp.zeros_like(field[..., :1]), field[..., :-1]], axis=-1)


def bilinear(block, flow):
    top = block[:, :, 1:-1]
    lower = block[:, :, 2:]
    frac_row = flow[:, 0:1]
    frac_col = flow[:, 1:2]
    upper_mix = (1.0 - frac_col) * top + frac_col * shift_left(top)
    lower_mix = (1.0 - frac_col) * lower + frac_col * shift_left(lower)
    return (1.0 - frac_row) * upper_mix + frac_row * lower_mix


def spring_force(padded, flow_down, flow_up, down_valid, up_valid, row_ids, nrows):
    field = padded[1:-1, :, 1:-1]
    north = padded[1:-1, :, :-2]
    south = padded[1:-1, :, 2:]
    cols = field.shape[-1]
    in_north = (row_ids > 0).astype(jnp.float32)[:, None]
    in_south = (row_ids < nrows - 1).astype(jnp.float32)[:, None]
    col_ids = jnp.arange(cols)
    in_west = (col_ids > 0).astype(jnp.float32)
    in_east = (col_ids < cols - 1).astype(jnp.float32)
    intra = in_north * (north - field) + in_south * (south - field)
    intra = intra + in_west * (shift_right(field) - field) + in_east * (shift_left(field) - field)
    towards_prev = down_valid * (flow_down + bilinear(padded[:-2], flow_down) - field)
    towards_next = up_valid * (flow_up + bilinear(padded[2:], flow_up) - field)
    return 1.0 * intra + 1.0 * (towards_prev + towards_next)


def ghost_field(field):
    rimmed = extended(field, (("strip", 2),), 1)
    before = shifted(rimmed, "gz", 1)
    after = shifted(rimmed, "gz", -1)
    return jnp.concatenate([before, rimmed, after], axis=0)


def local(positions, velocity, flow_down, flow_up, flow_mask, resets, dt_index):
    sec_local = positions.shape[0]
    rows = positions.shape[2]
    sections = sec_local * lax.axis_size("gz")
    nrows = rows * lax.axis_size("strip")
    sec_ids = lax.axis_index("gz") * sec_local + jnp.arange(sec_local)
    row_ids = lax.axis_index("strip") * rows + jnp.arange(rows)
    down_valid = (flow_mask[0] * (sec_ids > 0).astype(jnp.int32)[:, None, None]).astype(
        jnp.float32
    )[:, None]
    up_valid = (flow_mask[1] * (sec_ids < sections - 1).astype(jnp.int32)[:, None, None]).astype(
        jnp.float32
    )[:, None]
    field = positions
    speed = velocity
    alpha = jnp.full((sec_local,), 0.1, jnp.float32)
    for step in range(STEPS):
        padded = ghost_field(field)
        force = spring_force(padded, flow_down, flow_up, down_valid, up_valid, row_ids, nrows)
        dt = 0.1 * jnp.power(jnp.float32(1.25), dt_index[step].astype(jnp.float32))
        reset = resets[step] == 1
        alpha = jnp.where(reset, jnp.float32(0.1), 0.99 * alpha)
        factor = alpha[:, None, None, None]
        kicked = speed + dt * force
        force_sq = lax.psum(jnp.sum(force * force), ("gz", "strip"))
        kicked_sq = lax.psum(jnp.sum(kicked * kicked), ("gz", "strip"))
        mixed = (1.0 - factor) * kicked + factor * jnp.sqrt(kicked_sq / (force_sq + 1e-06)) * force
        speed = jnp.where(reset[:, None, None, None], jnp.zeros_like(mixed), mixed)
        field = field + dt * speed
    return (field, speed)


def solution(mesh):
    placed = (
        P("gz", None, "strip", None),
        P("gz", None, "strip", None),
        P("gz", None, "strip", None),
        P("gz", None, "strip", None),
        P(None, "gz", "strip", None),
        P(None, "gz"),
        P(),
    )
    return jax.shard_map(
        local,
        mesh=mesh,
        in_specs=placed,
        out_specs=(P("gz", None, "strip", None), P("gz", None, "strip", None)),
        check_vma=False,
    )
```

profile of v0, /device:TPU:1, one launch (start us, length us, event | category | flops | bytes accessed | tf_op | source)
XLA Modules:
  0.0 391.2 jit_solution(4093841873448863952)
XLA Ops:
  1.4 4.6 %collective-permute-start = (f32[1,2,1,640]{3,2,1,0:T(1,128)S(1)}, f32[1,2,1,640]{3,2,1,0:T(1,128)S(1)}, u32[]{:S(2)}, u32[]{:S(2)}) collective-permute-start(f32[1,2,1,640]{3,2,1,0:T(1,128)S(1)} %get-tuple-element.55), channel_id=1, source_target_pairs={{0,1},{1,2},{2,3},{3,4},{4,5},{5,6},{6,7},{8,9},{9,10},{10,11},{11... | collective-permute-start | bytes 15368 | tf_op jit(solution)/shard_map/ppermute | solution.py:16
  6.0 5.5 %collective-permute-start.1 = (f32[1,2,1,640]{3,2,1,0:T(1,128)S(1)}, f32[1,2,1,640]{3,2,1,0:T(1,128)S(1)}, u32[]{:S(2)}, u32[]{:S(2)}) collective-permute-start(f32[1,2,1,640]{3,2,1,0:T(1,128)S(1)} %get-tuple-element.56), channel_id=1, source_target_pairs={{1,0},{2,1},{3,2},{4,3},{5,4},{6,5},{7,6},{9,8},{10,9},{11,10},{12... | collective-permute-start | bytes 15368 | tf_op jit(solution)/shard_map/ppermute | solution.py:17
  11.6 1.1 fusion.90
  16.2 1.3 collective-permute-start.2
  17.5 1.3 collective-permute-start.3
  18.8 3.1 collective-permute-done.2
  22.1 4.1 %collective-permute-done.3 = f32[1,2,34,640]{3,2,1,0:T(8,128)S(1)} collective-permute-done((f32[1,2,34,640]{3,2,1,0:T(8,128)S(1)}, f32[1,2,34,640]{3,2,1,0:T(8,128)S(1)}, u32[]{:S(2)}, u32[]{:S(2)}) %collective-permute-start.3) | collective-permute-done | bytes 174112 | tf_op jit(solution)/shard_map/ppermute | solution.py:25
  27.4 109.4 %all-reduce.20 = (f32[]{:T(128)}, f32[]{:T(128)}) all-reduce(f32[]{:T(128)} %get-tuple-element.7, f32[]{:T(128)} %get-tuple-element.6), channel_id=1, replica_groups=mesh['gz'=64,'strip'=8] {'gz','strip'}, use_global_device_ids=true, to_apply=%region_1.2 | all-reduce | flops 2 | bytes 16 | tf_op jit(solution)/shard_map/psum | solution.py:95
  138.1 2.5 collective-permute-start.4
  140.7 1.9 collective-permute-start.5
  143.9 1.7 collective-permute-done.5
  145.6 1.8 collective-permute-start.6
  147.6 1.3 collective-permute-start.7
  148.8 2.2 collective-permute-done.6
  151.2 4.1 %collective-permute-done.7 = f32[1,2,34,640]{3,2,1,0:T(8,128)S(1)} collective-permute-done((f32[1,2,34,640]{3,2,1,0:T(8,128)S(1)}, f32[1,2,34,640]{3,2,1,0:T(8,128)S(1)}, u32[]{:S(2)}, u32[]{:S(2)}) %collective-permute-start.7) | collective-permute-done | bytes 174112 | tf_op jit(solution)/shard_map/ppermute | solution.py:25
  156.4 106.5 %all-reduce.19 = (f32[]{:T(128)}, f32[]{:T(128)}) all-reduce(f32[]{:T(128)} %get-tuple-element.5, f32[]{:T(128)} %get-tuple-element.4), channel_id=1, replica_groups=mesh['gz'=64,'strip'=8] {'gz','strip'}, use_global_device_ids=true, to_apply=%region_5.6 | all-reduce | flops 2 | bytes 16 | tf_op jit(solution)/shard_map/psum | solution.py:95
  264.4 2.4 collective-permute-start.8
  266.8 1.9 collective-permute-start.9
  270.1 1.6 collective-permute-done.9
  271.8 1.9 collective-permute-start.10
  273.8 1.3 collective-permute-start.11
  275.1 2.1 collective-permute-done.10
  277.3 4.1 %collective-permute-done.11 = f32[1,2,34,640]{3,2,1,0:T(8,128)S(1)} collective-permute-done((f32[1,2,34,640]{3,2,1,0:T(8,128)S(1)}, f32[1,2,34,640]{3,2,1,0:T(8,128)S(1)}, u32[]{:S(2)}, u32[]{:S(2)}) %collective-permute-start.11) | collective-permute-done | bytes 174112 | tf_op jit(solution)/shard_map/ppermute | solution.py:25
  282.5 106.6 %all-reduce.18 = (f32[]{:T(128)}, f32[]{:T(128)}) all-reduce(f32[]{:T(128)} %get-tuple-element.3, f32[]{:T(128)} %get-tuple-element.2), channel_id=1, replica_groups=mesh['gz'=64,'strip'=8] {'gz','strip'}, use_global_device_ids=true, to_apply=%region_9.10 | all-reduce | flops 2 | bytes 16 | tf_op jit(solution)/shard_map/psum | solution.py:95
  (44 shorter events, 7.9 us)
Async XLA Ops:
  1.4 14.6 %collective-permute-start = (f32[1,2,1,640]{3,2,1,0:T(1,128)S(1)}, f32[1,2,1,640]{3,2,1,0:T(1,128)S(1)}, u32[]{:S(2)}, u32[]{:S(2)}) collective-permute-start(f32[1,2,1,640]{3,2,1,0:T(1,128)S(1)} %get-tuple-element.55), channel_id=1, source_target_pairs={{0,1},{1,2},{2,3},{3,4},{4,5},{5,6},{6,7},{8,9},{9,10},{10,11},{11... | collective-permute-start | bytes 15368 | tf_op jit(solution)/shard_map/ppermute | solution.py:16
  6.0 10.1 %collective-permute-start.1 = (f32[1,2,1,640]{3,2,1,0:T(1,128)S(1)}, f32[1,2,1,640]{3,2,1,0:T(1,128)S(1)}, u32[]{:S(2)}, u32[]{:S(2)}) collective-permute-start(f32[1,2,1,640]{3,2,1,0:T(1,128)S(1)} %get-tuple-element.56), channel_id=1, source_target_pairs={{1,0},{2,1},{3,2},{4,3},{5,4},{6,5},{7,6},{9,8},{10,9},{11,10},{12... | collective-permute-start | bytes 15368 | tf_op jit(solution)/shard_map/ppermute | solution.py:17
  11.5 2.4 copy-start.6
  11.6 3.1 copy-start.1
  11.6 3.1 copy-start.2
  12.7 0.7 copy-start.5
  14.6 1.5 copy-start
  16.1 1.4 copy-start.4
  16.2 5.7 %collective-permute-start.2 = (f32[1,2,34,640]{3,2,1,0:T(8,128)S(1)}, f32[1,2,34,640]{3,2,1,0:T(8,128)S(1)}, u32[]{:S(2)}, u32[]{:S(2)}) collective-permute-start(f32[1,2,34,640]{3,2,1,0:T(8,128)S(1)} %pad_maximum_fusion), channel_id=1, source_target_pairs={{0,8},{8,16},{16,24},{24,32},{32,40},{40,48},{48,56},{56,64},{64,7... | collective-permute-start | bytes 522248 | tf_op jit(solution)/shard_map/ppermute | solution.py:25
  17.5 8.7 %collective-permute-start.3 = (f32[1,2,34,640]{3,2,1,0:T(8,128)S(1)}, f32[1,2,34,640]{3,2,1,0:T(8,128)S(1)}, u32[]{:S(2)}, u32[]{:S(2)}) collective-permute-start(f32[1,2,34,640]{3,2,1,0:T(8,128)S(1)} %pad_maximum_fusion), channel_id=1, source_target_pairs={{8,0},{16,8},{24,16},{32,24},{40,32},{48,40},{56,48},{64,56},{72,6... | collective-permute-start | bytes 522248 | tf_op jit(solution)/shard_map/ppermute | solution.py:25
  22.0 4.3 %copy-start.3 = (f32[1,2,32,640]{3,2,1,0:T(8,128)S(1)}, f32[1,2,32,640]{3,2,1,0:T(8,128)}, u32[]{:S(2)}) copy-start(f32[1,2,32,640]{3,2,1,0:T(8,128)} %param.8) | copy-start | bytes 491524
  138.1 5.8 %collective-permute-start.4 = (f32[1,2,1,640]{3,2,1,0:T(1,128)S(1)}, f32[1,2,1,640]{3,2,1,0:T(1,128)S(1)}, u32[]{:S(2)}, u32[]{:S(2)}) collective-permute-start(f32[1,2,1,640]{3,2,1,0:T(1,128)S(1)} %get-tuple-element.41), channel_id=1, source_target_pairs={{0,1},{1,2},{2,3},{3,4},{4,5},{5,6},{6,7},{8,9},{9,10},{10,11},{11... | collective-permute-start | bytes 15368 | tf_op jit(solution)/shard_map/ppermute | solution.py:16
  140.7 4.9 %collective-permute-start.5 = (f32[1,2,1,640]{3,2,1,0:T(1,128)S(1)}, f32[1,2,1,640]{3,2,1,0:T(1,128)S(1)}, u32[]{:S(2)}, u32[]{:S(2)}) collective-permute-start(f32[1,2,1,640]{3,2,1,0:T(1,128)S(1)} %get-tuple-element.42), channel_id=1, source_target_pairs={{1,0},{2,1},{3,2},{4,3},{5,4},{6,5},{7,6},{9,8},{10,9},{11,10},{12... | collective-permute-start | bytes 15368 | tf_op jit(solution)/shard_map/ppermute | solution.py:17
  145.6 5.4 %collective-permute-start.6 = (f32[1,2,34,640]{3,2,1,0:T(8,128)S(1)}, f32[1,2,34,640]{3,2,1,0:T(8,128)S(1)}, u32[]{:S(2)}, u32[]{:S(2)}) collective-permute-start(f32[1,2,34,640]{3,2,1,0:T(8,128)S(1)} %pad_maximum_fusion.1), channel_id=1, source_target_pairs={{0,8},{8,16},{16,24},{24,32},{32,40},{40,48},{48,56},{56,64},{64,7... | collective-permute-start | bytes 522248 | tf_op jit(solution)/shard_map/ppermute | solution.py:25
  147.6 7.7 %collective-permute-start.7 = (f32[1,2,34,640]{3,2,1,0:T(8,128)S(1)}, f32[1,2,34,640]{3,2,1,0:T(8,128)S(1)}, u32[]{:S(2)}, u32[]{:S(2)}) collective-permute-start(f32[1,2,34,640]{3,2,1,0:T(8,128)S(1)} %pad_maximum_fusion.1), channel_id=1, source_target_pairs={{8,0},{16,8},{24,16},{32,24},{40,32},{48,40},{56,48},{64,56},{72,6... | collective-permute-start | bytes 522248 | tf_op jit(solution)/shard_map/ppermute | solution.py:25
  264.4 5.8 %collective-permute-start.8 = (f32[1,2,1,640]{3,2,1,0:T(1,128)S(1)}, f32[1,2,1,640]{3,2,1,0:T(1,128)S(1)}, u32[]{:S(2)}, u32[]{:S(2)}) collective-permute-start(f32[1,2,1,640]{3,2,1,0:T(1,128)S(1)} %get-tuple-element.37), channel_id=1, source_target_pairs={{0,1},{1,2},{2,3},{3,4},{4,5},{5,6},{6,7},{8,9},{9,10},{10,11},{11... | collective-permute-start | bytes 15368 | tf_op jit(solution)/shard_map/ppermute | solution.py:16
  266.8 4.9 %collective-permute-start.9 = (f32[1,2,1,640]{3,2,1,0:T(1,128)S(1)}, f32[1,2,1,640]{3,2,1,0:T(1,128)S(1)}, u32[]{:S(2)}, u32[]{:S(2)}) collective-permute-start(f32[1,2,1,640]{3,2,1,0:T(1,128)S(1)} %get-tuple-element.38), channel_id=1, source_target_pairs={{1,0},{2,1},{3,2},{4,3},{5,4},{6,5},{7,6},{9,8},{10,9},{11,10},{12... | collective-permute-start | bytes 15368 | tf_op jit(solution)/shard_map/ppermute | solution.py:17
  271.8 5.4 %collective-permute-start.10 = (f32[1,2,34,640]{3,2,1,0:T(8,128)S(1)}, f32[1,2,34,640]{3,2,1,0:T(8,128)S(1)}, u32[]{:S(2)}, u32[]{:S(2)}) collective-permute-start(f32[1,2,34,640]{3,2,1,0:T(8,128)S(1)} %pad_maximum_fusion.2), channel_id=1, source_target_pairs={{0,8},{8,16},{16,24},{24,32},{32,40},{40,48},{48,56},{56,64},{64,7... | collective-permute-start | bytes 522248 | tf_op jit(solution)/shard_map/ppermute | solution.py:25
  273.8 7.6 %collective-permute-start.11 = (f32[1,2,34,640]{3,2,1,0:T(8,128)S(1)}, f32[1,2,34,640]{3,2,1,0:T(8,128)S(1)}, u32[]{:S(2)}, u32[]{:S(2)}) collective-permute-start(f32[1,2,34,640]{3,2,1,0:T(8,128)S(1)} %pad_maximum_fusion.2), channel_id=1, source_target_pairs={{8,0},{16,8},{24,16},{32,24},{40,32},{48,40},{56,48},{64,56},{72,6... | collective-permute-start | bytes 522248 | tf_op jit(solution)/shard_map/ppermute | solution.py:25
where the time goes:
time: 392 us; the launch traced here: 391 us
  blocking collectives  322 us (82%)
  starting transfers between devices  27.7 us (7%)
  waiting for transfers between devices  22.9 us (6%)
  between operations  9.05 us (2%)
  local copies, waits for them, and re-layouts  4.99 us (1%)
  other arithmetic  4.08 us (1%)
    psum x3, blocking collectives, local(): kicked_sq = lax.psum(jnp.sum(kicked * kicked), ('gz', 'strip'))  322 us
    ppermute x6, waiting for transfers between devices, shifted(): return lax.ppermute(value, axis, pairs)  19.6 us
    ppermute x3, starting transfers between devices, extended(): before = lax.ppermute(last, axis, up)  9.55 us
    ppermute x3, starting transfers between devices, extended(): after = lax.ppermute(initial, axis, down)  9.32 us
    ppermute x6, starting transfers between devices, shifted(): return lax.ppermute(value, axis, pairs)  8.85 us
  transfers between devices with their start and end apart: 12, of which 8 were waited for; matrix products, arithmetic and copies ran while one was open for 1% of the time, Pallas kernels for 0%

commit v1 on v0

v1 whole, which is shorter than its diff:
```python
import jax
import jax.numpy as jnp
from jax import lax
from jax.experimental import pallas as pl
from jax.experimental.pallas import tpu as pltpu
from jax.sharding import Mesh, PartitionSpec as P

GZ = ("z", "x")
X_CHIPS = 4
DEEP = 3
VMEM = pl.BlockSpec(memory_space=pltpu.VMEM)
SMEM = pl.BlockSpec(memory_space=pltpu.SMEM)
N_SUMS = 28


def exchange(value, axes, size):
    up = [(i, i + 1) for i in range(size - 1)]
    down = [(j, i) for i, j in up]
    return lax.ppermute(value, axes, up), lax.ppermute(value, axes, down)


class Stencil:
    def __init__(self, strip, nstrips, flow_down, flow_up, mask_down, mask_up):
        rows, cols = mask_down.shape
        own = rows - 8
        ring = lax.broadcasted_iota(jnp.int32, (rows, 1), 0)
        row = strip * own + jnp.where(ring < own + 4, ring, ring - rows)
        last = nstrips * own - 1
        self.north = jnp.where((row > 0) & (row <= last), 1.0, 0.0).astype(jnp.float32)
        self.south = jnp.where((row >= 0) & (row < last), 1.0, 0.0).astype(jnp.float32)
        col = lax.broadcasted_iota(jnp.int32, (1, cols), 1)
        self.west = jnp.where(col > 0, 1.0, 0.0).astype(jnp.float32)
        self.east = jnp.where(col < cols - 1, 1.0, 0.0).astype(jnp.float32)
        self.down = flow_down
        self.up = flow_up
        self.mask_down = mask_down
        self.mask_up = mask_up
        degree = (self.north + self.south) + (self.west + self.east)
        self.pull = degree + (mask_down + mask_up)
        self.rows, self.cols = rows, cols

    def below(self, value):
        return pltpu.roll(value, self.rows - 1, 0)

    def above(self, value):
        return pltpu.roll(value, 1, 0)

    def right(self, value):
        return pltpu.roll(value, self.cols - 1, 1) * self.east

    def left(self, value):
        return pltpu.roll(value, 1, 1) * self.west

    def sample(self, value, flow):
        step = self.right(value) - value
        here = value + flow[1] * step
        lower = self.below(value) + flow[1] * self.below(step)
        return here + flow[0] * (lower - here)

    def __call__(self, own, before, after):
        total = self.north * self.above(own) + self.south * self.below(own)
        total = total + (self.left(own) + self.right(own)) - self.pull * own
        total = total + self.mask_down * self.sample(before, self.down)
        return total + self.mask_up * self.sample(after, self.up)

    def bias(self, comp):
        return self.mask_down * self.down[comp] + self.mask_up * self.up[comp]


def stencil_of(ids, nstrips, fd, fu, mk):
    return Stencil(ids[0], nstrips, (fd[0], fd[1]), (fu[0], fu[1]), mk[0], mk[1])


def factors(reset, alpha):
    alpha = jnp.where(reset > 0.5, jnp.float32(0.1), 0.99 * alpha)
    keep = jnp.where(reset > 0.5, jnp.float32(0.0), jnp.float32(1.0))
    return alpha, (1.0 - alpha) * keep, alpha * keep


def resets_of(field):
    at = field.shape[1] - 5
    return field[0, at : at + 1], field[0, at + 1 : at + 2]


def after_first(u0, v0, f0, dt0, k0, g0):
    va = k0 * (v0 + dt0 * f0)
    vb = g0 * f0
    return va, vb, u0 + dt0 * va, dt0 * vb


def after_second(first, fa, fb, dt1, k1, g1):
    va, vb, ua, ub = first
    vel = (k1 * (va + dt1 * fa), k1 * (vb + dt1 * fb), g1 * fa, g1 * fb)
    return vel, (ua + dt1 * vel[0], ub + dt1 * vel[1], dt1 * vel[2], dt1 * vel[3])


def first_kernel(nstrips, ids, u, ub, ua, v, fd, fu, mk, out):
    op = stencil_of(ids, nstrips, fd, fu, mk)
    for c in range(2):
        out[c] = op(u[c], ub[c], ua[c]) + op.bias(c)
        out[2 + c] = v[c]


def second_kernel(nstrips, ids, dts, u, ub, ua, p, pb, pa, fd, fu, mk, out):
    op = stencil_of(ids, nstrips, fd, fu, mk)
    weights = [factors(resets_of(f)[0], jnp.float32(0.1)) for f in (u, ub, ua)]
    for c in range(2):
        parts = [
            after_first(f[c], q[2 + c], q[c], dts[0], k, g)
            for f, q, (_, k, g) in zip((u, ub, ua), (p, pb, pa), weights)
        ]
        out[c] = op(*[x[2] for x in parts]) + op.bias(c)
        out[2 + c] = op(*[x[3] for x in parts])


def products(fields):
    return [fields[i] * fields[j] for i in range(len(fields)) for j in range(i, len(fields))]


def tile_sum(value):
    rows = value.shape[0]
    tall = value[0:8]
    for r in range(8, rows, 8):
        tall = tall + value[r : r + 8]
    total = tall[:, 0:128]
    for col in range(128, value.shape[1], 128):
        total = total + tall[:, col : col + 128]
    return total


def third_kernel(nstrips, ids, dts, u, ub, ua, p, pb, pa, q, qb, qa, fd, fu, mk, out, sums):
    op = stencil_of(ids, nstrips, fd, fu, mk)
    rows = out.shape[1]
    dt0, dt1, dt2 = dts[0], dts[1], dts[2]
    weights = []
    for f in (u, ub, ua):
        r0, r1 = resets_of(f)
        alpha, k0, g0 = factors(r0, jnp.float32(0.1))
        _, k1, g1 = factors(r1, alpha)
        weights.append((k0, g0, k1, g1))
    totals = [None] * N_SUMS
    for c in range(2):
        sides = []
        for f, m, n, (k0, g0, k1, g1) in zip((u, ub, ua), (p, pb, pa), (q, qb, qa), weights):
            one = after_first(f[c], m[2 + c], m[c], dt0, k0, g0)
            sides.append((one, *after_second(one, n[c], n[2 + c], dt1, k1, g1)))
        forces = []
        for i in range(4):
            force = op(sides[0][2][i], sides[1][2][i], sides[2][2][i])
            if i == 0:
                force = force + op.bias(c)
            force = force[:rows]
            out[4 * c + i] = force
            forces.append(force)
        va, vb = sides[0][0][0][:rows], sides[0][0][1][:rows]
        f0, fa, fb = p[c, :rows], q[c, :rows], q[2 + c, :rows]
        kicked = [x[:rows] + dt2 * y for x, y in zip(sides[0][1], forces)]
        terms = products([f0]) + products([p[2 + c, :rows] + dt0 * f0])
        terms += products([fa, fb]) + products([va + dt1 * fa, vb + dt1 * fb])
        terms += products(forces) + products(kicked)
        for i, term in enumerate(terms):
            part = tile_sum(term)
            totals[i] = part if c == 0 else totals[i] + part
    lane = lax.broadcasted_iota(jnp.int32, (1, 128), 1)
    row = jnp.zeros((1, 128), jnp.float32)
    for i, total in enumerate(totals):
        whole = jnp.sum(jnp.sum(total, axis=0, keepdims=True), axis=1, keepdims=True)
        row = jnp.where(lane == i, whole, row)
    sums[...] = row


def form(sums, at, size, basis):
    total = None
    for i in range(size):
        for j in range(i, size):
            term = sums[:, at : at + 1]
            at += 1
            for b in basis[i] + basis[j]:
                term = term * b
            if i != j:
                term = 2.0 * term
            total = term if total is None else total + term
    return jnp.maximum(total, 0.0)


def ratio(kicked, force):
    return jnp.sqrt(kicked / (force + 1e-06))


def last_kernel(dts, rs, parts, u, p, q, f2, pos, vel):
    rows = pos.shape[1]
    sums = jnp.sum(parts[...], axis=0)
    c0 = ratio(jnp.maximum(sums[:, 1:2], 0.0), sums[:, 0:1])
    one = ((), (c0,))
    c1 = ratio(form(sums, 5, 2, one), form(sums, 2, 2, one))
    two = ((), (c0,), (c1,), (c0, c1))
    c2 = ratio(form(sums, 18, 4, two), form(sums, 8, 4, two))
    alpha = jnp.float32(0.1)
    weights = []
    for i in range(3):
        alpha = jnp.where(rs[i] == 1, jnp.float32(0.1), 0.99 * alpha)
        keep = jnp.where(rs[i] == 1, jnp.float32(0.0), jnp.float32(1.0))
        weights.append(((1.0 - alpha) * keep, alpha * keep))
    for c in range(2):
        f = f2[4 * c] + c0 * f2[4 * c + 1] + c1 * (f2[4 * c + 2] + c0 * f2[4 * c + 3])
        field, speed = u[c, :rows], p[2 + c, :rows]
        forces = (p[c, :rows], q[c, :rows] + c0 * q[2 + c, :rows], f)
        for i, (force, factor) in enumerate(zip(forces, (c0, c1, c2))):
            keep, mix = weights[i]
            speed = keep * (speed + dts[i] * force) + (mix * factor) * force
            field = field + dts[i] * speed
        pos[c] = field
        vel[c] = speed


def call(kernel, out_shape, specs, *args):
    return pl.pallas_call(
        kernel,
        out_shape=out_shape,
        in_specs=specs,
        out_specs=jax.tree.map(lambda _: VMEM, out_shape),
        compiler_params=pltpu.CompilerParams(vmem_limit_bytes=40 * 2**20),
    )(*args)


def f32(*shape):
    return jax.ShapeDtypeStruct(shape, jnp.float32)


def local(positions, velocity, flow_down, flow_up, flow_mask, resets, dt_index):
    nstrips, nz, nx = lax.axis_size("strip"), lax.axis_size("z"), lax.axis_size("x")
    section = lax.axis_index(GZ)
    _, comps, rows, cols = positions.shape
    ring = rows + 8
    valid = jnp.stack([section > 0, section < nz * nx - 1]).astype(jnp.int32)
    masks = (flow_mask[:, 0] * valid[:, None, None]).astype(jnp.float32)
    dts = 0.1 * jnp.power(jnp.float32(1.25), dt_index.astype(jnp.float32))
    ids = jnp.reshape(lax.axis_index("strip"), (1,))
    resets = resets[:, 0]
    fields = [positions[0], velocity[0], flow_down[0], flow_up[0], masks]
    deep = [DEEP] + [DEEP - 1] * 4

    def packed(cut):
        slabs = [cut(f, d).reshape(-1, cols) for f, d in zip(fields, deep)]
        return jnp.concatenate(slabs + [jnp.zeros((2, cols), jnp.float32)], axis=0)

    from_above = packed(lambda f, d: f[:, rows - d :])
    from_below = packed(lambda f, d: f[:, :d])
    above = lax.ppermute(from_above, "strip", [(i, i + 1) for i in range(nstrips - 1)])
    below = lax.ppermute(from_below, "strip", [(i + 1, i) for i in range(nstrips - 1)])
    marks = (resets[:2] == 1).astype(jnp.float32)
    wide, at = [], 0
    for f, d in zip(fields, deep):
        lower = below[at : at + 2 * d].reshape(2, d, cols)
        upper = above[at : at + 2 * d].reshape(2, d, cols)
        at += 2 * d
        if d == DEEP:
            gap = jnp.broadcast_to(marks[None, :, None], (2, 2, cols))
        else:
            gap = jnp.zeros((2, 8 - 2 * d, cols), jnp.float32)
        wide.append(jnp.concatenate([f, lower, gap, upper], axis=1))
    u, v, fd, fu, mk = wide

    ub, ua = exchange(u, GZ, nz * nx)
    p = call(
        lambda *refs: first_kernel(nstrips, *refs),
        f32(4, ring, cols),
        [SMEM] + [VMEM] * 7,
        ids, u, ub, ua, v, fd, fu, mk,
    )
    pb, pa = exchange(p, GZ, nz * nx)
    q = call(
        lambda *refs: second_kernel(nstrips, *refs),
        f32(4, ring, cols),
        [SMEM] * 2 + [VMEM] * 9,
        ids, dts, u, ub, ua, p, pb, pa, fd, fu, mk,
    )
    qb, qa = exchange(q, GZ, nz * nx)
    f2, sums = call(
        lambda *refs: third_kernel(nstrips, *refs),
        (f32(8, rows, cols), f32(1, 128)),
        [SMEM] * 2 + [VMEM] * 12,
        ids, dts, u, ub, ua, p, pb, pa, q, qb, qa, fd, fu, mk,
    )
    near = nx * nstrips
    sums = lax.all_to_all(jnp.broadcast_to(sums, (near, 1, 128)), ("x", "strip"), 0, 0)
    sums = jnp.sum(sums, axis=0)
    sums = lax.all_to_all(jnp.broadcast_to(sums, (nz, 1, 128)), "z", 0, 0)
    pos, vel = call(
        last_kernel,
        (f32(comps, rows, cols), f32(comps, rows, cols)),
        [SMEM] * 2 + [VMEM] * 5,
        dts, resets, sums, u, p, q, f2,
    )
    return pos[None], vel[None]


def solution(mesh):
    sections, strips = mesh.devices.shape
    split = mesh.devices.reshape(sections // X_CHIPS, X_CHIPS, strips)
    field = P(GZ, None, "strip", None)
    placed = (field, field, field, field, P(None, GZ, "strip", None), P(None, GZ), P())
    return jax.shard_map(
        local,
        mesh=Mesh(split, ("z", "x", "strip")),
        in_specs=placed,
        out_specs=(field, field),
        check_vma=False,
    )
```

time: 392 us -> 112 us (0.29)
  blocking collectives: 322 us -> 54.2 us
  between operations: 9.05 us -> 0.94 us
  Pallas kernels: 0 us -> 6.76 us
  waiting for transfers between devices: 22.9 us -> 17.6 us
    psum x3 -> x0, blocking collectives: 322 us -> none  [local(): kicked_sq = lax.psum(jnp.sum(kicked * kicked), ('gz', 'strip'))]
    all_to_all x0 -> x2, blocking collectives: none -> 54.2 us  [the longest x1 30.2 us: local(): sums = lax.all_to_all(jnp.broadcast_to(sums, (nz, 1, 128)), 'z', 0, 0)]
    pallas_call x0 -> x4, Pallas kernels: none -> 6.76 us  [call(): pl.pallas_call(kernel, out_shape=out_shape, in_specs=specs, out_specs=jax...]
    ppermute x12 -> x8, waiting for transfers between devices: 22.9 us -> 17.6 us  [the longest x6 16.9 us: exchange(): return (lax.ppermute(value, axes, up), lax.ppermute(value, axes, down))]
    ppermute x12 -> x8, starting transfers between devices: 27.7 us -> 27.6 us  [the longest x6 17.5 us: exchange(): return (lax.ppermute(value, axes, up), lax.ppermute(value, axes, down))]
  transfers between devices with their start and end apart: 12 -> 8, of which waited for: 8 -> 7; matrix products, arithmetic and copies ran while one was open for 1% -> 1% of each run, Pallas kernels for 0% -> 0%
where the time goes in v1:
time: 112 us; the launch traced here: 111 us
  blocking collectives  54.2 us (48%)
  starting transfers between devices  27.6 us (25%)
  waiting for transfers between devices  17.6 us (16%)
  Pallas kernels  6.76 us (6%)
  local copies, waits for them, and re-layouts  3.65 us (3%)
    all_to_all x1, blocking collectives, local(): sums = lax.all_to_all(jnp.broadcast_to(sums, (nz, 1, 128)), 'z', 0, 0)  30.2 us
    all_to_all x1, blocking collectives, local(): lax.all_to_all(jnp.broadcast_to(sums, (near, 1, 128)), ('x', 'strip'), 0, 0)  24 us
    ppermute x6, starting transfers between devices, exchange(): return (lax.ppermute(value, axes, up), lax.ppermute(value, axes, down))  17.5 us
    ppermute x6, waiting for transfers between devices, exchange(): return (lax.ppermute(value, axes, up), lax.ppermute(value, axes, down))  16.9 us
    pallas_call x4, Pallas kernels, call(): pl.pallas_call(kernel, out_shape=out_shape, in_specs=specs, out_specs=jax...  6.76 us
    ppermute x1, starting transfers between devices, local(): lax.ppermute(from_below, 'strip', [(i + 1, i) for i in range(nstrips - 1)])  5.48 us
    ppermute x1, starting transfers between devices, local(): lax.ppermute(from_above, 'strip', [(i, i + 1) for i in range(nstrips - 1)])  4.59 us
    slice x5, local copies, waits for them, and re-layouts, local(): from_below = packed(lambda f, d: f[:, :d])  2.49 us
  transfers between devices with their start and end apart: 8, of which 7 were waited for; matrix products, arithmetic and copies ran while one was open for 1% of the time, Pallas kernels for 0%

profile of v1, /device:TPU:1, one launch (start us, length us, event | category | flops | bytes accessed | tf_op | source)
XLA Modules:
  0.0 111.2 jit_solution(14039233674996366217)
XLA Ops:
  0.7 0.9 fusion.5
  1.5 0.8 fusion.4
  2.4 0.8 fusion.3
  3.7 4.6 %collective-permute-start.1 = (f32[24,640]{1,0:T(8,128)S(1)}, f32[24,640]{1,0:T(8,128)S(1)}, u32[]{:S(2)}, u32[]{:S(2)}) collective-permute-start(f32[24,640]{1,0:T(8,128)S(1)} %concatenate.26), channel_id=1, source_target_pairs={{0,1},{1,2},{2,3},{3,4},{4,5},{5,6},{6,7},{8,9},{9,10},{10,11},{11... | collective-permute-start | bytes 184328 | tf_op jit(solution)/shard_map/ppermute | solution.py:249
  8.7 5.5 %collective-permute-start = (f32[24,640]{1,0:T(8,128)S(1)}, f32[24,640]{1,0:T(8,128)S(1)}, u32[]{:S(2)}, u32[]{:S(2)}) collective-permute-start(f32[24,640]{1,0:T(8,128)S(1)} %concatenate.25), channel_id=1, source_target_pairs={{1,0},{2,1},{3,2},{4,3},{5,4},{6,5},{7,6},{9,8},{10,9},{11,10},{12... | collective-permute-start | bytes 184328 | tf_op jit(solution)/shard_map/ppermute | solution.py:250
  14.4 0.7 collective-permute-done
  15.2 1.4 %collective-permute-start.3 = (f32[2,40,640]{2,1,0:T(8,128)S(1)}, f32[2,40,640]{2,1,0:T(8,128)S(1)}, u32[]{:S(2)}, u32[]{:S(2)}) collective-permute-start(f32[2,40,640]{2,1,0:T(8,128)S(1)} %pad_maximum_fusion.refs_1_.refs_2_.u), channel_id=1, source_target_pairs={{8,0},{16,8},{24,16},{32,24},{40,32},{48,40},{56,48},{64,56},{72,6... | collective-permute-start | bytes 614408 | tf_op jit(solution)/shard_map/ppermute | solution.py:19
  16.7 4.0 %collective-permute-start.2 = (f32[2,40,640]{2,1,0:T(8,128)S(1)}, f32[2,40,640]{2,1,0:T(8,128)S(1)}, u32[]{:S(2)}, u32[]{:S(2)}) collective-permute-start(f32[2,40,640]{2,1,0:T(8,128)S(1)} %pad_maximum_fusion.refs_1_.refs_2_.u), channel_id=1, source_target_pairs={{0,8},{8,16},{16,24},{24,32},{32,40},{40,48},{48,56},{56,64},{64,7... | collective-permute-start | bytes 614408 | tf_op jit(solution)/shard_map/ppermute | solution.py:19
  21.0 2.5 %collective-permute-done.3.refs_3_.refs_4_ = f32[2,40,640]{2,1,0:T(8,128)S(1)} collective-permute-done((f32[2,40,640]{2,1,0:T(8,128)S(1)}, f32[2,40,640]{2,1,0:T(8,128)S(1)}, u32[]{:S(2)}, u32[]{:S(2)}) %collective-permute-start.3) | collective-permute-done | bytes 204832 | tf_op jit(solution)/shard_map/ppermute | solution.py:19
  23.6 0.9 collective-permute-done.2.refs_2_.refs_3_
  24.5 0.5 shard_map.86.refs_5_.p
  25.0 1.3 %collective-permute-start.5 = (f32[4,40,640]{2,1,0:T(8,128)S(1)}, f32[4,40,640]{2,1,0:T(8,128)S(1)}, u32[]{:S(2)}, u32[]{:S(2)}) collective-permute-start(f32[4,40,640]{2,1,0:T(8,128)S(1)} %shard_map.86.refs_5_.p), channel_id=1, source_target_pairs={{8,0},{16,8},{24,16},{32,24},{40,32},{48,40},{56,48},{64,56},{72,6... | collective-permute-start | bytes 1228808 | tf_op jit(solution)/shard_map/ppermute | solution.py:19
  26.3 4.8 %collective-permute-start.4 = (f32[4,40,640]{2,1,0:T(8,128)S(1)}, f32[4,40,640]{2,1,0:T(8,128)S(1)}, u32[]{:S(2)}, u32[]{:S(2)}) collective-permute-start(f32[4,40,640]{2,1,0:T(8,128)S(1)} %shard_map.86.refs_5_.p), channel_id=1, source_target_pairs={{0,8},{8,16},{16,24},{24,32},{32,40},{40,48},{48,56},{56,64},{64,7... | collective-permute-start | bytes 1228808 | tf_op jit(solution)/shard_map/ppermute | solution.py:19
  31.0 6.3 %collective-permute-done.5.refs_7_ = f32[4,40,640]{2,1,0:T(8,128)S(1)} collective-permute-done((f32[4,40,640]{2,1,0:T(8,128)S(1)}, f32[4,40,640]{2,1,0:T(8,128)S(1)}, u32[]{:S(2)}, u32[]{:S(2)}) %collective-permute-start.5) | collective-permute-done | bytes 409632 | tf_op jit(solution)/shard_map/ppermute | solution.py:19
  37.3 0.9 collective-permute-done.4.refs_6_
  38.2 1.5 %shard_map.87.refs_8_.q = f32[4,40,640]{2,1,0:T(8,128)S(1)} custom-call(s32[1]{0:T(128)} %bitcast.1.refs_0_, f32[3]{0:T(128)S(1)} %power_multiply_fusion.refs_1_.dts, f32[2,40,640]{2,1,0:T(8,128)S(1)} %pad_maximum_fusion.refs_1_.refs_2_.u, f32[2,40,640]{2,1,0:T(8,128)S(1)} %collective-permute-done.2.refs_2_.refs_3_, ...), custom_call_target="tpu_custom_call" | custom-call | tf_op jit(solution)/shard_map/pallas_call | solution.py:217
  39.7 1.3 %collective-permute-start.7 = (f32[4,40,640]{2,1,0:T(8,128)S(1)}, f32[4,40,640]{2,1,0:T(8,128)S(1)}, u32[]{:S(2)}, u32[]{:S(2)}) collective-permute-start(f32[4,40,640]{2,1,0:T(8,128)S(1)} %shard_map.87.refs_8_.q), channel_id=1, source_target_pairs={{8,0},{16,8},{24,16},{32,24},{40,32},{48,40},{56,48},{64,56},{72,6... | collective-permute-start | bytes 1228808 | tf_op jit(solution)/shard_map/ppermute | solution.py:19
  41.0 4.8 %collective-permute-start.6 = (f32[4,40,640]{2,1,0:T(8,128)S(1)}, f32[4,40,640]{2,1,0:T(8,128)S(1)}, u32[]{:S(2)}, u32[]{:S(2)}) collective-permute-start(f32[4,40,640]{2,1,0:T(8,128)S(1)} %shard_map.87.refs_8_.q), channel_id=1, source_target_pairs={{0,8},{8,16},{16,24},{24,32},{32,40},{40,48},{48,56},{56,64},{64,7... | collective-permute-start | bytes 1228808 | tf_op jit(solution)/shard_map/ppermute | solution.py:19
  45.8 5.4 %collective-permute-done.7.refs_10_ = f32[4,40,640]{2,1,0:T(8,128)S(1)} collective-permute-done((f32[4,40,640]{2,1,0:T(8,128)S(1)}, f32[4,40,640]{2,1,0:T(8,128)S(1)}, u32[]{:S(2)}, u32[]{:S(2)}) %collective-permute-start.7) | collective-permute-done | bytes 409632 | tf_op jit(solution)/shard_map/ppermute | solution.py:19
  51.2 0.9 collective-permute-done.6.refs_9_
  52.1 2.8 %shard_map.88 = (f32[8,32,640]{2,1,0:T(8,128)S(1)}, f32[1,128]{1,0:T(1,128)S(1)}) custom-call(s32[1]{0:T(128)} %bitcast.1.refs_0_, f32[3]{0:T(128)S(1)} %power_multiply_fusion.refs_1_.dts, f32[2,40,640]{2,1,0:T(8,128)S(1)} %pad_maximum_fusion.refs_1_.refs_2_.u, f32[2,40,640]{2,1,0:T(8,128)S(1)} %collective-permute-done.2.refs_2_.refs_3_, ...), custom_call_target="tpu_custom_call" | custom-call | tf_op jit(solution)/shard_map/pallas_call | solution.py:217
  54.9 24.0 %all_to_all.10 = f32[32,1,128]{2,1,0:T(1,128)S(1)} all-to-all(f32[32,1,128]{2,1,0:T(1,128)S(1)} %broadcast_in_dim.20), channel_id=1, replica_groups=mesh['z'=16,'x'=4,'strip'=8] {'x','strip'}, dimensions={0} | all-to-all | bytes 32768 | tf_op jit(solution)/shard_map/all_to_all | solution.py:286
  79.0 30.2 %all_to_all.11.parts = f32[16,1,128]{2,1,0:T(1,128)S(1)} all-to-all(f32[16,1,128]{2,1,0:T(1,128)S(1)} %broadcast_in_dim.21), channel_id=1, replica_groups=mesh['z'=16,'x'=4,'strip'=8] {'z'}, dimensions={0} | all-to-all | bytes 16384 | tf_op jit(solution)/shard_map/all_to_all | solution.py:288
  109.2 2.0 %shard_map.89 = (f32[2,32,640]{2,1,0:T(8,128)}, f32[2,32,640]{2,1,0:T(8,128)}) custom-call(f32[3]{0:T(128)S(1)} %power_multiply_fusion.refs_1_.dts, s32[3]{0:T(128)S(1)} %bitcast.18, f32[16,1,128]{2,1,0:T(1,128)S(1)} %all_to_all.11.parts, f32[2,40,640]{2,1,0:T(8,128)S(1)} %pad_maximum_fusion.refs_1_.refs_2_.u, f32[4,40,640]{2,1,0:T(8,128)S(1)} %shard_map.86.refs_5_.p, ...), custom_call_target="tpu_custom_call" | custom-call | tf_op jit(solution)/shard_map/pallas_call | solution.py:217
  (56 shorter events, 1.6 us)
Async XLA Ops:
  0.6 2.6 %copy-start.1 = (f32[1,2,32,640]{3,2,1,0:T(8,128)S(1)}, f32[1,2,32,640]{3,2,1,0:T(8,128)}, u32[]{:S(2)}) copy-start(f32[1,2,32,640]{3,2,1,0:T(8,128)} %param.7) | copy-start | bytes 491524
  0.7 2.7 %copy-start.5 = (s32[2,1,32,640]{3,2,1,0:T(8,128)S(1)}, s32[2,1,32,640]{3,2,1,0:T(8,128)}, u32[]{:S(2)}) copy-start(s32[2,1,32,640]{3,2,1,0:T(8,128)} %param.11) | copy-start | bytes 491524
  3.7 10.7 %collective-permute-start.1 = (f32[24,640]{1,0:T(8,128)S(1)}, f32[24,640]{1,0:T(8,128)S(1)}, u32[]{:S(2)}, u32[]{:S(2)}) collective-permute-start(f32[24,640]{1,0:T(8,128)S(1)} %concatenate.26), channel_id=1, source_target_pairs={{0,1},{1,2},{2,3},{3,4},{4,5},{5,6},{6,7},{8,9},{9,10},{10,11},{11... | collective-permute-start | bytes 184328 | tf_op jit(solution)/shard_map/ppermute | solution.py:249
  8.4 5.8 %copy-start = (s32[3,1]{0,1:T(1,128)S(1)}, s32[3,1]{0,1:T(1,128)}, u32[]{:S(2)}) copy-start(s32[3,1]{0,1:T(1,128)} %param.12) | copy-start | bytes 40
  8.7 6.4 %collective-permute-start = (f32[24,640]{1,0:T(8,128)S(1)}, f32[24,640]{1,0:T(8,128)S(1)}, u32[]{:S(2)}, u32[]{:S(2)}) collective-permute-start(f32[24,640]{1,0:T(8,128)S(1)} %concatenate.25), channel_id=1, source_target_pairs={{1,0},{2,1},{3,2},{4,3},{5,4},{6,5},{7,6},{9,8},{10,9},{11,10},{12... | collective-permute-start | bytes 184328 | tf_op jit(solution)/shard_map/ppermute | solution.py:250
  15.1 5.8 %copy-start.4 = (f32[1,2,32,640]{3,2,1,0:T(8,128)S(1)}, f32[1,2,32,640]{3,2,1,0:T(8,128)}, u32[]{:S(2)}) copy-start(f32[1,2,32,640]{3,2,1,0:T(8,128)} %param.10) | copy-start | bytes 491524
  15.2 5.7 %copy-start.2 = (f32[1,2,32,640]{3,2,1,0:T(8,128)S(1)}, f32[1,2,32,640]{3,2,1,0:T(8,128)}, u32[]{:S(2)}) copy-start(f32[1,2,32,640]{3,2,1,0:T(8,128)} %param.8) | copy-start | bytes 491524
  15.2 5.7 %copy-start.3 = (f32[1,2,32,640]{3,2,1,0:T(8,128)S(1)}, f32[1,2,32,640]{3,2,1,0:T(8,128)}, u32[]{:S(2)}) copy-start(f32[1,2,32,640]{3,2,1,0:T(8,128)} %param.9) | copy-start | bytes 491524
  15.2 8.3 %collective-permute-start.3 = (f32[2,40,640]{2,1,0:T(8,128)S(1)}, f32[2,40,640]{2,1,0:T(8,128)S(1)}, u32[]{:S(2)}, u32[]{:S(2)}) collective-permute-start(f32[2,40,640]{2,1,0:T(8,128)S(1)} %pad_maximum_fusion.refs_1_.refs_2_.u), channel_id=1, source_target_pairs={{8,0},{16,8},{24,16},{32,24},{40,32},{48,40},{56,48},{64,56},{72,6... | collective-permute-start | bytes 614408 | tf_op jit(solution)/shard_map/ppermute | solution.py:19
  16.7 7.8 %collective-permute-start.2 = (f32[2,40,640]{2,1,0:T(8,128)S(1)}, f32[2,40,640]{2,1,0:T(8,128)S(1)}, u32[]{:S(2)}, u32[]{:S(2)}) collective-permute-start(f32[2,40,640]{2,1,0:T(8,128)S(1)} %pad_maximum_fusion.refs_1_.refs_2_.u), channel_id=1, source_target_pairs={{0,8},{8,16},{16,24},{24,32},{32,40},{40,48},{48,56},{56,64},{64,7... | collective-permute-start | bytes 614408 | tf_op jit(solution)/shard_map/ppermute | solution.py:19
  24.4 6.6 %copy-start.6 = (s32[3]{0:T(128)S(1)}, s32[3]{0:T(128)}, u32[]{:S(2)}) copy-start(s32[3]{0:T(128)} %param.13) | copy-start | bytes 40
  25.0 12.4 %collective-permute-start.5 = (f32[4,40,640]{2,1,0:T(8,128)S(1)}, f32[4,40,640]{2,1,0:T(8,128)S(1)}, u32[]{:S(2)}, u32[]{:S(2)}) collective-permute-start(f32[4,40,640]{2,1,0:T(8,128)S(1)} %shard_map.86.refs_5_.p), channel_id=1, source_target_pairs={{8,0},{16,8},{24,16},{32,24},{40,32},{48,40},{56,48},{64,56},{72,6... | collective-permute-start | bytes 1228808 | tf_op jit(solution)/shard_map/ppermute | solution.py:19
  26.3 12.0 %collective-permute-start.4 = (f32[4,40,640]{2,1,0:T(8,128)S(1)}, f32[4,40,640]{2,1,0:T(8,128)S(1)}, u32[]{:S(2)}, u32[]{:S(2)}) collective-permute-start(f32[4,40,640]{2,1,0:T(8,128)S(1)} %shard_map.86.refs_5_.p), channel_id=1, source_target_pairs={{0,8},{8,16},{16,24},{24,32},{32,40},{40,48},{48,56},{56,64},{64,7... | collective-permute-start | bytes 1228808 | tf_op jit(solution)/shard_map/ppermute | solution.py:19
  39.7 11.5 %collective-permute-start.7 = (f32[4,40,640]{2,1,0:T(8,128)S(1)}, f32[4,40,640]{2,1,0:T(8,128)S(1)}, u32[]{:S(2)}, u32[]{:S(2)}) collective-permute-start(f32[4,40,640]{2,1,0:T(8,128)S(1)} %shard_map.87.refs_8_.q), channel_id=1, source_target_pairs={{8,0},{16,8},{24,16},{32,24},{40,32},{48,40},{56,48},{64,56},{72,6... | collective-permute-start | bytes 1228808 | tf_op jit(solution)/shard_map/ppermute | solution.py:19
  41.0 11.1 %collective-permute-start.6 = (f32[4,40,640]{2,1,0:T(8,128)S(1)}, f32[4,40,640]{2,1,0:T(8,128)S(1)}, u32[]{:S(2)}, u32[]{:S(2)}) collective-permute-start(f32[4,40,640]{2,1,0:T(8,128)S(1)} %shard_map.87.refs_8_.q), channel_id=1, source_target_pairs={{0,8},{8,16},{16,24},{24,32},{32,40},{40,48},{48,56},{56,64},{64,7... | collective-permute-start | bytes 1228808 | tf_op jit(solution)/shard_map/ppermute | solution.py:19

commit v2 on v1

--- a/solution.py
+++ b/solution.py
@@ -13,10 +13,10 @@
 N_SUMS = 28
 
 
-def exchange(value, axes, size):
-    up = [(i, i + 1) for i in range(size - 1)]
-    down = [(j, i) for i, j in up]
-    return lax.ppermute(value, axes, up), lax.ppermute(value, axes, down)
+def swap(value, size):
+    first = [(i, i ^ 1) for i in range(size)]
+    second = [(i, ((i - 1) ^ 1) + 1) for i in range(1, size - 1)]
+    return lax.ppermute(value, GZ, first), lax.ppermute(value, GZ, second)
 
 
 class Stencil:
@@ -77,9 +77,18 @@
     return alpha, (1.0 - alpha) * keep, alpha * keep
 
 
-def resets_of(field):
-    at = field.shape[1] - 5
-    return field[0, at : at + 1], field[0, at + 1 : at + 2]
+def from_neighbour(packet, rows, at):
+    tail = packet[4 * rows :]
+    tail = tail if at == 0 else pltpu.roll(tail, 8 - at, 0)
+    return jnp.concatenate([packet[rows * at : rows * at + rows], tail], axis=0)
+
+
+def weights_of(marks):
+    weights = []
+    for side in range(3):
+        alpha, keep, mix = factors(marks[3 * side], jnp.float32(0.1))
+        weights.append((keep, mix, *factors(marks[3 * side + 1], alpha)[1:]))
+    return weights
 
 
 def after_first(u0, v0, f0, dt0, k0, g0):
@@ -94,23 +103,29 @@
     return vel, (ua + dt1 * vel[0], ub + dt1 * vel[1], dt1 * vel[2], dt1 * vel[3])
 
 
-def first_kernel(nstrips, ids, u, ub, ua, v, fd, fu, mk, out):
-    op = stencil_of(ids, nstrips, fd, fu, mk)
+def first_kernel(nstrips, ids, u, ue, uo, fe, fo, mk, out):
+    op = stencil_of(ids, nstrips, fe, fo, mk)
     for c in range(2):
-        out[c] = op(u[c], ub[c], ua[c]) + op.bias(c)
-        out[2 + c] = v[c]
-
-
-def second_kernel(nstrips, ids, dts, u, ub, ua, p, pb, pa, fd, fu, mk, out):
-    op = stencil_of(ids, nstrips, fd, fu, mk)
-    weights = [factors(resets_of(f)[0], jnp.float32(0.1)) for f in (u, ub, ua)]
+        out[c] = op(u[c], ue[c], uo[c]) + op.bias(c)
+
+
+def second_kernel(nstrips, ids, dts, marks, u, ue, uo, v, ve, vo, p, pe, po, fe, fo, mk, q, tails):
+    op = stencil_of(ids, nstrips, fe, fo, mk)
+    rows = p.shape[1] - 8
+    q[4 * rows :] = jnp.zeros((8, q.shape[1]), jnp.float32)
     for c in range(2):
         parts = [
-            after_first(f[c], q[2 + c], q[c], dts[0], k, g)
-            for f, q, (_, k, g) in zip((u, ub, ua), (p, pb, pa), weights)
+            after_first(f[c], w[c], x[c], dts[0], k[0], k[1])
+            for f, w, x, k in zip((u, ue, uo), (v, ve, vo), (p, pe, po), weights_of(marks))
         ]
-        out[c] = op(*[x[2] for x in parts]) + op.bias(c)
-        out[2 + c] = op(*[x[3] for x in parts])
+        for i in range(2):
+            force = op(*[x[2 + i] for x in parts])
+            if i == 0:
+                force = force + op.bias(c)
+            at = 2 * i + c
+            q[rows * at : rows * at + rows] = force[:rows]
+            q[4 * rows + at : 4 * rows + at + 1] = force[rows : rows + 1]
+            tails[8 * at : 8 * at + 8] = force[rows:]
 
 
 def products(fields):
@@ -128,22 +143,24 @@
     return total
 
 
-def third_kernel(nstrips, ids, dts, u, ub, ua, p, pb, pa, q, qb, qa, fd, fu, mk, out, sums):
-    op = stencil_of(ids, nstrips, fd, fu, mk)
+def third_kernel(nstrips, ids, dts, marks, u, ue, uo, v, ve, vo, p, pe, po, q, tails, qe, qo, fe, fo, mk, out, sums):
+    op = stencil_of(ids, nstrips, fe, fo, mk)
     rows = out.shape[1]
     dt0, dt1, dt2 = dts[0], dts[1], dts[2]
-    weights = []
-    for f in (u, ub, ua):
-        r0, r1 = resets_of(f)
-        alpha, k0, g0 = factors(r0, jnp.float32(0.1))
-        _, k1, g1 = factors(r1, alpha)
-        weights.append((k0, g0, k1, g1))
+    weights = weights_of(marks)
     totals = [None] * N_SUMS
     for c in range(2):
+        cores = [q[rows * at : rows * at + rows] for at in (c, 2 + c)]
+        own = [
+            jnp.concatenate([core, tails[8 * at : 8 * at + 8]], axis=0)
+            for core, at in zip(cores, (c, 2 + c))
+        ]
+        even = [from_neighbour(qe, rows, at) for at in (c, 2 + c)]
+        odd = [from_neighbour(qo, rows, at) for at in (c, 2 + c)]
         sides = []
-        for f, m, n, (k0, g0, k1, g1) in zip((u, ub, ua), (p, pb, pa), (q, qb, qa), weights):
-            one = after_first(f[c], m[2 + c], m[c], dt0, k0, g0)
-            sides.append((one, *after_second(one, n[c], n[2 + c], dt1, k1, g1)))
+        for f, w, x, n, (k0, g0, k1, g1) in zip((u, ue, uo), (v, ve, vo), (p, pe, po), (own, even, odd), weights):
+            one = after_first(f[c], w[c], x[c], dt0, k0, g0)
+            sides.append((one, *after_second(one, n[0], n[1], dt1, k1, g1)))
         forces = []
         for i in range(4):
             force = op(sides[0][2][i], sides[1][2][i], sides[2][2][i])
@@ -153,9 +170,9 @@
             out[4 * c + i] = force
             forces.append(force)
         va, vb = sides[0][0][0][:rows], sides[0][0][1][:rows]
-        f0, fa, fb = p[c, :rows], q[c, :rows], q[2 + c, :rows]
+        f0, (fa, fb) = p[c, :rows], cores
         kicked = [x[:rows] + dt2 * y for x, y in zip(sides[0][1], forces)]
-        terms = products([f0]) + products([p[2 + c, :rows] + dt0 * f0])
+        terms = products([f0]) + products([v[c, :rows] + dt0 * f0])
         terms += products([fa, fb]) + products([va + dt1 * fa, vb + dt1 * fb])
         terms += products(forces) + products(kicked)
         for i, term in enumerate(terms):
@@ -187,7 +204,7 @@
     return jnp.sqrt(kicked / (force + 1e-06))
 
 
-def last_kernel(dts, rs, parts, u, p, q, f2, pos, vel):
+def last_kernel(dts, marks, parts, u, v, p, q, f2, pos, vel):
     rows = pos.shape[1]
     sums = jnp.sum(parts[...], axis=0)
     c0 = ratio(jnp.maximum(sums[:, 1:2], 0.0), sums[:, 0:1])
@@ -198,13 +215,13 @@
     alpha = jnp.float32(0.1)
     weights = []
     for i in range(3):
-        alpha = jnp.where(rs[i] == 1, jnp.float32(0.1), 0.99 * alpha)
-        keep = jnp.where(rs[i] == 1, jnp.float32(0.0), jnp.float32(1.0))
-        weights.append(((1.0 - alpha) * keep, alpha * keep))
+        alpha, keep, mix = factors(marks[i], alpha)
+        weights.append((keep, mix))
     for c in range(2):
         f = f2[4 * c] + c0 * f2[4 * c + 1] + c1 * (f2[4 * c + 2] + c0 * f2[4 * c + 3])
-        field, speed = u[c, :rows], p[2 + c, :rows]
-        forces = (p[c, :rows], q[c, :rows] + c0 * q[2 + c, :rows], f)
+        field, speed = u[c, :rows], v[c, :rows]
+        cores = [q[rows * at : rows * at + rows] for at in (c, 2 + c)]
+        forces = (p[c, :rows], cores[0] + c0 * cores[1], f)
         for i, (force, factor) in enumerate(zip(forces, (c0, c1, c2))):
             keep, mix = weights[i]
             speed = keep * (speed + dts[i] * force) + (mix * factor) * force
@@ -232,55 +249,61 @@
     section = lax.axis_index(GZ)
     _, comps, rows, cols = positions.shape
     ring = rows + 8
+    core = f32(comps, rows, cols)
+    marks = (resets[:, 0] == 1).astype(jnp.float32)
+    tile = jnp.broadcast_to(jnp.pad(marks, (0, 5))[:, None], (8, cols))
+    start = [positions.reshape(-1, cols), velocity.reshape(-1, cols), tile]
+    even, odd = swap(jnp.concatenate(start, axis=0), nz * nx)
+    ends = [(x[: 2 * rows].reshape(2, rows, cols), x[2 * rows : 4 * rows].reshape(2, rows, cols)) for x in (even, odd)]
+    marks = jnp.concatenate([marks] + [x[4 * rows : 4 * rows + 3, 0] for x in (even, odd)])
+    dts = 0.1 * jnp.power(jnp.float32(1.25), dt_index.astype(jnp.float32))
+    ids = jnp.reshape(lax.axis_index("strip"), (1,))
+    is_odd = section % 2 == 1
     valid = jnp.stack([section > 0, section < nz * nx - 1]).astype(jnp.int32)
     masks = (flow_mask[:, 0] * valid[:, None, None]).astype(jnp.float32)
-    dts = 0.1 * jnp.power(jnp.float32(1.25), dt_index.astype(jnp.float32))
-    ids = jnp.reshape(lax.axis_index("strip"), (1,))
-    resets = resets[:, 0]
-    fields = [positions[0], velocity[0], flow_down[0], flow_up[0], masks]
-    deep = [DEEP] + [DEEP - 1] * 4
+    masks = jnp.where(is_odd, masks, masks[::-1])
+    flow_even = jnp.where(is_odd, flow_down[0], flow_up[0])
+    flow_odd = jnp.where(is_odd, flow_up[0], flow_down[0])
+    fields = [positions[0], velocity[0], flow_even, flow_odd, masks, *ends[0], *ends[1]]
+    deep = [DEEP] + [DEEP - 1] * 4 + [DEEP, DEEP - 1] * 2
+    spare = jnp.zeros((-2 * sum(deep) % 8, cols), jnp.float32)
 
     def packed(cut):
         slabs = [cut(f, d).reshape(-1, cols) for f, d in zip(fields, deep)]
-        return jnp.concatenate(slabs + [jnp.zeros((2, cols), jnp.float32)], axis=0)
+        return jnp.concatenate(slabs + [spare], axis=0)
 
     from_above = packed(lambda f, d: f[:, rows - d :])
     from_below = packed(lambda f, d: f[:, :d])
     above = lax.ppermute(from_above, "strip", [(i, i + 1) for i in range(nstrips - 1)])
     below = lax.ppermute(from_below, "strip", [(i + 1, i) for i in range(nstrips - 1)])
-    marks = (resets[:2] == 1).astype(jnp.float32)
     wide, at = [], 0
     for f, d in zip(fields, deep):
         lower = below[at : at + 2 * d].reshape(2, d, cols)
         upper = above[at : at + 2 * d].reshape(2, d, cols)
         at += 2 * d
-        if d == DEEP:
-            gap = jnp.broadcast_to(marks[None, :, None], (2, 2, cols))
-        else:
-            gap = jnp.zeros((2, 8 - 2 * d, cols), jnp.float32)
+        gap = jnp.zeros((2, 8 - 2 * d, cols), jnp.float32)
         wide.append(jnp.concatenate([f, lower, gap, upper], axis=1))
-    u, v, fd, fu, mk = wide
-
-    ub, ua = exchange(u, GZ, nz * nx)
+    u, v, fe, fo, mk, ue, ve, uo, vo = wide
+
     p = call(
         lambda *refs: first_kernel(nstrips, *refs),
-        f32(4, ring, cols),
-        [SMEM] + [VMEM] * 7,
-        ids, u, ub, ua, v, fd, fu, mk,
-    )
-    pb, pa = exchange(p, GZ, nz * nx)
-    q = call(
+        f32(comps, ring, cols),
+        [SMEM] + [VMEM] * 6,
+        ids, u, ue, uo, fe, fo, mk,
+    )
+    pe, po = swap(p, nz * nx)
+    q, tails = call(
         lambda *refs: second_kernel(nstrips, *refs),
-        f32(4, ring, cols),
-        [SMEM] * 2 + [VMEM] * 9,
-        ids, dts, u, ub, ua, p, pb, pa, fd, fu, mk,
-    )
-    qb, qa = exchange(q, GZ, nz * nx)
+        (f32(4 * rows + 8, cols), f32(32, cols)),
+        [SMEM] * 3 + [VMEM] * 12,
+        ids, dts, marks, u, ue, uo, v, ve, vo, p, pe, po, fe, fo, mk,
+    )
+    qe, qo = swap(q, nz * nx)
     f2, sums = call(
         lambda *refs: third_kernel(nstrips, *refs),
-        (f32(8, rows, cols), f32(1, 128)),
-        [SMEM] * 2 + [VMEM] * 12,
-        ids, dts, u, ub, ua, p, pb, pa, q, qb, qa, fd, fu, mk,
+        (f32(4 * comps, rows, cols), f32(1, 128)),
+        [SMEM] * 3 + [VMEM] * 16,
+        ids, dts, marks, u, ue, uo, v, ve, vo, p, pe, po, q, tails, qe, qo, fe, fo, mk,
     )
     near = nx * nstrips
     sums = lax.all_to_all(jnp.broadcast_to(sums, (near, 1, 128)), ("x", "strip"), 0, 0)
@@ -288,9 +311,9 @@
     sums = lax.all_to_all(jnp.broadcast_to(sums, (nz, 1, 128)), "z", 0, 0)
     pos, vel = call(
         last_kernel,
-        (f32(comps, rows, cols), f32(comps, rows, cols)),
-        [SMEM] * 2 + [VMEM] * 5,
-        dts, resets, sums, u, p, q, f2,
+        (core, core),
+        [SMEM] * 2 + [VMEM] * 6,
+        dts, marks, sums, u, v, p, q, f2,
     )
     return pos[None], vel[None]
 

time: 112 us -> 105 us (0.938)
  blocking collectives: 54.2 us -> 44.3 us
  starting transfers between devices: 27.6 us -> 29.6 us
  other arithmetic: 0.41 us -> 2.39 us
    all_to_all x1, blocking collectives: 24 us -> 18.4 us  [local(): lax.all_to_all(jnp.broadcast_to(sums, (near, 1, 128)), ('x', 'strip'), 0, 0)]
    all_to_all x1, blocking collectives: 30.2 us -> 25.9 us  [local(): sums = lax.all_to_all(jnp.broadcast_to(sums, (nz, 1, 128)), 'z', 0, 0)]
    ppermute x1, starting transfers between devices: 5.48 us -> 1.92 us  [local(): lax.ppermute(from_below, 'strip', [(i + 1, i) for i in range(nstrips - 1)])]
    ppermute x1, waiting for transfers between devices: 0.67 us -> 3.95 us  [local(): lax.ppermute(from_below, 'strip', [(i + 1, i) for i in range(nstrips - 1)])]
    ppermute x6, starting transfers between devices: 17.5 us -> 20.8 us  [swap(): return (lax.ppermute(value, GZ, first), lax.ppermute(value, GZ, second))]
    ppermute x6, waiting for transfers between devices: 16.9 us -> 13.8 us  [swap(): return (lax.ppermute(value, GZ, first), lax.ppermute(value, GZ, second))]
    slice x5 -> x8, local copies, waits for them, and re-layouts: 2.49 us -> 0.09 us  [local(): from_below = packed(lambda f, d: f[:, :d])]
    ppermute x1, starting transfers between devices: 4.59 us -> 6.89 us  [local(): lax.ppermute(from_above, 'strip', [(i, i + 1) for i in range(nstrips - 1)])]
  transfers between devices with their start and end apart: 8 -> 8, of which waited for: 7 -> 4; matrix products, arithmetic and copies ran while one was open for 1% -> 2% of each run, Pallas kernels for 0% -> 0%
where the time goes in v2:
time: 105 us
  blocking collectives  44.3 us (42%)
  starting transfers between devices  29.6 us (28%)
  waiting for transfers between devices  17.7 us (17%)
  Pallas kernels  6.78 us (6%)
  local copies, waits for them, and re-layouts  3.16 us (3%)
  other arithmetic  2.39 us (2%)
  between operations  1.1 us (1%)
    all_to_all x1, blocking collectives, local(): sums = lax.all_to_all(jnp.broadcast_to(sums, (nz, 1, 128)), 'z', 0, 0)  25.9 us
    ppermute x6, starting transfers between devices, swap(): return (lax.ppermute(value, GZ, first), lax.ppermute(value, GZ, second))  20.8 us
    all_to_all x1, blocking collectives, local(): lax.all_to_all(jnp.broadcast_to(sums, (near, 1, 128)), ('x', 'strip'), 0, 0)  18.4 us
    ppermute x6, waiting for transfers between devices, swap(): return (lax.ppermute(value, GZ, first), lax.ppermute(value, GZ, second))  13.8 us
    ppermute x1, starting transfers between devices, local(): lax.ppermute(from_above, 'strip', [(i, i + 1) for i in range(nstrips - 1)])  6.89 us
    pallas_call x4, Pallas kernels, call(): pl.pallas_call(kernel, out_shape=out_shape, in_specs=specs, out_specs=jax...  6.78 us
    ppermute x1, waiting for transfers between devices, local(): lax.ppermute(from_below, 'strip', [(i + 1, i) for i in range(nstrips - 1)])  3.95 us
  transfers between devices with their start and end apart: 8, of which 4 were waited for; matrix products, arithmetic and copies ran while one was open for 2% of the time, Pallas kernels for 0%

profile of v2, /device:TPU:1, one launch (start us, length us, event | category | flops | bytes accessed | tf_op | source)
XLA Modules:
  0.0 105.0 jit_solution(12976106339809548187)
XLA Ops:
  0.6 0.7 fusion.1
  1.3 1.1 %maximum_maximum_fusion = f32[136,640]{1,0:T(8,128)S(1)} fusion(f32[64,640]{1,0:T(8,128)} %bitcast.37, f32[64,640]{1,0:T(8,128)} %bitcast.30, f32[136]{0:T(256)S(1)} %compare_select_fusion), kind=kLoop, calls=%fused_computation | loop fusion | flops 174080 | bytes 676384 | tf_op jit(solution)/shard_map/concatenate | solution.py:256
  2.5 0.8 collective-permute-start.1
  3.3 6.4 %collective-permute-start = (f32[136,640]{1,0:T(8,128)S(1)}, f32[136,640]{1,0:T(8,128)S(1)}, u32[]{:S(2)}, u32[]{:S(2)}) collective-permute-start(f32[136,640]{1,0:T(8,128)S(1)} %maximum_maximum_fusion), channel_id=1, source_target_pairs={{0,8},{8,0},{16,24},{24,16},{32,40},{40,32},{48,56},{56,48},{64,72... | collective-permute-start | bytes 1044488 | tf_op jit(solution)/shard_map/ppermute | solution.py:19
  10.0 0.8 copy-done.3
  11.2 3.8 %collective-permute-done = f32[136,640]{1,0:T(8,128)S(1)} collective-permute-done((f32[136,640]{1,0:T(8,128)S(1)}, f32[136,640]{1,0:T(8,128)S(1)}, u32[]{:S(2)}, u32[]{:S(2)}) %collective-permute-start) | collective-permute-done | bytes 348192 | tf_op jit(solution)/shard_map/ppermute | solution.py:19
  15.1 0.5 concatenate.46
  15.6 6.9 %collective-permute-start.3 = (f32[48,640]{1,0:T(8,128)S(1)}, f32[48,640]{1,0:T(8,128)S(1)}, u32[]{:S(2)}, u32[]{:S(2)}) collective-permute-start(f32[48,640]{1,0:T(8,128)S(1)} %concatenate.46), channel_id=1, source_target_pairs={{0,1},{1,2},{2,3},{3,4},{4,5},{5,6},{6,7},{8,9},{9,10},{10,11},{11... | collective-permute-start | bytes 368648 | tf_op jit(solution)/shard_map/ppermute | solution.py:277
  22.9 0.5 concatenate.45
  23.4 1.9 %collective-permute-start.2 = (f32[48,640]{1,0:T(8,128)S(1)}, f32[48,640]{1,0:T(8,128)S(1)}, u32[]{:S(2)}, u32[]{:S(2)}) collective-permute-start(f32[48,640]{1,0:T(8,128)S(1)} %concatenate.45), channel_id=1, source_target_pairs={{1,0},{2,1},{3,2},{4,3},{5,4},{6,5},{7,6},{9,8},{10,9},{11,10},{12... | collective-permute-start | bytes 368648 | tf_op jit(solution)/shard_map/ppermute | solution.py:278
  25.7 3.9 %collective-permute-done.2 = f32[48,640]{1,0:T(8,128)S(1)} collective-permute-done((f32[48,640]{1,0:T(8,128)S(1)}, f32[48,640]{1,0:T(8,128)S(1)}, u32[]{:S(2)}, u32[]{:S(2)}) %collective-permute-start.2) | collective-permute-done | bytes 122912 | tf_op jit(solution)/shard_map/ppermute | solution.py:278
  29.9 0.2 pad_maximum_fusion.8
  30.1 0.5 shard_map.86.refs_9_.p
  30.6 0.7 collective-permute-start.5
  31.3 5.6 %collective-permute-start.4 = (f32[2,40,640]{2,1,0:T(8,128)S(1)}, f32[2,40,640]{2,1,0:T(8,128)S(1)}, u32[]{:S(2)}, u32[]{:S(2)}) collective-permute-start(f32[2,40,640]{2,1,0:T(8,128)S(1)} %shard_map.86.refs_9_.p), channel_id=1, source_target_pairs={{0,8},{8,0},{16,24},{24,16},{32,40},{40,32},{48,56},{56,48},{64,72... | collective-permute-start | bytes 614408 | tf_op jit(solution)/shard_map/ppermute | solution.py:19
  37.1 2.9 %collective-permute-done.4.refs_10_ = f32[2,40,640]{2,1,0:T(8,128)S(1)} collective-permute-done((f32[2,40,640]{2,1,0:T(8,128)S(1)}, f32[2,40,640]{2,1,0:T(8,128)S(1)}, u32[]{:S(2)}, u32[]{:S(2)}) %collective-permute-start.4) | collective-permute-done | bytes 204832 | tf_op jit(solution)/shard_map/ppermute | solution.py:19
  40.0 1.5 %shard_map.87 = (f32[136,640]{1,0:T(8,128)S(1)}, f32[32,640]{1,0:T(8,128)S(1)}) custom-call(s32[1]{0:T(128)} %bitcast.3.refs_0_, f32[3]{0:T(128)S(1)} %power_multiply_fusion.refs_1_.dts, f32[9]{0:T(128)S(1)} %pad_maximum_fusion.9.refs_2_.marks, f32[2,40,640]{2,1,0:T(8,128)S(1)} %get-tuple-element.64.refs_1_.refs_3_.u, ...), custom_call_target="tpu_custom_call" | custom-call | tf_op jit(solution)/shard_map/pallas_call | solution.py:234
  41.6 0.7 collective-permute-start.7
  42.2 6.6 %collective-permute-start.6 = (f32[136,640]{1,0:T(8,128)S(1)}, f32[136,640]{1,0:T(8,128)S(1)}, u32[]{:S(2)}, u32[]{:S(2)}) collective-permute-start(f32[136,640]{1,0:T(8,128)S(1)} %get-tuple-element.8.refs_12_.q), channel_id=1, source_target_pairs={{0,8},{8,0},{16,24},{24,16},{32,40},{40,32},{48,56},{56,48},{64,72... | collective-permute-start | bytes 1044488 | tf_op jit(solution)/shard_map/ppermute | solution.py:19
  48.9 7.0 %collective-permute-done.6.refs_14_ = f32[136,640]{1,0:T(8,128)S(1)} collective-permute-done((f32[136,640]{1,0:T(8,128)S(1)}, f32[136,640]{1,0:T(8,128)S(1)}, u32[]{:S(2)}, u32[]{:S(2)}) %collective-permute-start.6) | collective-permute-done | bytes 348192 | tf_op jit(solution)/shard_map/ppermute | solution.py:19
  55.9 2.8 %shard_map.88 = (f32[8,32,640]{2,1,0:T(8,128)S(1)}, f32[1,128]{1,0:T(1,128)S(1)}) custom-call(s32[1]{0:T(128)} %bitcast.3.refs_0_, f32[3]{0:T(128)S(1)} %power_multiply_fusion.refs_1_.dts, f32[9]{0:T(128)S(1)} %pad_maximum_fusion.9.refs_2_.marks, f32[2,40,640]{2,1,0:T(8,128)S(1)} %get-tuple-element.64.refs_1_.refs_3_.u, ...), custom_call_target="tpu_custom_call" | custom-call | tf_op jit(solution)/shard_map/pallas_call | solution.py:234
  58.7 18.4 %all_to_all.10 = f32[32,1,128]{2,1,0:T(1,128)S(1)} all-to-all(f32[32,1,128]{2,1,0:T(1,128)S(1)} %broadcast_in_dim.24), channel_id=1, replica_groups=mesh['z'=16,'x'=4,'strip'=8] {'x','strip'}, dimensions={0} | all-to-all | bytes 32768 | tf_op jit(solution)/shard_map/all_to_all | solution.py:309
  77.1 25.9 %all_to_all.11.parts = f32[16,1,128]{2,1,0:T(1,128)S(1)} all-to-all(f32[16,1,128]{2,1,0:T(1,128)S(1)} %broadcast_in_dim.25), channel_id=1, replica_groups=mesh['z'=16,'x'=4,'strip'=8] {'z'}, dimensions={0} | all-to-all | bytes 16384 | tf_op jit(solution)/shard_map/all_to_all | solution.py:311
  103.0 2.0 %shard_map.89 = (f32[2,32,640]{2,1,0:T(8,128)}, f32[2,32,640]{2,1,0:T(8,128)}) custom-call(f32[3]{0:T(128)S(1)} %power_multiply_fusion.refs_1_.dts, f32[9]{0:T(128)S(1)} %pad_maximum_fusion.9.refs_2_.marks, f32[16,1,128]{2,1,0:T(1,128)S(1)} %all_to_all.11.parts, f32[2,40,640]{2,1,0:T(8,128)S(1)} %get-tuple-element.64.refs_1_.refs_3_.u, ...), custom_call_target="tpu_custom_call" | custom-call | tf_op jit(solution)/shard_map/pallas_call | solution.py:234
  (83 shorter events, 1.7 us)
Async XLA Ops:
  1.3 8.4 %copy-start.1 = (f32[1,2,32,640]{3,2,1,0:T(8,128)S(1)}, f32[1,2,32,640]{3,2,1,0:T(8,128)}, u32[]{:S(2)}) copy-start(f32[1,2,32,640]{3,2,1,0:T(8,128)} %param.8) | copy-start | bytes 491524
  1.3 8.4 %copy-start = (f32[1,2,32,640]{3,2,1,0:T(8,128)S(1)}, f32[1,2,32,640]{3,2,1,0:T(8,128)}, u32[]{:S(2)}) copy-start(f32[1,2,32,640]{3,2,1,0:T(8,128)} %param.7) | copy-start | bytes 491524
  2.4 7.4 %copy-start.2 = (s32[2,1,32,640]{3,2,1,0:T(8,128)S(1)}, s32[2,1,32,640]{3,2,1,0:T(8,128)}, u32[]{:S(2)}) copy-start(s32[2,1,32,640]{3,2,1,0:T(8,128)} %param.11) | copy-start | bytes 491524
  2.5 8.6 %collective-permute-start.1 = (f32[136,640]{1,0:T(8,128)S(1)}, f32[136,640]{1,0:T(8,128)S(1)}, u32[]{:S(2)}, u32[]{:S(2)}) collective-permute-start(f32[136,640]{1,0:T(8,128)S(1)} %maximum_maximum_fusion), channel_id=1, source_target_pairs={{8,16},{16,8},{24,32},{32,24},{40,48},{48,40},{56,64},{64,56},{72,... | collective-permute-start | bytes 1044488 | tf_op jit(solution)/shard_map/ppermute | solution.py:19
  3.3 11.7 %collective-permute-start = (f32[136,640]{1,0:T(8,128)S(1)}, f32[136,640]{1,0:T(8,128)S(1)}, u32[]{:S(2)}, u32[]{:S(2)}) collective-permute-start(f32[136,640]{1,0:T(8,128)S(1)} %maximum_maximum_fusion), channel_id=1, source_target_pairs={{0,8},{8,0},{16,24},{24,16},{32,40},{40,32},{48,56},{56,48},{64,72... | collective-permute-start | bytes 1044488 | tf_op jit(solution)/shard_map/ppermute | solution.py:19
  10.0 0.9 copy-start.3
  10.0 1.0 copy-start.4
  15.1 7.4 %copy-start.5 = (s32[3]{0:T(128)S(1)}, s32[3]{0:T(128)}, u32[]{:S(2)}) copy-start(s32[3]{0:T(128)} %param.13) | copy-start | bytes 40
  15.6 9.8 %collective-permute-start.3 = (f32[48,640]{1,0:T(8,128)S(1)}, f32[48,640]{1,0:T(8,128)S(1)}, u32[]{:S(2)}, u32[]{:S(2)}) collective-permute-start(f32[48,640]{1,0:T(8,128)S(1)} %concatenate.46), channel_id=1, source_target_pairs={{0,1},{1,2},{2,3},{3,4},{4,5},{5,6},{6,7},{8,9},{9,10},{10,11},{11... | collective-permute-start | bytes 368648 | tf_op jit(solution)/shard_map/ppermute | solution.py:277
  23.4 6.2 %collective-permute-start.2 = (f32[48,640]{1,0:T(8,128)S(1)}, f32[48,640]{1,0:T(8,128)S(1)}, u32[]{:S(2)}, u32[]{:S(2)}) collective-permute-start(f32[48,640]{1,0:T(8,128)S(1)} %concatenate.45), channel_id=1, source_target_pairs={{1,0},{2,1},{3,2},{4,3},{5,4},{6,5},{7,6},{9,8},{10,9},{11,10},{12... | collective-permute-start | bytes 368648 | tf_op jit(solution)/shard_map/ppermute | solution.py:278
  30.6 6.5 %collective-permute-start.5 = (f32[2,40,640]{2,1,0:T(8,128)S(1)}, f32[2,40,640]{2,1,0:T(8,128)S(1)}, u32[]{:S(2)}, u32[]{:S(2)}) collective-permute-start(f32[2,40,640]{2,1,0:T(8,128)S(1)} %shard_map.86.refs_9_.p), channel_id=1, source_target_pairs={{8,16},{16,8},{24,32},{32,24},{40,48},{48,40},{56,64},{64,56},{72,... | collective-permute-start | bytes 614408 | tf_op jit(solution)/shard_map/ppermute | solution.py:19
  31.3 8.8 %collective-permute-start.4 = (f32[2,40,640]{2,1,0:T(8,128)S(1)}, f32[2,40,640]{2,1,0:T(8,128)S(1)}, u32[]{:S(2)}, u32[]{:S(2)}) collective-permute-start(f32[2,40,640]{2,1,0:T(8,128)S(1)} %shard_map.86.refs_9_.p), channel_id=1, source_target_pairs={{0,8},{8,0},{16,24},{24,16},{32,40},{40,32},{48,56},{56,48},{64,72... | collective-permute-start | bytes 614408 | tf_op jit(solution)/shard_map/ppermute | solution.py:19
  41.6 7.3 %collective-permute-start.7 = (f32[136,640]{1,0:T(8,128)S(1)}, f32[136,640]{1,0:T(8,128)S(1)}, u32[]{:S(2)}, u32[]{:S(2)}) collective-permute-start(f32[136,640]{1,0:T(8,128)S(1)} %get-tuple-element.8.refs_12_.q), channel_id=1, source_target_pairs={{8,16},{16,8},{24,32},{32,24},{40,48},{48,40},{56,64},{64,56},{72,... | collective-permute-start | bytes 1044488 | tf_op jit(solution)/shard_map/ppermute | solution.py:19
  42.2 13.7 %collective-permute-start.6 = (f32[136,640]{1,0:T(8,128)S(1)}, f32[136,640]{1,0:T(8,128)S(1)}, u32[]{:S(2)}, u32[]{:S(2)}) collective-permute-start(f32[136,640]{1,0:T(8,128)S(1)} %get-tuple-element.8.refs_12_.q), channel_id=1, source_target_pairs={{0,8},{8,0},{16,24},{24,16},{32,40},{40,32},{48,56},{56,48},{64,72... | collective-permute-start | bytes 1044488 | tf_op jit(solution)/shard_map/ppermute | solution.py:19

commit v3 on v2

v3 whole, which is shorter than its diff:
```python
import jax
import jax.numpy as jnp
from jax import lax
from jax.experimental import pallas as pl
from jax.experimental.pallas import tpu as pltpu
from jax.sharding import Mesh, PartitionSpec as P

GZ = ("z", "x")
X_CHIPS = 4
DEEP = (3, 2, 2, 2, 2, 3, 2, 3, 2)
VMEM = pl.BlockSpec(memory_space=pltpu.VMEM)
SMEM = pl.BlockSpec(memory_space=pltpu.SMEM)
ANY = pl.BlockSpec(memory_space=pl.ANY)


def swap(value, axes, size):
    first = [(i, i ^ 1) for i in range(size)]
    second = [(i, ((i - 1) ^ 1) + 1) for i in range(1, size - 1)]
    values = value if isinstance(value, tuple) else (value, value)
    return lax.ppermute(values[0], axes, first), lax.ppermute(values[1], axes, second)


class Stencil:
    def __init__(self, strip, nstrips, flow_even, flow_odd, mask_even, mask_odd):
        rows, cols = mask_even.shape
        own = rows - 8
        ring = lax.broadcasted_iota(jnp.int32, (rows, 1), 0)
        row = strip * own + jnp.where(ring < own + 4, ring, ring - rows)
        last = nstrips * own - 1
        self.north = jnp.where((row > 0) & (row <= last), 1.0, 0.0).astype(jnp.float32)
        self.south = jnp.where((row >= 0) & (row < last), 1.0, 0.0).astype(jnp.float32)
        col = lax.broadcasted_iota(jnp.int32, (1, cols), 1)
        self.west = jnp.where(col > 0, 1.0, 0.0).astype(jnp.float32)
        self.east = jnp.where(col < cols - 1, 1.0, 0.0).astype(jnp.float32)
        self.flow_even = flow_even
        self.flow_odd = flow_odd
        self.mask_even = mask_even
        self.mask_odd = mask_odd
        degree = (self.north + self.south) + (self.west + self.east)
        self.pull = degree + (mask_even + mask_odd)
        self.rows, self.cols = rows, cols

    def below(self, value):
        return pltpu.roll(value, self.rows - 1, 0)

    def above(self, value):
        return pltpu.roll(value, 1, 0)

    def right(self, value):
        return pltpu.roll(value, self.cols - 1, 1) * self.east

    def left(self, value):
        return pltpu.roll(value, 1, 1) * self.west

    def sample(self, value, flow):
        step = self.right(value) - value
        here = value + flow[1] * step
        lower = self.below(value) + flow[1] * self.below(step)
        return here + flow[0] * (lower - here)

    def inner(self, own):
        total = self.north * self.above(own) + self.south * self.below(own)
        return total + (self.left(own) + self.right(own)) - self.pull * own

    def even(self, value):
        return self.mask_even * self.sample(value, self.flow_even)

    def odd(self, value):
        return self.mask_odd * self.sample(value, self.flow_odd)

    def __call__(self, own, even, odd):
        return self.inner(own) + (self.even(even) + self.odd(odd))

    def bias(self, comp):
        return self.mask_even * self.flow_even[comp] + self.mask_odd * self.flow_odd[comp]


def stencil_of(ids, nstrips, fe, fo, mk):
    return Stencil(ids[0], nstrips, (fe[0], fe[1]), (fo[0], fo[1]), mk[0], mk[1])


def factors(reset, alpha):
    alpha = jnp.where(reset > 0.5, jnp.float32(0.1), 0.99 * alpha)
    keep = jnp.where(reset > 0.5, jnp.float32(0.0), jnp.float32(1.0))
    return alpha, (1.0 - alpha) * keep, alpha * keep


def gamma():
    return 0.99 * jnp.float32(0.1)


def weights_of(marks):
    weights = []
    for side in range(3):
        alpha = factors(marks[3 * side], jnp.float32(0.1))[0]
        rho = jnp.where(marks[3 * side] > 0.5, jnp.float32(0.0), jnp.float32(1.0))
        weights.append((rho, *factors(marks[3 * side + 1], alpha)[1:]))
    return weights


def start_kernel(pos, vel, tile, out, sems):
    rows = pos.shape[0]
    copies = [
        pltpu.make_async_copy(src, out.at[pl.ds(at, size)], sems.at[i])
        for i, (src, at, size) in enumerate(((pos, 0, rows), (vel, rows, rows), (tile, 2 * rows, 8)))
    ]
    for copy in copies:
        copy.start()
    for copy in copies:
        copy.wait()


def rims_kernel(ids, u, v, fe, fo, mk, even, odd, first, second):
    rows = u.shape[1]
    sides = [(x, rows * at) for x in (even, odd) for at in range(4)]
    comps = [(f.at[c], 0) for f in (u, v, fe, fo, mk) for c in range(2)]
    comps += [(x, at) for x, at in sides]

    def fill(upper, lower):
        at = 0
        for i, (src, base) in enumerate(comps):
            deep = DEEP[i // 2]
            upper[at : at + deep] = src[base : base + deep]
            lower[at : at + deep] = src[base + rows - deep : base + rows]
            at += deep
        for out in (upper, lower):
            out[at:] = jnp.zeros((out.shape[0] - at, out.shape[1]), jnp.float32)

    @pl.when(ids[0] % 2 == 1)
    def _():
        fill(first, second)

    @pl.when(ids[0] % 2 == 0)
    def _():
        fill(second, first)


def first_kernel(nstrips, ids, marks, u, ue, uo, v, ve, vo, fe, fo, mk, packet, tails):
    op = stencil_of(ids, nstrips, fe, fo, mk)
    rows = u.shape[1] - 8
    rho, rho_even, rho_odd = [w[0] for w in weights_of(marks)]
    end = 4 * rows
    for c in range(2):
        f0 = op(u[c], ue[c], uo[c]) + op.bias(c)
        h = op(rho * v[c], rho_even * ve[c], rho_odd * vo[c])
        for at, value in ((c, f0), (2 + c, h)):
            packet[rows * at : rows * at + rows] = value[:rows]
            tails[8 * at : 8 * at + 8] = value[rows:]
        packet[end + 3 * c : end + 3 * c + 2] = f0[rows : rows + 2]
        last = end + (7, 2)[c]
        packet[last : last + 1] = f0[rows + 7 :]
        packet[end + 5 + c : end + 6 + c] = h[rows : rows + 1]


def own_ring(packet, tails, rows, at):
    return jnp.concatenate([packet[rows * at : rows * at + rows], tails[8 * at : 8 * at + 8]], axis=0)


def side_ring(packet, rows, at, size, shift):
    tail = packet[size * rows :]
    tail = pltpu.roll(tail, 8 - shift, 0) if shift else tail
    return jnp.concatenate([packet[rows * at : rows * at + rows], tail], axis=0)


def side_force(packet, rows, c):
    return side_ring(packet, rows, c, 4, 3 * c)


def side_h(packet, rows, c):
    return side_ring(packet, rows, 2 + c, 4, 5 + c)


def second_kernel(nstrips, ids, marks, p, ptails, pe, po, fe, fo, mk, packet, tails):
    op = stencil_of(ids, nstrips, fe, fo, mk)
    rows = mk.shape[1] - 8
    rho, rho_even, rho_odd = [w[0] for w in weights_of(marks)]
    packet[2 * rows :] = jnp.zeros((8, packet.shape[1]), jnp.float32)
    for c in range(2):
        f0 = own_ring(p, ptails, rows, c)
        g = op(rho * f0, rho_even * side_force(pe, rows, c), rho_odd * side_force(po, rows, c))
        packet[rows * c : rows * c + rows] = g[:rows]
        packet[2 * rows + c : 2 * rows + c + 1] = g[rows : rows + 1]
        tails[8 * c : 8 * c + 8] = g[rows:]


def products(fields, pairs):
    return [fields[i] * fields[j] for i, j in pairs]


def all_pairs(size):
    return [(i, j) for i in range(size) for j in range(i, size)]


EARLY = [(0, 0), (0, 2), (2, 2)]
LATE = [pair for pair in all_pairs(4) if pair not in EARLY]
N_EARLY = 2 + 3 + 3 + 2 * len(EARLY)
N_LATE = 2 * len(LATE)


def tile_sum(value):
    rows = value.shape[0]
    tall = value[0:8]
    for r in range(8, rows, 8):
        tall = tall + value[r : r + 8]
    total = tall[:, 0:128]
    for col in range(128, value.shape[1], 128):
        total = total + tall[:, col : col + 128]
    return total


def lanes_of(totals, at):
    lane = lax.broadcasted_iota(jnp.int32, (1, 128), 1)
    row = jnp.zeros((1, 128), jnp.float32)
    for i, total in enumerate(totals):
        whole = jnp.sum(jnp.sum(total, axis=0, keepdims=True), axis=1, keepdims=True)
        row = jnp.where(lane == at + i, whole, row)
    return row


def gathered(totals, terms):
    parts = [tile_sum(term) for term in terms]
    return parts if totals is None else [x + y for x, y in zip(totals, parts)]


def third_kernel(nstrips, ids, dts, marks, v, ve, vo, p, ptails, pe, po, g, gtails, fe, fo, mk, f2, w2, sums):
    op = stencil_of(ids, nstrips, fe, fo, mk)
    rows = mk.shape[1] - 8
    dt0, dt1, dt2 = dts[0], dts[1], dts[2]
    kappa = 1.0 - gamma()
    weights = weights_of(marks)
    totals = None
    for c in range(2):
        f0s = [own_ring(p, ptails, rows, c), side_force(pe, rows, c), side_force(po, rows, c)]
        hs = [own_ring(p, ptails, rows, 2 + c), side_h(pe, rows, c), side_h(po, rows, c)]
        vs = [v[c], ve[c], vo[c]]
        ts = [f0 + (dt0 * kappa) * h for f0, h in zip(f0s, hs)]
        g0 = dt0 * own_ring(g, gtails, rows, c)
        one = [k1 * ((rho * kappa) * v0 + dt1 * t) for v0, t, (rho, k1, _) in zip(vs, ts, weights)]
        mix = [g1 * t for t, (_, _, g1) in zip(ts, weights)]
        rho, k1, g1 = weights[0]
        mu = k1 * (rho * f0s[0] + dt1 * g0)
        both = g1 * g0
        sides = [(w[1] * w[0]) * f0 for f0, w in zip(f0s[1:], weights[1:])]
        forces = [
            ts[0] + dt1 * op(*one),
            g0 + dt1 * op(mu, *sides),
            dt1 * op(*mix),
            dt1 * op.inner(both),
        ]
        forces = [f[:rows] for f in forces]
        kicked = [x[:rows] + dt2 * f for x, f in zip((one[0], mu, mix[0], both), forces)]
        for i in range(4):
            f2[4 * c + i] = forces[i]
            w2[4 * c + i] = kicked[i]
        f0, v0, t, g0 = f0s[0][:rows], vs[0][:rows], ts[0][:rows], g0[:rows]
        terms = products([f0, v0 + dt0 * f0], [(0, 0), (1, 1)]) + products([t, g0], all_pairs(2))
        terms += products([(rho * kappa) * v0 + dt1 * t, rho * f0 + dt1 * g0], all_pairs(2))
        terms += products(forces, EARLY) + products(kicked, EARLY)
        totals = gathered(totals, terms)
    sums[...] = lanes_of(totals, 0)


def fourth_kernel(nstrips, ids, dts, marks, part, w2, early, ge, go, fe, fo, mk, f2, sums):
    op = stencil_of(ids, nstrips, fe, fo, mk)
    rows = part.shape[1]
    dt0, dt1, dt2 = dts[0], dts[1], dts[2]
    weights = weights_of(marks)
    totals = None
    for c in range(2):
        even = op.even(side_ring(ge, rows, c, 2, c))[:rows]
        odd = op.odd(side_ring(go, rows, c, 2, c))[:rows]
        scale = dt1 * dt0
        mu = scale * dt1 * (weights[1][1] * even + weights[2][1] * odd)
        both = scale * (weights[1][2] * even + weights[2][2] * odd)
        forces = [part[4 * c], part[4 * c + 1] + mu, part[4 * c + 2], part[4 * c + 3] + both]
        kicked = [w2[4 * c], w2[4 * c + 1] + dt2 * mu, w2[4 * c + 2], w2[4 * c + 3] + dt2 * both]
        f2[2 * c] = forces[1]
        f2[2 * c + 1] = forces[3]
        totals = gathered(totals, products(forces, LATE) + products(kicked, LATE))
    sums[...] = early[...] + lanes_of(totals, N_EARLY)


def form(coefficients, basis):
    total = None
    for (i, j), term in coefficients.items():
        for b in basis[i] + basis[j]:
            term = term * b
        if i != j:
            term = 2.0 * term
        total = term if total is None else total + term
    return jnp.maximum(total, 0.0)


def ratio(kicked, force):
    return jnp.sqrt(kicked / (force + 1e-06))


def last_kernel(dts, marks, parts, u, v, p, g, part, f2, pos, vel):
    rows = pos.shape[1]
    sums = jnp.sum(parts[...], axis=0)
    lanes = [sums[:, i : i + 1] for i in range(N_EARLY + N_LATE)]

    def take(pairs, at):
        return {pair: lanes[at + i] for i, pair in enumerate(pairs)}

    dt0, dt1, dt2 = dts[0], dts[1], dts[2]
    kappa = 1.0 - gamma()
    c0 = ratio(lanes[1], lanes[0])
    mu = kappa * dt0 + gamma() * c0
    one = ((), (mu,))
    c1 = ratio(form(take(all_pairs(2), 5), one), form(take(all_pairs(2), 2), one))
    two = ((), (mu,), (c1,), (mu, c1))
    force_sq = take(EARLY, 8) | take(LATE, N_EARLY)
    kicked_sq = take(EARLY, 8 + len(EARLY)) | take(LATE, N_EARLY + len(LATE))
    c2 = ratio(form(kicked_sq, two), form(force_sq, two))
    rho, k1, g1 = weights_of(marks)[0]
    alpha = factors(marks[1], factors(marks[0], jnp.float32(0.1))[0])[0]
    _, k2, g2 = factors(marks[2], alpha)
    for c in range(2):
        f0, h = p[rows * c : rows * c + rows], p[rows * (2 + c) : rows * (2 + c) + rows]
        speed = rho * (kappa * v[c, :rows] + mu * f0)
        field = u[c, :rows] + dt0 * speed
        force = f0 + (dt0 * kappa) * h + (mu * dt0) * g[rows * c : rows * c + rows]
        speed = k1 * (speed + dt1 * force) + (g1 * c1) * force
        field = field + dt1 * speed
        force = part[4 * c] + mu * f2[2 * c] + c1 * (part[4 * c + 2] + mu * f2[2 * c + 1])
        speed = k2 * (speed + dt2 * force) + (g2 * c2) * force
        pos[c] = field + dt2 * speed
        vel[c] = speed


def call(kernel, out_shape, specs, *args, **more):
    return pl.pallas_call(
        kernel,
        out_shape=out_shape,
        in_specs=specs,
        out_specs=jax.tree.map(lambda _: VMEM, out_shape),
        compiler_params=pltpu.CompilerParams(vmem_limit_bytes=40 * 2**20),
        **more,
    )(*args)


def f32(*shape):
    return jax.ShapeDtypeStruct(shape, jnp.float32)


def local(positions, velocity, flow_down, flow_up, flow_mask, resets, dt_index):
    nstrips, nz, nx = lax.axis_size("strip"), lax.axis_size("z"), lax.axis_size("x")
    section, strip = lax.axis_index(GZ), lax.axis_index("strip")
    _, comps, rows, cols = positions.shape
    core = f32(comps, rows, cols)
    marks = (resets[:, 0] == 1).astype(jnp.float32)
    tile = jnp.broadcast_to(jnp.pad(marks, (0, 5))[:, None], (8, cols))
    start = call(
        start_kernel,
        f32(4 * rows + 8, cols),
        [ANY] * 3,
        positions.reshape(-1, cols), velocity.reshape(-1, cols), tile,
        scratch_shapes=[pltpu.SemaphoreType.DMA((3,))],
    )
    even, odd = swap(start, GZ, nz * nx)
    marks = jnp.concatenate([marks] + [x[4 * rows : 4 * rows + 3, 0] for x in (even, odd)])
    dts = 0.1 * jnp.power(jnp.float32(1.25), dt_index.astype(jnp.float32))
    ids = jnp.reshape(strip, (1,))
    is_odd = section % 2 == 1
    valid = jnp.stack([section > 0, section < nz * nx - 1]).astype(jnp.int32)
    masks = (flow_mask[:, 0] * valid[:, None, None]).astype(jnp.float32)
    masks = jnp.where(is_odd, masks, masks[::-1])
    flow_even = jnp.where(is_odd, flow_down[0], flow_up[0])
    flow_odd = jnp.where(is_odd, flow_up[0], flow_down[0])
    own = start[: 4 * rows].reshape(2, comps, rows, cols)
    fields = [own[0], own[1], flow_even, flow_odd, masks]
    size = -(-2 * sum(DEEP) // 8) * 8
    rims = call(
        rims_kernel,
        (f32(size, cols), f32(size, cols)),
        [SMEM] + [VMEM] * 7,
        ids, *fields, even, odd,
    )
    first, second = swap(tuple(rims), "strip", nstrips)
    below = jnp.where(strip % 2 == 1, second, first)
    above = jnp.where(strip % 2 == 1, first, second)
    for x in (even, odd):
        fields += list(x[: 4 * rows].reshape(2, comps, rows, cols))
    wide, at = [], 0
    for f, d in zip(fields, DEEP):
        lower = below[at : at + 2 * d].reshape(2, d, cols)
        upper = above[at : at + 2 * d].reshape(2, d, cols)
        at += 2 * d
        gap = jnp.zeros((2, 8 - 2 * d, cols), jnp.float32)
        wide.append(jnp.concatenate([f, lower, gap, upper], axis=1))
    u, v, fe, fo, mk, ue, ve, uo, vo = wide

    p, ptails = call(
        lambda *refs: first_kernel(nstrips, *refs),
        (f32(4 * rows + 8, cols), f32(32, cols)),
        [SMEM] * 2 + [VMEM] * 9,
        ids, marks, u, ue, uo, v, ve, vo, fe, fo, mk,
    )
    pe, po = swap(p, GZ, nz * nx)
    g, gtails = call(
        lambda *refs: second_kernel(nstrips, *refs),
        (f32(2 * rows + 8, cols), f32(16, cols)),
        [SMEM] * 2 + [VMEM] * 7,
        ids, marks, p, ptails, pe, po, fe, fo, mk,
    )
    ge, go = swap(g, GZ, nz * nx)
    part, w2, early = call(
        lambda *refs: third_kernel(nstrips, *refs),
        (f32(4 * comps, rows, cols), f32(4 * comps, rows, cols), f32(1, 128)),
        [SMEM] * 3 + [VMEM] * 12,
        ids, dts, marks, v, ve, vo, p, ptails, pe, po, g, gtails, fe, fo, mk,
        cost_estimate=pl.CostEstimate(flops=6_000_000, bytes_accessed=4_000_000, transcendentals=0),
    )
    f2, sums = call(
        lambda *refs: fourth_kernel(nstrips, *refs),
        (f32(2 * comps, rows, cols), f32(1, 128)),
        [SMEM] * 3 + [VMEM] * 8,
        ids, dts, marks, part, w2, early, ge, go, fe, fo, mk,
    )
    near = nx * nstrips
    sums = lax.all_to_all(jnp.broadcast_to(sums, (near, 1, 128)), ("x", "strip"), 0, 0)
    sums = jnp.sum(sums, axis=0)
    sums = lax.all_to_all(jnp.broadcast_to(sums, (nz, 1, 128)), "z", 0, 0)
    pos, vel = call(
        last_kernel,
        (core, core),
        [SMEM] * 2 + [VMEM] * 7,
        dts, marks, sums, u, v, p, g, part, f2,
    )
    return pos[None], vel[None]


def solution(mesh):
    sections, strips = mesh.devices.shape
    split = mesh.devices.reshape(sections // X_CHIPS, X_CHIPS, strips)
    field = P(GZ, None, "strip", None)
    placed = (field, field, field, field, P(None, GZ, "strip", None), P(None, GZ), P())
    return jax.shard_map(
        local,
        mesh=Mesh(split, ("z", "x", "strip")),
        in_specs=placed,
        out_specs=(field, field),
        check_vma=False,
    )
```

time: 105 us -> 101 us (0.962)
  waiting for transfers between devices: 17.7 us -> 13.9 us
  blocking collectives: 44.3 us -> 42 us
  Pallas kernels: 6.78 us -> 8.19 us
  local copies, waits for them, and re-layouts: 3.16 us -> 4.3 us
  other arithmetic: 2.39 us -> 1.28 us
    ppermute x8, waiting for transfers between devices: 17.7 us -> 13.9 us  [the longest x4 13.6 us: swap(): lax.ppermute(values[0], axes, first)]
    unnamed x12, local copies, waits for them, and re-layouts: 0.94 us -> 3.4 us
    all_to_all x1, blocking collectives: 18.4 us -> 16 us  [local(): lax.all_to_all(jnp.broadcast_to(sums, (near, 1, 128)), ('x', 'strip'), 0, 0)]
    pallas_call x4 -> x7, Pallas kernels: 6.78 us -> 8.19 us  [call(): pl.pallas_call(kernel, out_shape=out_shape, in_specs=specs, out_specs=jax...]
    concatenate x2 -> x0, other arithmetic: 1.14 us -> none  [local(): even, odd = swap(jnp.concatenate(start, axis=0), nz * nx)]
    concatenate x2 -> x0, local copies, waits for them, and re-layouts: 1.05 us -> none  [packed(): return jnp.concatenate(slabs + [spare], axis=0)]
  transfers between devices with their start and end apart: 8 -> 8, of which waited for: 4 -> 5; matrix products, arithmetic and copies ran while one was open for 2% -> 1% of each run, Pallas kernels for 0% -> 2%
where the time goes in v3:
time: 101 us; the launch traced here: 100 us
  blocking collectives  42 us (42%)
  starting transfers between devices  29.4 us (29%)
  waiting for transfers between devices  13.9 us (14%)
  Pallas kernels  8.19 us (8%)
  local copies, waits for them, and re-layouts  4.3 us (4%)
  other arithmetic  1.28 us (1%)
    all_to_all x1, blocking collectives, local(): sums = lax.all_to_all(jnp.broadcast_to(sums, (nz, 1, 128)), 'z', 0, 0)  26 us
    ppermute x4, starting transfers between devices, swap(): lax.ppermute(values[0], axes, first)  20.5 us
    all_to_all x1, blocking collectives, local(): lax.all_to_all(jnp.broadcast_to(sums, (near, 1, 128)), ('x', 'strip'), 0, 0)  16 us
    ppermute x4, waiting for transfers between devices, swap(): lax.ppermute(values[0], axes, first)  13.6 us
    ppermute x4, starting transfers between devices, swap(): lax.ppermute(values[1], axes, second)  8.92 us
    pallas_call x7, Pallas kernels, call(): pl.pallas_call(kernel, out_shape=out_shape, in_specs=specs, out_specs=jax...  8.19 us
    unnamed x12, local copies, waits for them, and re-layouts  3.4 us
  transfers between devices with their start and end apart: 8, of which 5 were waited for; matrix products, arithmetic and copies ran while one was open for 1% of the time, Pallas kernels for 2%

profile of v3, /device:TPU:1, one launch (start us, length us, event | category | flops | bytes accessed | tf_op | source)
XLA Modules:
  0.0 100.1 jit_solution(18438316229958411646)
XLA Ops:
  0.6 0.7 fusion.1
  1.4 0.9 copy-done
  2.3 0.9 copy-done.1
  3.7 0.7 collective-permute-start.1
  4.3 6.4 %collective-permute-start = (f32[136,640]{1,0:T(8,128)S(1)}, f32[136,640]{1,0:T(8,128)S(1)}, u32[]{:S(2)}, u32[]{:S(2)}) collective-permute-start(f32[136,640]{1,0:T(8,128)S(1)} %shard_map.86), channel_id=1, source_target_pairs={{0,8},{8,0},{16,24},{24,16},{32,40},{40,32},{48,56},{56,48},{64,72... | collective-permute-start | bytes 1044488 | tf_op jit(solution)/shard_map/ppermute | solution.py:20
  10.9 0.8 copy-done.2
  12.0 0.7 copy-done.3
  12.8 3.2 %collective-permute-done.even = f32[136,640]{1,0:T(8,128)S(1)} collective-permute-done((f32[136,640]{1,0:T(8,128)S(1)}, f32[136,640]{1,0:T(8,128)S(1)}, u32[]{:S(2)}, u32[]{:S(2)}) %collective-permute-start) | collective-permute-done | bytes 348192 | tf_op jit(solution)/shard_map/ppermute | solution.py:20
  16.1 6.9 %collective-permute-start.2 = (f32[48,640]{1,0:T(8,128)S(1)}, f32[48,640]{1,0:T(8,128)S(1)}, u32[]{:S(2)}, u32[]{:S(2)}) collective-permute-start(f32[48,640]{1,0:T(8,128)S(1)} %get-tuple-element.15), channel_id=1, source_target_pairs={{1,2},{2,1},{3,4},{4,3},{5,6},{6,5},{9,10},{10,9},{11,12},{12,11},... | collective-permute-start | bytes 368648 | tf_op jit(solution)/shard_map/ppermute | solution.py:20
  23.0 1.9 %collective-permute-start.3 = (f32[48,640]{1,0:T(8,128)S(1)}, f32[48,640]{1,0:T(8,128)S(1)}, u32[]{:S(2)}, u32[]{:S(2)}) collective-permute-start(f32[48,640]{1,0:T(8,128)S(1)} %get-tuple-element.16), channel_id=1, source_target_pairs={{0,1},{1,0},{2,3},{3,2},{4,5},{5,4},{6,7},{7,6},{8,9},{9,8},{10,11... | collective-permute-start | bytes 368648 | tf_op jit(solution)/shard_map/ppermute | solution.py:20
  25.6 0.7 collective-permute-done.3
  27.0 1.4 %shard_map.88 = (f32[136,640]{1,0:T(8,128)S(1)}, f32[32,640]{1,0:T(8,128)S(1)}) custom-call(s32[1]{0:T(128)} %bitcast.3.ids.refs_0_, f32[9]{0:T(128)S(1)} %pad_maximum_fusion.9.refs_1_.refs_2_.marks, f32[2,40,640]{2,1,0:T(8,128)S(1)} %get-tuple-element.64.refs_2_.u, f32[2,40,640]{2,1,0:T(8,128)S(1)} %get-tuple-element.63.refs_3_, ...), custom_call_target="tpu_custom_call" | custom-call | tf_op jit(solution)/shard_map/pallas_call | solution.py:333
  28.4 0.7 collective-permute-start.5
  29.1 5.6 %collective-permute-start.4 = (f32[136,640]{1,0:T(8,128)S(1)}, f32[136,640]{1,0:T(8,128)S(1)}, u32[]{:S(2)}, u32[]{:S(2)}) collective-permute-start(f32[136,640]{1,0:T(8,128)S(1)} %get-tuple-element.17.refs_2_.refs_6_.p), channel_id=1, source_target_pairs={{0,8},{8,0},{16,24},{24,16},{32,40},{40,32},{48,56},{56,48},{64,72... | collective-permute-start | bytes 1044488 | tf_op jit(solution)/shard_map/ppermute | solution.py:20
  34.7 8.1 %collective-permute-done.4.refs_4_.refs_8_ = f32[136,640]{1,0:T(8,128)S(1)} collective-permute-done((f32[136,640]{1,0:T(8,128)S(1)}, f32[136,640]{1,0:T(8,128)S(1)}, u32[]{:S(2)}, u32[]{:S(2)}) %collective-permute-start.4) | collective-permute-done | bytes 348192 | tf_op jit(solution)/shard_map/ppermute | solution.py:20
  42.8 1.0 shard_map.89
  43.8 0.7 collective-permute-start.7
  44.5 6.6 %collective-permute-start.6 = (f32[72,640]{1,0:T(8,128)S(1)}, f32[72,640]{1,0:T(8,128)S(1)}, u32[]{:S(2)}, u32[]{:S(2)}) collective-permute-start(f32[72,640]{1,0:T(8,128)S(1)} %get-tuple-element.19.refs_10_.g), channel_id=1, source_target_pairs={{0,8},{8,0},{16,24},{24,16},{32,40},{40,32},{48,56},{56,48},{64,72... | collective-permute-start | bytes 552968 | tf_op jit(solution)/shard_map/ppermute | solution.py:20
  51.1 2.1 %shard_map.90 = (f32[8,32,640]{2,1,0:T(8,128)S(1)}, f32[8,32,640]{2,1,0:T(8,128)S(1)}, f32[1,128]{1,0:T(1,128)S(1)}) custom-call(s32[1]{0:T(128)} %bitcast.3.ids.refs_0_, f32[3]{0:T(128)S(1)} %power_multiply_fusion.refs_1_.dts, f32[9]{0:T(128)S(1)} %pad_maximum_fusion.9.refs_1_.refs_2_.marks, f32[2,40,640]{2,1,0:T(8,128)S(1)} %get-tuple-element.61.refs_5_.refs_3_.v, ...), custom_call_target="tpu_custom_call" | custom-call | flops 6000000 | bytes 4000000 | tf_op jit(solution)/shard_map/pallas_call | solution.py:333
  53.2 1.6 %collective-permute-done.6.refs_6_ = f32[72,640]{1,0:T(8,128)S(1)} collective-permute-done((f32[72,640]{1,0:T(8,128)S(1)}, f32[72,640]{1,0:T(8,128)S(1)}, u32[]{:S(2)}, u32[]{:S(2)}) %collective-permute-start.6) | collective-permute-done | bytes 184352 | tf_op jit(solution)/shard_map/ppermute | solution.py:20
  54.8 1.2 %shard_map.91 = (f32[4,32,640]{2,1,0:T(8,128)S(1)}, f32[1,128]{1,0:T(1,128)S(1)}) custom-call(s32[1]{0:T(128)} %bitcast.3.ids.refs_0_, f32[3]{0:T(128)S(1)} %power_multiply_fusion.refs_1_.dts, f32[9]{0:T(128)S(1)} %pad_maximum_fusion.9.refs_1_.refs_2_.marks, f32[8,32,640]{2,1,0:T(8,128)S(1)} %get-tuple-element.21.refs_3_.part, ...), custom_call_target="tpu_custom_call" | custom-call | tf_op jit(solution)/shard_map/pallas_call | solution.py:333
  56.0 16.0 %all_to_all.10 = f32[32,1,128]{2,1,0:T(1,128)S(1)} all-to-all(f32[32,1,128]{2,1,0:T(1,128)S(1)} %broadcast_in_dim.20), channel_id=1, replica_groups=mesh['z'=16,'x'=4,'strip'=8] {'x','strip'}, dimensions={0} | all-to-all | bytes 32768 | tf_op jit(solution)/shard_map/all_to_all | solution.py:422
  72.0 26.0 %all_to_all.11.parts = f32[16,1,128]{2,1,0:T(1,128)S(1)} all-to-all(f32[16,1,128]{2,1,0:T(1,128)S(1)} %broadcast_in_dim.21), channel_id=1, replica_groups=mesh['z'=16,'x'=4,'strip'=8] {'z'}, dimensions={0} | all-to-all | bytes 16384 | tf_op jit(solution)/shard_map/all_to_all | solution.py:424
  98.0 2.0 %shard_map.92 = (f32[2,32,640]{2,1,0:T(8,128)}, f32[2,32,640]{2,1,0:T(8,128)}) custom-call(f32[3]{0:T(128)S(1)} %power_multiply_fusion.refs_1_.dts, f32[9]{0:T(128)S(1)} %pad_maximum_fusion.9.refs_1_.refs_2_.marks, f32[16,1,128]{2,1,0:T(1,128)S(1)} %all_to_all.11.parts, f32[2,40,640]{2,1,0:T(8,128)S(1)} %get-tuple-element.64.refs_2_.u, ...), custom_call_target="tpu_custom_call" | custom-call | tf_op jit(solution)/shard_map/pallas_call | solution.py:333
  (57 shorter events, 2.4 us)
Async XLA Ops:
  1.4 0.9 copy-start
  2.3 0.9 copy-start.1
  3.7 9.1 %collective-permute-start.1 = (f32[136,640]{1,0:T(8,128)S(1)}, f32[136,640]{1,0:T(8,128)S(1)}, u32[]{:S(2)}, u32[]{:S(2)}) collective-permute-start(f32[136,640]{1,0:T(8,128)S(1)} %shard_map.86), channel_id=1, source_target_pairs={{8,16},{16,8},{24,32},{32,24},{40,48},{48,40},{56,64},{64,56},{72,... | collective-permute-start | bytes 1044488 | tf_op jit(solution)/shard_map/ppermute | solution.py:20
  4.3 11.7 %collective-permute-start = (f32[136,640]{1,0:T(8,128)S(1)}, f32[136,640]{1,0:T(8,128)S(1)}, u32[]{:S(2)}, u32[]{:S(2)}) collective-permute-start(f32[136,640]{1,0:T(8,128)S(1)} %shard_map.86), channel_id=1, source_target_pairs={{0,8},{8,0},{16,24},{24,16},{32,40},{40,32},{48,56},{56,48},{64,72... | collective-permute-start | bytes 1044488 | tf_op jit(solution)/shard_map/ppermute | solution.py:20
  10.8 0.9 copy-start.2
  11.8 0.9 copy-start.3
  11.8 1.0 copy-start.4
  16.1 9.4 %collective-permute-start.2 = (f32[48,640]{1,0:T(8,128)S(1)}, f32[48,640]{1,0:T(8,128)S(1)}, u32[]{:S(2)}, u32[]{:S(2)}) collective-permute-start(f32[48,640]{1,0:T(8,128)S(1)} %get-tuple-element.15), channel_id=1, source_target_pairs={{1,2},{2,1},{3,4},{4,3},{5,6},{6,5},{9,10},{10,9},{11,12},{12,11},... | collective-permute-start | bytes 368648 | tf_op jit(solution)/shard_map/ppermute | solution.py:20
  23.0 3.2 %collective-permute-start.3 = (f32[48,640]{1,0:T(8,128)S(1)}, f32[48,640]{1,0:T(8,128)S(1)}, u32[]{:S(2)}, u32[]{:S(2)}) collective-permute-start(f32[48,640]{1,0:T(8,128)S(1)} %get-tuple-element.16), channel_id=1, source_target_pairs={{0,1},{1,0},{2,3},{3,2},{4,5},{5,4},{6,7},{7,6},{8,9},{9,8},{10,11... | collective-permute-start | bytes 368648 | tf_op jit(solution)/shard_map/ppermute | solution.py:20
  28.4 6.3 %collective-permute-start.5 = (f32[136,640]{1,0:T(8,128)S(1)}, f32[136,640]{1,0:T(8,128)S(1)}, u32[]{:S(2)}, u32[]{:S(2)}) collective-permute-start(f32[136,640]{1,0:T(8,128)S(1)} %get-tuple-element.17.refs_2_.refs_6_.p), channel_id=1, source_target_pairs={{8,16},{16,8},{24,32},{32,24},{40,48},{48,40},{56,64},{64,56},{72,... | collective-permute-start | bytes 1044488 | tf_op jit(solution)/shard_map/ppermute | solution.py:20
  29.1 13.7 %collective-permute-start.4 = (f32[136,640]{1,0:T(8,128)S(1)}, f32[136,640]{1,0:T(8,128)S(1)}, u32[]{:S(2)}, u32[]{:S(2)}) collective-permute-start(f32[136,640]{1,0:T(8,128)S(1)} %get-tuple-element.17.refs_2_.refs_6_.p), channel_id=1, source_target_pairs={{0,8},{8,0},{16,24},{24,16},{32,40},{40,32},{48,56},{56,48},{64,72... | collective-permute-start | bytes 1044488 | tf_op jit(solution)/shard_map/ppermute | solution.py:20
  43.8 7.3 %copy-start.5 = (s32[3]{0:T(128)S(1)}, s32[3]{0:T(128)}, u32[]{:S(2)}) copy-start(s32[3]{0:T(128)} %param.13) | copy-start | bytes 40
  43.8 9.4 %collective-permute-start.7 = (f32[72,640]{1,0:T(8,128)S(1)}, f32[72,640]{1,0:T(8,128)S(1)}, u32[]{:S(2)}, u32[]{:S(2)}) collective-permute-start(f32[72,640]{1,0:T(8,128)S(1)} %get-tuple-element.19.refs_10_.g), channel_id=1, source_target_pairs={{8,16},{16,8},{24,32},{32,24},{40,48},{48,40},{56,64},{64,56},{72,... | collective-permute-start | bytes 552968 | tf_op jit(solution)/shard_map/ppermute | solution.py:20
  44.5 10.3 %collective-permute-start.6 = (f32[72,640]{1,0:T(8,128)S(1)}, f32[72,640]{1,0:T(8,128)S(1)}, u32[]{:S(2)}, u32[]{:S(2)}) collective-permute-start(f32[72,640]{1,0:T(8,128)S(1)} %get-tuple-element.19.refs_10_.g), channel_id=1, source_target_pairs={{0,8},{8,0},{16,24},{24,16},{32,40},{40,32},{48,56},{56,48},{64,72... | collective-permute-start | bytes 552968 | tf_op jit(solution)/shard_map/ppermute | solution.py:20

commit v4 on v3

--- a/solution.py
+++ b/solution.py
@@ -75,8 +75,21 @@
         return self.mask_even * self.flow_even[comp] + self.mask_odd * self.flow_odd[comp]
 
 
-def stencil_of(ids, nstrips, fe, fo, mk):
-    return Stencil(ids[0], nstrips, (fe[0], fe[1]), (fo[0], fo[1]), mk[0], mk[1])
+U, V, FE, FO, MK, UE, VE, UO, VO = range(9)
+
+
+def ring(core, tails, field, c):
+    at = 8 * (2 * field + c)
+    return jnp.concatenate([core, tails[at : at + 8]], axis=0)
+
+
+def part(packet, rows, at):
+    return packet[rows * at : rows * at + rows]
+
+
+def stencil_of(ids, nstrips, fe, fo, mk, tails):
+    fields = [[ring(x[c], tails, i, c) for c in range(2)] for x, i in ((fe, FE), (fo, FO), (mk, MK))]
+    return Stencil(ids[0], nstrips, *fields[:2], *fields[2])
 
 
 def factors(reset, alpha):
@@ -98,23 +111,26 @@
     return weights
 
 
-def start_kernel(pos, vel, tile, out, sems):
+def start_kernel(rs, pos, vel, out, sems):
     rows = pos.shape[0]
     copies = [
-        pltpu.make_async_copy(src, out.at[pl.ds(at, size)], sems.at[i])
-        for i, (src, at, size) in enumerate(((pos, 0, rows), (vel, rows, rows), (tile, 2 * rows, 8)))
+        pltpu.make_async_copy(src, out.at[pl.ds(at, rows)], sems.at[i])
+        for i, (src, at) in enumerate(((pos, 0), (vel, rows)))
     ]
     for copy in copies:
         copy.start()
+    for i in range(8):
+        mark = jnp.where(rs[i] == 1, jnp.float32(1.0), jnp.float32(0.0)) if i < 3 else 0.0
+        out[2 * rows + i : 2 * rows + i + 1] = jnp.full((1, out.shape[1]), mark, jnp.float32)
     for copy in copies:
         copy.wait()
 
 
-def rims_kernel(ids, u, v, fe, fo, mk, even, odd, first, second):
-    rows = u.shape[1]
-    sides = [(x, rows * at) for x in (even, odd) for at in range(4)]
-    comps = [(f.at[c], 0) for f in (u, v, fe, fo, mk) for c in range(2)]
-    comps += [(x, at) for x, at in sides]
+def rims_kernel(ids, start, fe, fo, mk, even, odd, first, second):
+    rows = fe.shape[1]
+    comps = [(start, rows * at) for at in range(4)]
+    comps += [(x.at[c], 0) for x in (fe, fo, mk) for c in range(2)]
+    comps += [(x, rows * at) for x in (even, odd) for at in range(4)]
 
     def fill(upper, lower):
         at = 0
@@ -135,52 +151,77 @@
         fill(second, first)
 
 
-def first_kernel(nstrips, ids, marks, u, ue, uo, v, ve, vo, fe, fo, mk, packet, tails):
-    op = stencil_of(ids, nstrips, fe, fo, mk)
-    rows = u.shape[1] - 8
-    rho, rho_even, rho_odd = [w[0] for w in weights_of(marks)]
-    end = 4 * rows
-    for c in range(2):
-        f0 = op(u[c], ue[c], uo[c]) + op.bias(c)
-        h = op(rho * v[c], rho_even * ve[c], rho_odd * vo[c])
-        for at, value in ((c, f0), (2 + c, h)):
-            packet[rows * at : rows * at + rows] = value[:rows]
-            tails[8 * at : 8 * at + 8] = value[rows:]
+def first_kernel(nstrips, ids, start, even, odd, fe, fo, mk, first, second, packet, ftails, tails):
+    tails[...] = jnp.zeros(tails.shape, jnp.float32)
+
+    def fill(below, above):
+        at = 0
+        for i in range(2 * len(DEEP)):
+            deep = DEEP[i // 2]
+            tails[8 * i : 8 * i + deep] = below[at : at + deep]
+            tails[8 * i + 8 - deep : 8 * i + 8] = above[at : at + deep]
+            at += deep
+
+    @pl.when(ids[0] % 2 == 1)
+    def _():
+        fill(second, first)
+
+    @pl.when(ids[0] % 2 == 0)
+    def _():
+        fill(first, second)
+
+    op = stencil_of(ids, nstrips, fe, fo, mk, tails)
+    rows = fe.shape[1]
+    end = 2 * rows
+    packet[end:] = jnp.zeros((8, packet.shape[1]), jnp.float32)
+    for c in range(2):
+        us = [ring(part(x, rows, c), tails, i, c) for x, i in ((start, U), (even, UE), (odd, UO))]
+        f0 = op(*us) + op.bias(c)
+        packet[rows * c : rows * c + rows] = f0[:rows]
+        ftails[8 * c : 8 * c + 8] = f0[rows:]
         packet[end + 3 * c : end + 3 * c + 2] = f0[rows : rows + 2]
         last = end + (7, 2)[c]
         packet[last : last + 1] = f0[rows + 7 :]
-        packet[end + 5 + c : end + 6 + c] = h[rows : rows + 1]
-
-
-def own_ring(packet, tails, rows, at):
-    return jnp.concatenate([packet[rows * at : rows * at + rows], tails[8 * at : 8 * at + 8]], axis=0)
-
-
-def side_ring(packet, rows, at, size, shift):
-    tail = packet[size * rows :]
-    tail = pltpu.roll(tail, 8 - shift, 0) if shift else tail
-    return jnp.concatenate([packet[rows * at : rows * at + rows], tail], axis=0)
-
-
-def side_force(packet, rows, c):
-    return side_ring(packet, rows, c, 4, 3 * c)
-
-
-def side_h(packet, rows, c):
-    return side_ring(packet, rows, 2 + c, 4, 5 + c)
-
-
-def second_kernel(nstrips, ids, marks, p, ptails, pe, po, fe, fo, mk, packet, tails):
-    op = stencil_of(ids, nstrips, fe, fo, mk)
-    rows = mk.shape[1] - 8
-    rho, rho_even, rho_odd = [w[0] for w in weights_of(marks)]
+
+
+def velocities(start, even, odd, tails, rows, c):
+    return [ring(part(x, rows, 2 + c), tails, i, c) for x, i in ((start, V), (even, VE), (odd, VO))]
+
+
+def beside_kernel(nstrips, ids, marks, start, even, odd, f, ftails, fe, fo, mk, tails, packet, htails, inner):
+    op = stencil_of(ids, nstrips, fe, fo, mk, tails)
+    rows = fe.shape[1]
+    rhos = [w[0] for w in weights_of(marks)]
     packet[2 * rows :] = jnp.zeros((8, packet.shape[1]), jnp.float32)
     for c in range(2):
-        f0 = own_ring(p, ptails, rows, c)
-        g = op(rho * f0, rho_even * side_force(pe, rows, c), rho_odd * side_force(po, rows, c))
+        h = op(*[rho * x for rho, x in zip(rhos, velocities(start, even, odd, tails, rows, c))])
+        packet[rows * c : rows * c + rows] = h[:rows]
+        packet[2 * rows + c : 2 * rows + c + 1] = h[rows : rows + 1]
+        htails[8 * c : 8 * c + 8] = h[rows:]
+        inner[c] = op.inner(rhos[0] * own_ring(f, ftails, rows, c))
+
+
+def own_ring(packet, tails, rows, c):
+    return ring(part(packet, rows, c), tails, 0, c)
+
+
+def side_ring(packet, rows, c, step):
+    tail = packet[2 * rows :]
+    tail = pltpu.roll(tail, 8 - step * c, 0) if c else tail
+    return jnp.concatenate([part(packet, rows, c), tail], axis=0)
+
+
+def second_kernel(nstrips, ids, marks, inner, pe, po, fe, fo, mk, tails, packet, gtails):
+    op = stencil_of(ids, nstrips, fe, fo, mk, tails)
+    rows = mk.shape[1]
+    _, rho_even, rho_odd = [w[0] for w in weights_of(marks)]
+    packet[2 * rows :] = jnp.zeros((8, packet.shape[1]), jnp.float32)
+    for c in range(2):
+        even, odd = side_ring(pe, rows, c, 3), side_ring(po, rows, c, 3)
+        g = inner[c] + (rho_even * op.even(even) + rho_odd * op.odd(odd))
         packet[rows * c : rows * c + rows] = g[:rows]
         packet[2 * rows + c : 2 * rows + c + 1] = g[rows : rows + 1]
-        tails[8 * c : 8 * c + 8] = g[rows:]
+        gtails[8 * c : 8 * c + 8] = g[rows:]
 
 
 def products(fields, pairs):
@@ -222,33 +263,33 @@
     return parts if totals is None else [x + y for x, y in zip(totals, parts)]
 
 
-def third_kernel(nstrips, ids, dts, marks, v, ve, vo, p, ptails, pe, po, g, gtails, fe, fo, mk, f2, w2, sums):
-    op = stencil_of(ids, nstrips, fe, fo, mk)
-    rows = mk.shape[1] - 8
+def third_kernel(nstrips, ids, dts, marks, start, even, odd, f, ftails, pe, po, h, htails, he, ho, g, gtails, fe, fo, mk, tails, f2, w2, sums):
+    op = stencil_of(ids, nstrips, fe, fo, mk, tails)
+    rows = mk.shape[1]
     dt0, dt1, dt2 = dts[0], dts[1], dts[2]
     kappa = 1.0 - gamma()
     weights = weights_of(marks)
     totals = None
     for c in range(2):
-        f0s = [own_ring(p, ptails, rows, c), side_force(pe, rows, c), side_force(po, rows, c)]
-        hs = [own_ring(p, ptails, rows, 2 + c), side_h(pe, rows, c), side_h(po, rows, c)]
-        vs = [v[c], ve[c], vo[c]]
-        ts = [f0 + (dt0 * kappa) * h for f0, h in zip(f0s, hs)]
+        f0s = [own_ring(f, ftails, rows, c), side_ring(pe, rows, c, 3), side_ring(po, rows, c, 3)]
+        hs = [own_ring(h, htails, rows, c), side_ring(he, rows, c, 1), side_ring(ho, rows, c, 1)]
+        vs = velocities(start, even, odd, tails, rows, c)
+        ts = [x + (dt0 * kappa) * y for x, y in zip(f0s, hs)]
         g0 = dt0 * own_ring(g, gtails, rows, c)
         one = [k1 * ((rho * kappa) * v0 + dt1 * t) for v0, t, (rho, k1, _) in zip(vs, ts, weights)]
         mix = [g1 * t for t, (_, _, g1) in zip(ts, weights)]
         rho, k1, g1 = weights[0]
         mu = k1 * (rho * f0s[0] + dt1 * g0)
         both = g1 * g0
-        sides = [(w[1] * w[0]) * f0 for f0, w in zip(f0s[1:], weights[1:])]
+        sides = [(w[1] * w[0]) * x for x, w in zip(f0s[1:], weights[1:])]
         forces = [
             ts[0] + dt1 * op(*one),
             g0 + dt1 * op(mu, *sides),
             dt1 * op(*mix),
             dt1 * op.inner(both),
         ]
-        forces = [f[:rows] for f in forces]
-        kicked = [x[:rows] + dt2 * f for x, f in zip((one[0], mu, mix[0], both), forces)]
+        forces = [x[:rows] for x in forces]
+        kicked = [x[:rows] + dt2 * y for x, y in zip((one[0], mu, mix[0], both), forces)]
         for i in range(4):
             f2[4 * c + i] = forces[i]
             w2[4 * c + i] = kicked[i]
@@ -260,19 +301,19 @@
     sums[...] = lanes_of(totals, 0)
 
 
-def fourth_kernel(nstrips, ids, dts, marks, part, w2, early, ge, go, fe, fo, mk, f2, sums):
-    op = stencil_of(ids, nstrips, fe, fo, mk)
-    rows = part.shape[1]
+def fourth_kernel(nstrips, ids, dts, marks, known, w2, early, ge, go, fe, fo, mk, tails, f2, sums):
+    op = stencil_of(ids, nstrips, fe, fo, mk, tails)
+    rows = known.shape[1]
     dt0, dt1, dt2 = dts[0], dts[1], dts[2]
     weights = weights_of(marks)
     totals = None
     for c in range(2):
-        even = op.even(side_ring(ge, rows, c, 2, c))[:rows]
-        odd = op.odd(side_ring(go, rows, c, 2, c))[:rows]
+        even = op.even(side_ring(ge, rows, c, 1))[:rows]
+        odd = op.odd(side_ring(go, rows, c, 1))[:rows]
         scale = dt1 * dt0
         mu = scale * dt1 * (weights[1][1] * even + weights[2][1] * odd)
         both = scale * (weights[1][2] * even + weights[2][2] * odd)
-        forces = [part[4 * c], part[4 * c + 1] + mu, part[4 * c + 2], part[4 * c + 3] + both]
+        forces = [known[4 * c], known[4 * c + 1] + mu, known[4 * c + 2], known[4 * c + 3] + both]
         kicked = [w2[4 * c], w2[4 * c + 1] + dt2 * mu, w2[4 * c + 2], w2[4 * c + 3] + dt2 * both]
         f2[2 * c] = forces[1]
         f2[2 * c + 1] = forces[3]
@@ -295,7 +336,7 @@
     return jnp.sqrt(kicked / (force + 1e-06))
 
 
-def last_kernel(dts, marks, parts, u, v, p, g, part, f2, pos, vel):
+def last_kernel(dts, marks, parts, start, f, h, g, known, f2, pos, vel):
     rows = pos.shape[1]
     sums = jnp.sum(parts[...], axis=0)
     lanes = [sums[:, i : i + 1] for i in range(N_EARLY + N_LATE)]
@@ -317,25 +358,25 @@
     alpha = factors(marks[1], factors(marks[0], jnp.float32(0.1))[0])[0]
     _, k2, g2 = factors(marks[2], alpha)
     for c in range(2):
-        f0, h = p[rows * c : rows * c + rows], p[rows * (2 + c) : rows * (2 + c) + rows]
-        speed = rho * (kappa * v[c, :rows] + mu * f0)
-        field = u[c, :rows] + dt0 * speed
-        force = f0 + (dt0 * kappa) * h + (mu * dt0) * g[rows * c : rows * c + rows]
+        f0 = part(f, rows, c)
+        speed = rho * (kappa * part(start, rows, 2 + c) + mu * f0)
+        field = part(start, rows, c) + dt0 * speed
+        force = f0 + (dt0 * kappa) * part(h, rows, c) + (mu * dt0) * part(g, rows, c)
         speed = k1 * (speed + dt1 * force) + (g1 * c1) * force
         field = field + dt1 * speed
-        force = part[4 * c] + mu * f2[2 * c] + c1 * (part[4 * c + 2] + mu * f2[2 * c + 1])
+        force = known[4 * c] + mu * f2[2 * c] + c1 * (known[4 * c + 2] + mu * f2[2 * c + 1])
         speed = k2 * (speed + dt2 * force) + (g2 * c2) * force
         pos[c] = field + dt2 * speed
         vel[c] = speed
 
 
-def call(kernel, out_shape, specs, *args, **more):
+def call(kernel, out_shape, specs, *args, room=40 * 2**20, **more):
     return pl.pallas_call(
         kernel,
         out_shape=out_shape,
         in_specs=specs,
         out_specs=jax.tree.map(lambda _: VMEM, out_shape),
-        compiler_params=pltpu.CompilerParams(vmem_limit_bytes=40 * 2**20),
+        compiler_params=pltpu.CompilerParams(vmem_limit_bytes=room),
         **more,
     )(*args)
 
@@ -350,13 +391,13 @@
     _, comps, rows, cols = positions.shape
     core = f32(comps, rows, cols)
     marks = (resets[:, 0] == 1).astype(jnp.float32)
-    tile = jnp.broadcast_to(jnp.pad(marks, (0, 5))[:, None], (8, cols))
     start = call(
         start_kernel,
         f32(4 * rows + 8, cols),
-        [ANY] * 3,
-        positions.reshape(-1, cols), velocity.reshape(-1, cols), tile,
-        scratch_shapes=[pltpu.SemaphoreType.DMA((3,))],
+        [SMEM] + [ANY] * 2,
+        resets[:, 0], positions.reshape(-1, cols), velocity.reshape(-1, cols),
+        room=None,
+        scratch_shapes=[pltpu.SemaphoreType.DMA((2,))],
     )
     even, odd = swap(start, GZ, nz * nx)
     marks = jnp.concatenate([marks] + [x[4 * rows : 4 * rows + 3, 0] for x in (even, odd)])
@@ -368,55 +409,52 @@
     masks = jnp.where(is_odd, masks, masks[::-1])
     flow_even = jnp.where(is_odd, flow_down[0], flow_up[0])
     flow_odd = jnp.where(is_odd, flow_up[0], flow_down[0])
-    own = start[: 4 * rows].reshape(2, comps, rows, cols)
-    fields = [own[0], own[1], flow_even, flow_odd, masks]
     size = -(-2 * sum(DEEP) // 8) * 8
     rims = call(
         rims_kernel,
         (f32(size, cols), f32(size, cols)),
-        [SMEM] + [VMEM] * 7,
-        ids, *fields, even, odd,
+        [SMEM] + [VMEM] * 6,
+        ids, start, flow_even, flow_odd, masks, even, odd,
     )
     first, second = swap(tuple(rims), "strip", nstrips)
-    below = jnp.where(strip % 2 == 1, second, first)
-    above = jnp.where(strip % 2 == 1, first, second)
-    for x in (even, odd):
-        fields += list(x[: 4 * rows].reshape(2, comps, rows, cols))
-    wide, at = [], 0
-    for f, d in zip(fields, DEEP):
-        lower = below[at : at + 2 * d].reshape(2, d, cols)
-        upper = above[at : at + 2 * d].reshape(2, d, cols)
-        at += 2 * d
-        gap = jnp.zeros((2, 8 - 2 * d, cols), jnp.float32)
-        wide.append(jnp.concatenate([f, lower, gap, upper], axis=1))
-    u, v, fe, fo, mk, ue, ve, uo, vo = wide
-
-    p, ptails = call(
+    statics = (flow_even, flow_odd, masks)
+    side_by_side = pl.CostEstimate(flops=4_000_000, bytes_accessed=3_000_000, transcendentals=0)
+    packet = f32(2 * rows + 8, cols)
+    ends = (start, even, odd)
+    f, ftails, tails = call(
         lambda *refs: first_kernel(nstrips, *refs),
-        (f32(4 * rows + 8, cols), f32(32, cols)),
+        (packet, f32(16, cols), f32(16 * len(DEEP), cols)),
+        [SMEM] + [VMEM] * 8,
+        ids, *ends, *statics, first, second,
+    )
+    pe, po = swap(f, GZ, nz * nx)
+    h, htails, inner = call(
+        lambda *refs: beside_kernel(nstrips, *refs),
+        (packet, f32(16, cols), f32(comps, rows + 8, cols)),
         [SMEM] * 2 + [VMEM] * 9,
-        ids, marks, u, ue, uo, v, ve, vo, fe, fo, mk,
-    )
-    pe, po = swap(p, GZ, nz * nx)
+        ids, marks, *ends, f, ftails, *statics, tails,
+        cost_estimate=side_by_side,
+    )
+    he, ho = swap(h, GZ, nz * nx)
     g, gtails = call(
         lambda *refs: second_kernel(nstrips, *refs),
-        (f32(2 * rows + 8, cols), f32(16, cols)),
+        (packet, f32(16, cols)),
         [SMEM] * 2 + [VMEM] * 7,
-        ids, marks, p, ptails, pe, po, fe, fo, mk,
+        ids, marks, inner, pe, po, *statics, tails,
     )
     ge, go = swap(g, GZ, nz * nx)
-    part, w2, early = call(
+    known, w2, early = call(
         lambda *refs: third_kernel(nstrips, *refs),
         (f32(4 * comps, rows, cols), f32(4 * comps, rows, cols), f32(1, 128)),
-        [SMEM] * 3 + [VMEM] * 12,
-        ids, dts, marks, v, ve, vo, p, ptails, pe, po, g, gtails, fe, fo, mk,
-        cost_estimate=pl.CostEstimate(flops=6_000_000, bytes_accessed=4_000_000, transcendentals=0),
+        [SMEM] * 3 + [VMEM] * 17,
+        ids, dts, marks, *ends, f, ftails, pe, po, h, htails, he, ho, g, gtails, *statics, tails,
+        cost_estimate=side_by_side,
     )
     f2, sums = call(
         lambda *refs: fourth_kernel(nstrips, *refs),
         (f32(2 * comps, rows, cols), f32(1, 128)),
-        [SMEM] * 3 + [VMEM] * 8,
-        ids, dts, marks, part, w2, early, ge, go, fe, fo, mk,
+        [SMEM] * 3 + [VMEM] * 9,
+        ids, dts, marks, known, w2, early, ge, go, *statics, tails,
     )
     near = nx * nstrips
     sums = lax.all_to_all(jnp.broadcast_to(sums, (near, 1, 128)), ("x", "strip"), 0, 0)
@@ -426,7 +464,7 @@
         last_kernel,
         (core, core),
         [SMEM] * 2 + [VMEM] * 7,
-        dts, marks, sums, u, v, p, g, part, f2,
+        dts, marks, sums, start, f, h, g, known, f2,
     )
     return pos[None], vel[None]
 

time: 101 us -> 99.7 us (0.987)
  waiting for transfers between devices: 13.9 us -> 8.73 us
  starting transfers between devices: 29.4 us -> 34.1 us
  local copies, waits for them, and re-layouts: 4.3 us -> 1.24 us
  Pallas kernels: 8.19 us -> 10.4 us
  blocking collectives: 42 us -> 43.5 us
    ppermute x4 -> x5, waiting for transfers between devices: 13.6 us -> 5.19 us  [swap(): lax.ppermute(values[0], axes, first)]
    ppermute x4 -> x5, starting transfers between devices: 20.5 us -> 28.9 us  [swap(): lax.ppermute(values[0], axes, first)]
    ppermute x4 -> x5, starting transfers between devices: 8.92 us -> 5.22 us  [swap(): lax.ppermute(values[1], axes, second)]
    ppermute x4 -> x5, waiting for transfers between devices: 0.26 us -> 3.54 us  [swap(): lax.ppermute(values[1], axes, second)]
    unnamed x12, local copies, waits for them, and re-layouts: 3.4 us -> 0.97 us
    pallas_call x7 -> x8, Pallas kernels: 8.19 us -> 10.4 us  [call(): pl.pallas_call(kernel, out_shape=out_shape, in_specs=specs, out_specs=jax...]
    all_to_all x1, blocking collectives: 16 us -> 17.7 us  [local(): lax.all_to_all(jnp.broadcast_to(sums, (near, 1, 128)), ('x', 'strip'), 0, 0)]
  transfers between devices with their start and end apart: 8 -> 10, of which waited for: 5 -> 3; matrix products, arithmetic and copies ran while one was open for 1% -> 1% of each run, Pallas kernels for 2% -> 4%
where the time goes in v4:
time: 99.7 us; the launch traced here: 99.2 us
  blocking collectives  43.5 us (44%)
  starting transfers between devices  34.1 us (34%)
  Pallas kernels  10.4 us (10%)
  waiting for transfers between devices  8.73 us (9%)
  local copies, waits for them, and re-layouts  1.24 us (1%)
    ppermute x5, starting transfers between devices, swap(): lax.ppermute(values[0], axes, first)  28.9 us
    all_to_all x1, blocking collectives, local(): sums = lax.all_to_all(jnp.broadcast_to(sums, (nz, 1, 128)), 'z', 0, 0)  25.8 us
    all_to_all x1, blocking collectives, local(): lax.all_to_all(jnp.broadcast_to(sums, (near, 1, 128)), ('x', 'strip'), 0, 0)  17.7 us
    pallas_call x8, Pallas kernels, call(): pl.pallas_call(kernel, out_shape=out_shape, in_specs=specs, out_specs=jax...  10.4 us
    ppermute x5, starting transfers between devices, swap(): lax.ppermute(values[1], axes, second)  5.22 us
    ppermute x5, waiting for transfers between devices, swap(): lax.ppermute(values[0], axes, first)  5.19 us
    ppermute x5, waiting for transfers between devices, swap(): lax.ppermute(values[1], axes, second)  3.54 us
  transfers between devices with their start and end apart: 10, of which 3 were waited for; matrix products, arithmetic and copies ran while one was open for 1% of the time, Pallas kernels for 4%

profile of v4, /device:TPU:1, one launch (start us, length us, event | category | flops | bytes accessed | tf_op | source)
XLA Modules:
  0.0 99.2 jit_solution(16753460838772436202)
XLA Ops:
  0.6 2.5 %shard_map.86.start.refs_1_.refs_2_.refs_3_ = f32[136,640]{1,0:T(8,128)} custom-call(s32[3]{0:T(128)} %bitcast.23, f32[64,640]{1,0:T(8,128)} %bitcast.20, f32[64,640]{1,0:T(8,128)} %bitcast.21), custom_call_target="tpu_custom_call" | custom-call | tf_op jit(solution)/shard_map/pallas_call | solution.py:374
  3.2 0.7 collective-permute-start.1
  3.9 6.4 %collective-permute-start = (f32[136,640]{1,0:T(8,128)}, f32[136,640]{1,0:T(8,128)S(1)}, u32[]{:S(2)}, u32[]{:S(2)}) collective-permute-start(f32[136,640]{1,0:T(8,128)} %shard_map.86.start.refs_1_.refs_2_.refs_3_), channel_id=1, source_target_pairs={{0,8},{8,0},{16,24},{24,16},{32,40},{40,32},{48,56},{56,48},{64,72... | collective-permute-start | bytes 1044488 | tf_op jit(solution)/shard_map/ppermute | solution.py:20
  10.5 0.9 copy-done.2
  11.5 4.4 %collective-permute-done.even.refs_2_.refs_3_.refs_4_ = f32[136,640]{1,0:T(8,128)S(1)} collective-permute-done((f32[136,640]{1,0:T(8,128)}, f32[136,640]{1,0:T(8,128)S(1)}, u32[]{:S(2)}, u32[]{:S(2)}) %collective-permute-start) | collective-permute-done | bytes 348192 | tf_op jit(solution)/shard_map/ppermute | solution.py:20
  16.0 6.2 %collective-permute-start.2 = (f32[48,640]{1,0:T(8,128)S(1)}, f32[48,640]{1,0:T(8,128)S(1)}, u32[]{:S(2)}, u32[]{:S(2)}) collective-permute-start(f32[48,640]{1,0:T(8,128)S(1)} %get-tuple-element.19), channel_id=1, source_target_pairs={{0,1},{1,0},{2,3},{3,2},{4,5},{5,4},{6,7},{7,6},{8,9},{9,8},{10,11... | collective-permute-start | bytes 368648 | tf_op jit(solution)/shard_map/ppermute | solution.py:20
  22.2 2.5 %collective-permute-start.3 = (f32[48,640]{1,0:T(8,128)S(1)}, f32[48,640]{1,0:T(8,128)S(1)}, u32[]{:S(2)}, u32[]{:S(2)}) collective-permute-start(f32[48,640]{1,0:T(8,128)S(1)} %get-tuple-element.20), channel_id=1, source_target_pairs={{1,2},{2,1},{3,4},{4,3},{5,6},{6,5},{9,10},{10,9},{11,12},{12,11},... | collective-permute-start | bytes 368648 | tf_op jit(solution)/shard_map/ppermute | solution.py:20
  24.7 0.1 slice_reduce_fusion
  24.8 3.5 %collective-permute-done.3.refs_8_ = f32[48,640]{1,0:T(8,128)S(1)} collective-permute-done((f32[48,640]{1,0:T(8,128)S(1)}, f32[48,640]{1,0:T(8,128)S(1)}, u32[]{:S(2)}, u32[]{:S(2)}) %collective-permute-start.3) | collective-permute-done | bytes 122912 | tf_op jit(solution)/shard_map/ppermute | solution.py:20
  28.4 0.6 shard_map.88
  29.0 0.7 collective-permute-start.5
  29.7 5.0 %collective-permute-start.4 = (f32[72,640]{1,0:T(8,128)S(1)}, f32[72,640]{1,0:T(8,128)S(1)}, u32[]{:S(2)}, u32[]{:S(2)}) collective-permute-start(f32[72,640]{1,0:T(8,128)S(1)} %get-tuple-element.21.refs_5_.refs_6_.f), channel_id=1, source_target_pairs={{0,8},{8,0},{16,24},{24,16},{32,40},{40,32},{48,56},{56,48},{64,72... | collective-permute-start | bytes 552968 | tf_op jit(solution)/shard_map/ppermute | solution.py:20
  34.9 1.1 %shard_map.89 = (f32[72,640]{1,0:T(8,128)S(1)}, f32[16,640]{1,0:T(8,128)S(1)}, f32[2,40,640]{2,1,0:T(8,128)S(1)}) custom-call(s32[1]{0:T(128)} %bitcast.3.ids.refs_0_, f32[9]{0:T(128)S(1)} %pad_maximum_fusion.refs_1_.refs_2_.marks, f32[136,640]{1,0:T(8,128)S(1)} %copy-done, f32[136,640]{1,0:T(8,128)S(1)} %collective-permute-done.even.refs_2_.refs_3_.refs_4_, ...), custom_call_target="tpu_custom_call" | custom-call | flops 4000000 | bytes 3000000 | tf_op jit(solution)/shard_map/pallas_call | solution.py:374
  36.0 0.7 collective-permute-start.7
  36.7 6.6 %collective-permute-start.6 = (f32[72,640]{1,0:T(8,128)S(1)}, f32[72,640]{1,0:T(8,128)S(1)}, u32[]{:S(2)}, u32[]{:S(2)}) collective-permute-start(f32[72,640]{1,0:T(8,128)S(1)} %get-tuple-element.24.refs_10_.h), channel_id=1, source_target_pairs={{0,8},{8,0},{16,24},{24,16},{32,40},{40,32},{48,56},{56,48},{64,72... | collective-permute-start | bytes 552968 | tf_op jit(solution)/shard_map/ppermute | solution.py:20
  43.3 0.9 shard_map.90
  44.2 0.7 collective-permute-start.9
  44.9 4.7 %collective-permute-start.8 = (f32[72,640]{1,0:T(8,128)S(1)}, f32[72,640]{1,0:T(8,128)S(1)}, u32[]{:S(2)}, u32[]{:S(2)}) collective-permute-start(f32[72,640]{1,0:T(8,128)S(1)} %get-tuple-element.27.refs_14_.g), channel_id=1, source_target_pairs={{0,8},{8,0},{16,24},{24,16},{32,40},{40,32},{48,56},{56,48},{64,72... | collective-permute-start | bytes 552968 | tf_op jit(solution)/shard_map/ppermute | solution.py:20
  49.7 2.1 %shard_map.91 = (f32[8,32,640]{2,1,0:T(8,128)S(1)}, f32[8,32,640]{2,1,0:T(8,128)S(1)}, f32[1,128]{1,0:T(1,128)S(1)}) custom-call(s32[1]{0:T(128)} %bitcast.3.ids.refs_0_, f32[3]{0:T(128)S(1)} %power_multiply_fusion.refs_1_.dts, f32[9]{0:T(128)S(1)} %pad_maximum_fusion.refs_1_.refs_2_.marks, f32[136,640]{1,0:T(8,128)S(1)} %copy-done, ...), custom_call_target="tpu_custom_call" | custom-call | flops 4000000 | bytes 3000000 | tf_op jit(solution)/shard_map/pallas_call | solution.py:374
  51.7 0.8 collective-permute-done.8.refs_6_
  52.5 1.1 %shard_map.92 = (f32[4,32,640]{2,1,0:T(8,128)S(1)}, f32[1,128]{1,0:T(1,128)S(1)}) custom-call(s32[1]{0:T(128)} %bitcast.3.ids.refs_0_, f32[3]{0:T(128)S(1)} %power_multiply_fusion.refs_1_.dts, f32[9]{0:T(128)S(1)} %pad_maximum_fusion.refs_1_.refs_2_.marks, f32[8,32,640]{2,1,0:T(8,128)S(1)} %get-tuple-element.29.refs_3_.known, ...), custom_call_target="tpu_custom_call" | custom-call | tf_op jit(solution)/shard_map/pallas_call | solution.py:374
  53.7 17.7 %all_to_all.10 = f32[32,1,128]{2,1,0:T(1,128)S(1)} all-to-all(f32[32,1,128]{2,1,0:T(1,128)S(1)} %broadcast_in_dim.13), channel_id=1, replica_groups=mesh['z'=16,'x'=4,'strip'=8] {'x','strip'}, dimensions={0} | all-to-all | bytes 32768 | tf_op jit(solution)/shard_map/all_to_all | solution.py:460
  71.4 25.8 %all_to_all.11.parts = f32[16,1,128]{2,1,0:T(1,128)S(1)} all-to-all(f32[16,1,128]{2,1,0:T(1,128)S(1)} %broadcast_in_dim.14), channel_id=1, replica_groups=mesh['z'=16,'x'=4,'strip'=8] {'z'}, dimensions={0} | all-to-all | bytes 16384 | tf_op jit(solution)/shard_map/all_to_all | solution.py:462
  97.2 2.0 %shard_map.93 = (f32[2,32,640]{2,1,0:T(8,128)}, f32[2,32,640]{2,1,0:T(8,128)}) custom-call(f32[3]{0:T(128)S(1)} %power_multiply_fusion.refs_1_.dts, f32[9]{0:T(128)S(1)} %pad_maximum_fusion.refs_1_.refs_2_.marks, f32[16,1,128]{2,1,0:T(1,128)S(1)} %all_to_all.11.parts, f32[136,640]{1,0:T(8,128)S(1)} %copy-done, ...), custom_call_target="tpu_custom_call" | custom-call | tf_op jit(solution)/shard_map/pallas_call | solution.py:374
  (30 shorter events, 0.7 us)
Async XLA Ops:
  0.6 9.7 %copy-start.1 = (s32[2,1,32,640]{3,2,1,0:T(8,128)S(1)}, s32[2,1,32,640]{3,2,1,0:T(8,128)}, u32[]{:S(2)}) copy-start(s32[2,1,32,640]{3,2,1,0:T(8,128)} %param.11) | copy-start | bytes 491524
  3.2 8.3 %collective-permute-start.1 = (f32[136,640]{1,0:T(8,128)}, f32[136,640]{1,0:T(8,128)S(1)}, u32[]{:S(2)}, u32[]{:S(2)}) collective-permute-start(f32[136,640]{1,0:T(8,128)} %shard_map.86.start.refs_1_.refs_2_.refs_3_), channel_id=1, source_target_pairs={{8,16},{16,8},{24,32},{32,24},{40,48},{48,40},{56,64},{64,56},{72,... | collective-permute-start | bytes 1044488 | tf_op jit(solution)/shard_map/ppermute | solution.py:20
  3.9 12.0 %collective-permute-start = (f32[136,640]{1,0:T(8,128)}, f32[136,640]{1,0:T(8,128)S(1)}, u32[]{:S(2)}, u32[]{:S(2)}) collective-permute-start(f32[136,640]{1,0:T(8,128)} %shard_map.86.start.refs_1_.refs_2_.refs_3_), channel_id=1, source_target_pairs={{0,8},{8,0},{16,24},{24,16},{32,40},{40,32},{48,56},{56,48},{64,72... | collective-permute-start | bytes 1044488 | tf_op jit(solution)/shard_map/ppermute | solution.py:20
  10.4 0.9 copy-start.2
  10.5 1.0 copy-start.3
  10.5 5.4 %copy-start = (f32[136,640]{1,0:T(8,128)S(1)}, f32[136,640]{1,0:T(8,128)}, u32[]{:S(2)}) copy-start(f32[136,640]{1,0:T(8,128)} %shard_map.86.start.refs_1_.refs_2_.refs_3_) | copy-start | bytes 1044484
  16.0 8.7 %copy-start.4 = (s32[3,1]{0,1:T(1,128)S(1)}, s32[3,1]{0,1:T(1,128)}, u32[]{:S(2)}) copy-start(s32[3,1]{0,1:T(1,128)} %param.12) | copy-start | bytes 40
  16.0 8.9 %collective-permute-start.2 = (f32[48,640]{1,0:T(8,128)S(1)}, f32[48,640]{1,0:T(8,128)S(1)}, u32[]{:S(2)}, u32[]{:S(2)}) collective-permute-start(f32[48,640]{1,0:T(8,128)S(1)} %get-tuple-element.19), channel_id=1, source_target_pairs={{0,1},{1,0},{2,3},{3,2},{4,5},{5,4},{6,7},{7,6},{8,9},{9,8},{10,11... | collective-permute-start | bytes 368648 | tf_op jit(solution)/shard_map/ppermute | solution.py:20
  22.2 6.2 %collective-permute-start.3 = (f32[48,640]{1,0:T(8,128)S(1)}, f32[48,640]{1,0:T(8,128)S(1)}, u32[]{:S(2)}, u32[]{:S(2)}) collective-permute-start(f32[48,640]{1,0:T(8,128)S(1)} %get-tuple-element.20), channel_id=1, source_target_pairs={{1,2},{2,1},{3,4},{4,3},{5,6},{6,5},{9,10},{10,9},{11,12},{12,11},... | collective-permute-start | bytes 368648 | tf_op jit(solution)/shard_map/ppermute | solution.py:20
  29.0 14.3 %collective-permute-start.5 = (f32[72,640]{1,0:T(8,128)S(1)}, f32[72,640]{1,0:T(8,128)S(1)}, u32[]{:S(2)}, u32[]{:S(2)}) collective-permute-start(f32[72,640]{1,0:T(8,128)S(1)} %get-tuple-element.21.refs_5_.refs_6_.f), channel_id=1, source_target_pairs={{8,16},{16,8},{24,32},{32,24},{40,48},{48,40},{56,64},{64,56},{72,... | collective-permute-start | bytes 552968 | tf_op jit(solution)/shard_map/ppermute | solution.py:20
  29.7 13.7 %collective-permute-start.4 = (f32[72,640]{1,0:T(8,128)S(1)}, f32[72,640]{1,0:T(8,128)S(1)}, u32[]{:S(2)}, u32[]{:S(2)}) collective-permute-start(f32[72,640]{1,0:T(8,128)S(1)} %get-tuple-element.21.refs_5_.refs_6_.f), channel_id=1, source_target_pairs={{0,8},{8,0},{16,24},{24,16},{32,40},{40,32},{48,56},{56,48},{64,72... | collective-permute-start | bytes 552968 | tf_op jit(solution)/shard_map/ppermute | solution.py:20
  36.0 13.6 %collective-permute-start.7 = (f32[72,640]{1,0:T(8,128)S(1)}, f32[72,640]{1,0:T(8,128)S(1)}, u32[]{:S(2)}, u32[]{:S(2)}) collective-permute-start(f32[72,640]{1,0:T(8,128)S(1)} %get-tuple-element.24.refs_10_.h), channel_id=1, source_target_pairs={{8,16},{16,8},{24,32},{32,24},{40,48},{48,40},{56,64},{64,56},{72,... | collective-permute-start | bytes 552968 | tf_op jit(solution)/shard_map/ppermute | solution.py:20
  36.7 13.0 %collective-permute-start.6 = (f32[72,640]{1,0:T(8,128)S(1)}, f32[72,640]{1,0:T(8,128)S(1)}, u32[]{:S(2)}, u32[]{:S(2)}) collective-permute-start(f32[72,640]{1,0:T(8,128)S(1)} %get-tuple-element.24.refs_10_.h), channel_id=1, source_target_pairs={{0,8},{8,0},{16,24},{24,16},{32,40},{40,32},{48,56},{56,48},{64,72... | collective-permute-start | bytes 552968 | tf_op jit(solution)/shard_map/ppermute | solution.py:20
  44.2 5.4 %copy-start.5 = (s32[3]{0:T(128)S(1)}, s32[3]{0:T(128)}, u32[]{:S(2)}) copy-start(s32[3]{0:T(128)} %param.13) | copy-start | bytes 40
  44.2 7.5 %collective-permute-start.9 = (f32[72,640]{1,0:T(8,128)S(1)}, f32[72,640]{1,0:T(8,128)S(1)}, u32[]{:S(2)}, u32[]{:S(2)}) collective-permute-start(f32[72,640]{1,0:T(8,128)S(1)} %get-tuple-element.27.refs_14_.g), channel_id=1, source_target_pairs={{8,16},{16,8},{24,32},{32,24},{40,48},{48,40},{56,64},{64,56},{72,... | collective-permute-start | bytes 552968 | tf_op jit(solution)/shard_map/ppermute | solution.py:20
  44.9 7.6 %collective-permute-start.8 = (f32[72,640]{1,0:T(8,128)S(1)}, f32[72,640]{1,0:T(8,128)S(1)}, u32[]{:S(2)}, u32[]{:S(2)}) collective-permute-start(f32[72,640]{1,0:T(8,128)S(1)} %get-tuple-element.27.refs_14_.g), channel_id=1, source_target_pairs={{0,8},{8,0},{16,24},{24,16},{32,40},{40,32},{48,56},{56,48},{64,72... | collective-permute-start | bytes 552968 | tf_op jit(solution)/shard_map/ppermute | solution.py:20

commit v5 on v4

--- a/solution.py
+++ b/solution.py
@@ -111,18 +111,18 @@
     return weights
 
 
-def start_kernel(rs, pos, vel, out, sems):
+def start_kernel(resets, pos, vel, out, rs, sems):
     rows = pos.shape[0]
-    copies = [
-        pltpu.make_async_copy(src, out.at[pl.ds(at, rows)], sems.at[i])
-        for i, (src, at) in enumerate(((pos, 0), (vel, rows)))
-    ]
+    moves = ((resets, rs), (pos, out.at[pl.ds(0, rows)]), (vel, out.at[pl.ds(rows, rows)]))
+    copies = [pltpu.make_async_copy(src, dst, sems.at[i]) for i, (src, dst) in enumerate(moves)]
     for copy in copies:
         copy.start()
-    for i in range(8):
-        mark = jnp.where(rs[i] == 1, jnp.float32(1.0), jnp.float32(0.0)) if i < 3 else 0.0
+    out[2 * rows :] = jnp.zeros((8, out.shape[1]), jnp.float32)
+    copies[0].wait()
+    for i in range(3):
+        mark = jnp.where(rs[i] == 1, jnp.float32(1.0), jnp.float32(0.0))
         out[2 * rows + i : 2 * rows + i + 1] = jnp.full((1, out.shape[1]), mark, jnp.float32)
-    for copy in copies:
+    for copy in copies[1:]:
         copy.wait()
 
 
@@ -151,7 +151,7 @@
         fill(second, first)
 
 
-def first_kernel(nstrips, ids, start, even, odd, fe, fo, mk, first, second, packet, ftails, tails):
+def first_kernel(nstrips, ids, start, even, odd, fe, fo, mk, second, first, packet, ftails, tails):
     tails[...] = jnp.zeros(tails.shape, jnp.float32)
 
     def fill(below, above):
@@ -336,8 +336,9 @@
     return jnp.sqrt(kicked / (force + 1e-06))
 
 
-def last_kernel(dts, marks, parts, start, f, h, g, known, f2, pos, vel):
+def last_kernel(dts, marks, parts, start, f, h, g, known, f2, pos, vel, done, sems):
     rows = pos.shape[1]
+    copies = []
     sums = jnp.sum(parts[...], axis=0)
     lanes = [sums[:, i : i + 1] for i in range(N_EARLY + N_LATE)]
 
@@ -366,16 +367,21 @@
         field = field + dt1 * speed
         force = known[4 * c] + mu * f2[2 * c] + c1 * (known[4 * c + 2] + mu * f2[2 * c + 1])
         speed = k2 * (speed + dt2 * force) + (g2 * c2) * force
-        pos[c] = field + dt2 * speed
-        vel[c] = speed
-
-
-def call(kernel, out_shape, specs, *args, room=40 * 2**20, **more):
+        done[0, c] = field + dt2 * speed
+        done[1, c] = speed
+        for i, out in enumerate((pos, vel)):
+            copies.append(pltpu.make_async_copy(done.at[i, c], out.at[c], sems.at[i, c]))
+            copies[-1].start()
+    for copy in copies:
+        copy.wait()
+
+
+def call(kernel, out_shape, specs, *args, room=40 * 2**20, out_specs=None, **more):
     return pl.pallas_call(
         kernel,
         out_shape=out_shape,
         in_specs=specs,
-        out_specs=jax.tree.map(lambda _: VMEM, out_shape),
+        out_specs=out_specs or jax.tree.map(lambda _: VMEM, out_shape),
         compiler_params=pltpu.CompilerParams(vmem_limit_bytes=room),
         **more,
     )(*args)
@@ -394,10 +400,10 @@
     start = call(
         start_kernel,
         f32(4 * rows + 8, cols),
-        [SMEM] + [ANY] * 2,
+        [ANY] * 3,
         resets[:, 0], positions.reshape(-1, cols), velocity.reshape(-1, cols),
         room=None,
-        scratch_shapes=[pltpu.SemaphoreType.DMA((2,))],
+        scratch_shapes=[pltpu.SMEM((3,), jnp.int32), pltpu.SemaphoreType.DMA((3,))],
     )
     even, odd = swap(start, GZ, nz * nx)
     marks = jnp.concatenate([marks] + [x[4 * rows : 4 * rows + 3, 0] for x in (even, odd)])
@@ -425,7 +431,7 @@
         lambda *refs: first_kernel(nstrips, *refs),
         (packet, f32(16, cols), f32(16 * len(DEEP), cols)),
         [SMEM] + [VMEM] * 8,
-        ids, *ends, *statics, first, second,
+        ids, *ends, *statics, second, first,
     )
     pe, po = swap(f, GZ, nz * nx)
     h, htails, inner = call(
@@ -465,6 +471,8 @@
         (core, core),
         [SMEM] * 2 + [VMEM] * 7,
         dts, marks, sums, start, f, h, g, known, f2,
+        out_specs=(ANY, ANY),
+        scratch_shapes=[pltpu.VMEM((2, comps, rows, cols), jnp.float32), pltpu.SemaphoreType.DMA((2, comps))],
     )
     return pos[None], vel[None]
 

time: 99.7 us -> 96.9 us (0.972)
  waiting for transfers between devices: 8.73 us -> 6.98 us
    ppermute x5, starting transfers between devices: 5.22 us -> 9.48 us  [swap(): lax.ppermute(values[1], axes, second)]
    ppermute x5, starting transfers between devices: 28.9 us -> 25.2 us  [swap(): lax.ppermute(values[0], axes, first)]
    ppermute x5, waiting for transfers between devices: 3.54 us -> 0.49 us  [swap(): lax.ppermute(values[1], axes, second)]
    ppermute x5, waiting for transfers between devices: 5.19 us -> 6.48 us  [swap(): lax.ppermute(values[0], axes, first)]
  transfers between devices with their start and end apart: 10 -> 10, of which waited for: 3 -> 4; matrix products, arithmetic and copies ran while one was open for 1% -> 1% of each run, Pallas kernels for 4% -> 4%
where the time goes in v5:
time: 96.9 us; the launch traced here: 96.4 us
  blocking collectives  42.6 us (44%)
  starting transfers between devices  34.7 us (36%)
  Pallas kernels  9.66 us (10%)
  waiting for transfers between devices  6.98 us (7%)
  local copies, waits for them, and re-layouts  1.24 us (1%)
    all_to_all x1, blocking collectives, local(): sums = lax.all_to_all(jnp.broadcast_to(sums, (nz, 1, 128)), 'z', 0, 0)  25.8 us
    ppermute x5, starting transfers between devices, swap(): lax.ppermute(values[0], axes, first)  25.2 us
    all_to_all x1, blocking collectives, local(): lax.all_to_all(jnp.broadcast_to(sums, (near, 1, 128)), ('x', 'strip'), 0, 0)  16.8 us
    pallas_call x8, Pallas kernels, call(): pl.pallas_call(kernel, out_shape=out_shape, in_specs=specs, out_specs=out...  9.66 us
    ppermute x5, starting transfers between devices, swap(): lax.ppermute(values[1], axes, second)  9.48 us
    ppermute x5, waiting for transfers between devices, swap(): lax.ppermute(values[0], axes, first)  6.48 us
  transfers between devices with their start and end apart: 10, of which 4 were waited for; matrix products, arithmetic and copies ran while one was open for 1% of the time, Pallas kernels for 4%

profile of v5, /device:TPU:1, one launch (start us, length us, event | category | flops | bytes accessed | tf_op | source)
XLA Modules:
  0.0 96.4 jit_solution(8665328341855838928)
XLA Ops:
  0.6 1.8 %shard_map.86.start.refs_1_.refs_2_.refs_3_ = f32[136,640]{1,0:T(8,128)} custom-call(s32[3]{0:T(128)} %bitcast.23, f32[64,640]{1,0:T(8,128)} %bitcast.20, f32[64,640]{1,0:T(8,128)} %bitcast.21), custom_call_target="tpu_custom_call" | custom-call | tf_op jit(solution)/shard_map/pallas_call | solution.py:380
  2.4 0.7 collective-permute-start.1
  3.1 6.4 %collective-permute-start = (f32[136,640]{1,0:T(8,128)}, f32[136,640]{1,0:T(8,128)S(1)}, u32[]{:S(2)}, u32[]{:S(2)}) collective-permute-start(f32[136,640]{1,0:T(8,128)} %shard_map.86.start.refs_1_.refs_2_.refs_3_), channel_id=1, source_target_pairs={{0,8},{8,0},{16,24},{24,16},{32,40},{40,32},{48,56},{56,48},{64,72... | collective-permute-start | bytes 1044488 | tf_op jit(solution)/shard_map/ppermute | solution.py:20
  9.8 0.9 copy-done.2
  10.7 4.4 %collective-permute-done.even.refs_2_.refs_3_.refs_4_ = f32[136,640]{1,0:T(8,128)S(1)} collective-permute-done((f32[136,640]{1,0:T(8,128)}, f32[136,640]{1,0:T(8,128)S(1)}, u32[]{:S(2)}, u32[]{:S(2)}) %collective-permute-start) | collective-permute-done | bytes 348192 | tf_op jit(solution)/shard_map/ppermute | solution.py:20
  15.2 6.8 %collective-permute-start.2 = (f32[48,640]{1,0:T(8,128)S(1)}, f32[48,640]{1,0:T(8,128)S(1)}, u32[]{:S(2)}, u32[]{:S(2)}) collective-permute-start(f32[48,640]{1,0:T(8,128)S(1)} %get-tuple-element.19), channel_id=1, source_target_pairs={{1,2},{2,1},{3,4},{4,3},{5,6},{6,5},{9,10},{10,9},{11,12},{12,11},... | collective-permute-start | bytes 368648 | tf_op jit(solution)/shard_map/ppermute | solution.py:20
  22.0 1.9 %collective-permute-start.3 = (f32[48,640]{1,0:T(8,128)S(1)}, f32[48,640]{1,0:T(8,128)S(1)}, u32[]{:S(2)}, u32[]{:S(2)}) collective-permute-start(f32[48,640]{1,0:T(8,128)S(1)} %get-tuple-element.20), channel_id=1, source_target_pairs={{0,1},{1,0},{2,3},{3,2},{4,5},{5,4},{6,7},{7,6},{8,9},{9,8},{10,11... | collective-permute-start | bytes 368648 | tf_op jit(solution)/shard_map/ppermute | solution.py:20
  24.1 0.5 collective-permute-done.2.refs_7_
  24.6 0.7 collective-permute-done.3.refs_8_
  25.2 0.6 shard_map.88
  25.9 0.7 collective-permute-start.5
  26.5 5.6 %collective-permute-start.4 = (f32[72,640]{1,0:T(8,128)S(1)}, f32[72,640]{1,0:T(8,128)S(1)}, u32[]{:S(2)}, u32[]{:S(2)}) collective-permute-start(f32[72,640]{1,0:T(8,128)S(1)} %get-tuple-element.21.refs_5_.refs_6_.f), channel_id=1, source_target_pairs={{0,8},{8,0},{16,24},{24,16},{32,40},{40,32},{48,56},{56,48},{64,72... | collective-permute-start | bytes 552968 | tf_op jit(solution)/shard_map/ppermute | solution.py:20
  32.4 1.1 %shard_map.89 = (f32[72,640]{1,0:T(8,128)S(1)}, f32[16,640]{1,0:T(8,128)S(1)}, f32[2,40,640]{2,1,0:T(8,128)S(1)}) custom-call(s32[1]{0:T(128)} %bitcast.3.ids.refs_0_, f32[9]{0:T(128)S(1)} %pad_maximum_fusion.refs_1_.refs_2_.marks, f32[136,640]{1,0:T(8,128)S(1)} %copy-done, f32[136,640]{1,0:T(8,128)S(1)} %collective-permute-done.even.refs_2_.refs_3_.refs_4_, ...), custom_call_target="tpu_custom_call" | custom-call | flops 4000000 | bytes 3000000 | tf_op jit(solution)/shard_map/pallas_call | solution.py:380
  33.5 0.7 collective-permute-start.7
  34.2 6.6 %collective-permute-start.6 = (f32[72,640]{1,0:T(8,128)S(1)}, f32[72,640]{1,0:T(8,128)S(1)}, u32[]{:S(2)}, u32[]{:S(2)}) collective-permute-start(f32[72,640]{1,0:T(8,128)S(1)} %get-tuple-element.24.refs_10_.h), channel_id=1, source_target_pairs={{0,8},{8,0},{16,24},{24,16},{32,40},{40,32},{48,56},{56,48},{64,72... | collective-permute-start | bytes 552968 | tf_op jit(solution)/shard_map/ppermute | solution.py:20
  40.8 0.9 shard_map.90
  41.7 0.7 collective-permute-start.9
  42.4 4.7 %collective-permute-start.8 = (f32[72,640]{1,0:T(8,128)S(1)}, f32[72,640]{1,0:T(8,128)S(1)}, u32[]{:S(2)}, u32[]{:S(2)}) collective-permute-start(f32[72,640]{1,0:T(8,128)S(1)} %get-tuple-element.27.refs_14_.g), channel_id=1, source_target_pairs={{0,8},{8,0},{16,24},{24,16},{32,40},{40,32},{48,56},{56,48},{64,72... | collective-permute-start | bytes 552968 | tf_op jit(solution)/shard_map/ppermute | solution.py:20
  47.1 2.1 %shard_map.91 = (f32[8,32,640]{2,1,0:T(8,128)S(1)}, f32[8,32,640]{2,1,0:T(8,128)S(1)}, f32[1,128]{1,0:T(1,128)S(1)}) custom-call(s32[1]{0:T(128)} %bitcast.3.ids.refs_0_, f32[3]{0:T(128)S(1)} %power_multiply_fusion.refs_1_.dts, f32[9]{0:T(128)S(1)} %pad_maximum_fusion.refs_1_.refs_2_.marks, f32[136,640]{1,0:T(8,128)S(1)} %copy-done, ...), custom_call_target="tpu_custom_call" | custom-call | flops 4000000 | bytes 3000000 | tf_op jit(solution)/shard_map/pallas_call | solution.py:380
  49.2 1.4 %collective-permute-done.8.refs_6_ = f32[72,640]{1,0:T(8,128)S(1)} collective-permute-done((f32[72,640]{1,0:T(8,128)S(1)}, f32[72,640]{1,0:T(8,128)S(1)}, u32[]{:S(2)}, u32[]{:S(2)}) %collective-permute-start.8) | collective-permute-done | bytes 184352 | tf_op jit(solution)/shard_map/ppermute | solution.py:20
  50.6 1.1 %shard_map.92 = (f32[4,32,640]{2,1,0:T(8,128)S(1)}, f32[1,128]{1,0:T(1,128)S(1)}) custom-call(s32[1]{0:T(128)} %bitcast.3.ids.refs_0_, f32[3]{0:T(128)S(1)} %power_multiply_fusion.refs_1_.dts, f32[9]{0:T(128)S(1)} %pad_maximum_fusion.refs_1_.refs_2_.marks, f32[8,32,640]{2,1,0:T(8,128)S(1)} %get-tuple-element.29.refs_3_.known, ...), custom_call_target="tpu_custom_call" | custom-call | tf_op jit(solution)/shard_map/pallas_call | solution.py:380
  51.8 16.8 %all_to_all.10 = f32[32,1,128]{2,1,0:T(1,128)S(1)} all-to-all(f32[32,1,128]{2,1,0:T(1,128)S(1)} %broadcast_in_dim.13), channel_id=1, replica_groups=mesh['z'=16,'x'=4,'strip'=8] {'x','strip'}, dimensions={0} | all-to-all | bytes 32768 | tf_op jit(solution)/shard_map/all_to_all | solution.py:466
  68.6 25.8 %all_to_all.11.parts = f32[16,1,128]{2,1,0:T(1,128)S(1)} all-to-all(f32[16,1,128]{2,1,0:T(1,128)S(1)} %broadcast_in_dim.14), channel_id=1, replica_groups=mesh['z'=16,'x'=4,'strip'=8] {'z'}, dimensions={0} | all-to-all | bytes 16384 | tf_op jit(solution)/shard_map/all_to_all | solution.py:468
  94.4 2.0 %shard_map.93 = (f32[2,32,640]{2,1,0:T(8,128)}, f32[2,32,640]{2,1,0:T(8,128)}) custom-call(f32[3]{0:T(128)S(1)} %power_multiply_fusion.refs_1_.dts, f32[9]{0:T(128)S(1)} %pad_maximum_fusion.refs_1_.refs_2_.marks, f32[16,1,128]{2,1,0:T(1,128)S(1)} %all_to_all.11.parts, f32[136,640]{1,0:T(8,128)S(1)} %copy-done, ...), custom_call_target="tpu_custom_call" | custom-call | tf_op jit(solution)/shard_map/pallas_call | solution.py:380
  (30 shorter events, 0.8 us)
Async XLA Ops:
  0.6 9.0 %copy-start.1 = (s32[2,1,32,640]{3,2,1,0:T(8,128)S(1)}, s32[2,1,32,640]{3,2,1,0:T(8,128)}, u32[]{:S(2)}) copy-start(s32[2,1,32,640]{3,2,1,0:T(8,128)} %param.11) | copy-start | bytes 491524
  2.4 8.3 %collective-permute-start.1 = (f32[136,640]{1,0:T(8,128)}, f32[136,640]{1,0:T(8,128)S(1)}, u32[]{:S(2)}, u32[]{:S(2)}) collective-permute-start(f32[136,640]{1,0:T(8,128)} %shard_map.86.start.refs_1_.refs_2_.refs_3_), channel_id=1, source_target_pairs={{8,16},{16,8},{24,32},{32,24},{40,48},{48,40},{56,64},{64,56},{72,... | collective-permute-start | bytes 1044488 | tf_op jit(solution)/shard_map/ppermute | solution.py:20
  3.1 12.0 %collective-permute-start = (f32[136,640]{1,0:T(8,128)}, f32[136,640]{1,0:T(8,128)S(1)}, u32[]{:S(2)}, u32[]{:S(2)}) collective-permute-start(f32[136,640]{1,0:T(8,128)} %shard_map.86.start.refs_1_.refs_2_.refs_3_), channel_id=1, source_target_pairs={{0,8},{8,0},{16,24},{24,16},{32,40},{40,32},{48,56},{56,48},{64,72... | collective-permute-start | bytes 1044488 | tf_op jit(solution)/shard_map/ppermute | solution.py:20
  9.7 0.9 copy-start.2
  9.7 1.0 %copy-start.3 = (f32[1,2,32,640]{3,2,1,0:T(8,128)S(1)}, f32[1,2,32,640]{3,2,1,0:T(8,128)}, u32[]{:S(2)}) copy-start(f32[1,2,32,640]{3,2,1,0:T(8,128)} %param.9) | copy-start | bytes 491524
  9.7 5.4 %copy-start = (f32[136,640]{1,0:T(8,128)S(1)}, f32[136,640]{1,0:T(8,128)}, u32[]{:S(2)}) copy-start(f32[136,640]{1,0:T(8,128)} %shard_map.86.start.refs_1_.refs_2_.refs_3_) | copy-start | bytes 1044484
  15.2 8.7 %copy-start.4 = (s32[3,1]{0,1:T(1,128)S(1)}, s32[3,1]{0,1:T(1,128)}, u32[]{:S(2)}) copy-start(s32[3,1]{0,1:T(1,128)} %param.12) | copy-start | bytes 40
  15.2 9.3 %collective-permute-start.2 = (f32[48,640]{1,0:T(8,128)S(1)}, f32[48,640]{1,0:T(8,128)S(1)}, u32[]{:S(2)}, u32[]{:S(2)}) collective-permute-start(f32[48,640]{1,0:T(8,128)S(1)} %get-tuple-element.19), channel_id=1, source_target_pairs={{1,2},{2,1},{3,4},{4,3},{5,6},{6,5},{9,10},{10,9},{11,12},{12,11},... | collective-permute-start | bytes 368648 | tf_op jit(solution)/shard_map/ppermute | solution.py:20
  22.0 3.2 %collective-permute-start.3 = (f32[48,640]{1,0:T(8,128)S(1)}, f32[48,640]{1,0:T(8,128)S(1)}, u32[]{:S(2)}, u32[]{:S(2)}) collective-permute-start(f32[48,640]{1,0:T(8,128)S(1)} %get-tuple-element.20), channel_id=1, source_target_pairs={{0,1},{1,0},{2,3},{3,2},{4,5},{5,4},{6,7},{7,6},{8,9},{9,8},{10,11... | collective-permute-start | bytes 368648 | tf_op jit(solution)/shard_map/ppermute | solution.py:20
  25.9 14.9 %collective-permute-start.5 = (f32[72,640]{1,0:T(8,128)S(1)}, f32[72,640]{1,0:T(8,128)S(1)}, u32[]{:S(2)}, u32[]{:S(2)}) collective-permute-start(f32[72,640]{1,0:T(8,128)S(1)} %get-tuple-element.21.refs_5_.refs_6_.f), channel_id=1, source_target_pairs={{8,16},{16,8},{24,32},{32,24},{40,48},{48,40},{56,64},{64,56},{72,... | collective-permute-start | bytes 552968 | tf_op jit(solution)/shard_map/ppermute | solution.py:20
  26.5 14.3 %collective-permute-start.4 = (f32[72,640]{1,0:T(8,128)S(1)}, f32[72,640]{1,0:T(8,128)S(1)}, u32[]{:S(2)}, u32[]{:S(2)}) collective-permute-start(f32[72,640]{1,0:T(8,128)S(1)} %get-tuple-element.21.refs_5_.refs_6_.f), channel_id=1, source_target_pairs={{0,8},{8,0},{16,24},{24,16},{32,40},{40,32},{48,56},{56,48},{64,72... | collective-permute-start | bytes 552968 | tf_op jit(solution)/shard_map/ppermute | solution.py:20
  33.5 13.6 %collective-permute-start.7 = (f32[72,640]{1,0:T(8,128)S(1)}, f32[72,640]{1,0:T(8,128)S(1)}, u32[]{:S(2)}, u32[]{:S(2)}) collective-permute-start(f32[72,640]{1,0:T(8,128)S(1)} %get-tuple-element.24.refs_10_.h), channel_id=1, source_target_pairs={{8,16},{16,8},{24,32},{32,24},{40,48},{48,40},{56,64},{64,56},{72,... | collective-permute-start | bytes 552968 | tf_op jit(solution)/shard_map/ppermute | solution.py:20
  34.2 13.0 %collective-permute-start.6 = (f32[72,640]{1,0:T(8,128)S(1)}, f32[72,640]{1,0:T(8,128)S(1)}, u32[]{:S(2)}, u32[]{:S(2)}) collective-permute-start(f32[72,640]{1,0:T(8,128)S(1)} %get-tuple-element.24.refs_10_.h), channel_id=1, source_target_pairs={{0,8},{8,0},{16,24},{24,16},{32,40},{40,32},{48,56},{56,48},{64,72... | collective-permute-start | bytes 552968 | tf_op jit(solution)/shard_map/ppermute | solution.py:20
  41.7 5.4 %copy-start.5 = (s32[3]{0:T(128)S(1)}, s32[3]{0:T(128)}, u32[]{:S(2)}) copy-start(s32[3]{0:T(128)} %param.13) | copy-start | bytes 40
  41.7 7.5 %collective-permute-start.9 = (f32[72,640]{1,0:T(8,128)S(1)}, f32[72,640]{1,0:T(8,128)S(1)}, u32[]{:S(2)}, u32[]{:S(2)}) collective-permute-start(f32[72,640]{1,0:T(8,128)S(1)} %get-tuple-element.27.refs_14_.g), channel_id=1, source_target_pairs={{8,16},{16,8},{24,32},{32,24},{40,48},{48,40},{56,64},{64,56},{72,... | collective-permute-start | bytes 552968 | tf_op jit(solution)/shard_map/ppermute | solution.py:20
  42.4 8.2 %collective-permute-start.8 = (f32[72,640]{1,0:T(8,128)S(1)}, f32[72,640]{1,0:T(8,128)S(1)}, u32[]{:S(2)}, u32[]{:S(2)}) collective-permute-start(f32[72,640]{1,0:T(8,128)S(1)} %get-tuple-element.27.refs_14_.g), channel_id=1, source_target_pairs={{0,8},{8,0},{16,24},{24,16},{32,40},{40,32},{48,56},{56,48},{64,72... | collective-permute-start | bytes 552968 | tf_op jit(solution)/shard_map/ppermute | solution.py:20

commit v6 on v5

--- a/solution.py
+++ b/solution.py
@@ -188,15 +188,13 @@
     return [ring(part(x, rows, 2 + c), tails, i, c) for x, i in ((start, V), (even, VE), (odd, VO))]
 
 
-def beside_kernel(nstrips, ids, marks, start, even, odd, f, ftails, fe, fo, mk, tails, packet, htails, inner):
+def beside_kernel(nstrips, ids, marks, start, even, odd, f, ftails, fe, fo, mk, tails, hs, htails, inner):
     op = stencil_of(ids, nstrips, fe, fo, mk, tails)
     rows = fe.shape[1]
     rhos = [w[0] for w in weights_of(marks)]
-    packet[2 * rows :] = jnp.zeros((8, packet.shape[1]), jnp.float32)
     for c in range(2):
         h = op(*[rho * x for rho, x in zip(rhos, velocities(start, even, odd, tails, rows, c))])
-        packet[rows * c : rows * c + rows] = h[:rows]
-        packet[2 * rows + c : 2 * rows + c + 1] = h[rows : rows + 1]
+        hs[rows * c : rows * c + rows] = h[:rows]
         htails[8 * c : 8 * c + 8] = h[rows:]
         inner[c] = op.inner(rhos[0] * own_ring(f, ftails, rows, c))
 
@@ -205,22 +203,25 @@
     return ring(part(packet, rows, c), tails, 0, c)
 
 
-def side_ring(packet, rows, c, step):
-    tail = packet[2 * rows :]
-    tail = pltpu.roll(tail, 8 - step * c, 0) if c else tail
-    return jnp.concatenate([part(packet, rows, c), tail], axis=0)
-
-
-def second_kernel(nstrips, ids, marks, inner, pe, po, fe, fo, mk, tails, packet, gtails):
+def side_ring(packet, rows, at, step):
+    tail = packet[packet.shape[0] - 8 :]
+    tail = pltpu.roll(tail, 8 - step * at, 0) if at else tail
+    return jnp.concatenate([part(packet, rows, at), tail], axis=0)
+
+
+def second_kernel(nstrips, ids, marks, inner, pe, po, h, htails, fe, fo, mk, tails, packet, gtails):
     op = stencil_of(ids, nstrips, fe, fo, mk, tails)
     rows = mk.shape[1]
     _, rho_even, rho_odd = [w[0] for w in weights_of(marks)]
-    packet[2 * rows :] = jnp.zeros((8, packet.shape[1]), jnp.float32)
-    for c in range(2):
+    end = 4 * rows
+    packet[end:] = jnp.zeros((8, packet.shape[1]), jnp.float32)
+    packet[2 * rows : end] = h[...]
+    for c in range(2):
+        packet[end + 2 + c : end + 3 + c] = htails[8 * c : 8 * c + 1]
         even, odd = side_ring(pe, rows, c, 3), side_ring(po, rows, c, 3)
         g = inner[c] + (rho_even * op.even(even) + rho_odd * op.odd(odd))
         packet[rows * c : rows * c + rows] = g[:rows]
-        packet[2 * rows + c : 2 * rows + c + 1] = g[rows : rows + 1]
+        packet[end + c : end + c + 1] = g[rows : rows + 1]
         gtails[8 * c : 8 * c + 8] = g[rows:]
 
 
@@ -232,10 +233,8 @@
     return [(i, j) for i in range(size) for j in range(i, size)]
 
 
-EARLY = [(0, 0), (0, 2), (2, 2)]
-LATE = [pair for pair in all_pairs(4) if pair not in EARLY]
-N_EARLY = 2 + 3 + 3 + 2 * len(EARLY)
-N_LATE = 2 * len(LATE)
+N_EARLY = 2 + 3 + 3
+N_LATE = 2 * len(all_pairs(4))
 
 
 def tile_sum(value):
@@ -263,7 +262,7 @@
     return parts if totals is None else [x + y for x, y in zip(totals, parts)]
 
 
-def third_kernel(nstrips, ids, dts, marks, start, even, odd, f, ftails, pe, po, h, htails, he, ho, g, gtails, fe, fo, mk, tails, f2, w2, sums):
+def third_kernel(nstrips, ids, dts, marks, start, even, odd, f, ftails, pe, po, h, htails, g, gtails, fe, fo, mk, tails, f2, w2, sums):
     op = stencil_of(ids, nstrips, fe, fo, mk, tails)
     rows = mk.shape[1]
     dt0, dt1, dt2 = dts[0], dts[1], dts[2]
@@ -272,9 +271,8 @@
     totals = None
     for c in range(2):
         f0s = [own_ring(f, ftails, rows, c), side_ring(pe, rows, c, 3), side_ring(po, rows, c, 3)]
-        hs = [own_ring(h, htails, rows, c), side_ring(he, rows, c, 1), side_ring(ho, rows, c, 1)]
         vs = velocities(start, even, odd, tails, rows, c)
-        ts = [x + (dt0 * kappa) * y for x, y in zip(f0s, hs)]
+        ts = [f0s[0] + (dt0 * kappa) * own_ring(h, htails, rows, c), *f0s[1:]]
         g0 = dt0 * own_ring(g, gtails, rows, c)
         one = [k1 * ((rho * kappa) * v0 + dt1 * t) for v0, t, (rho, k1, _) in zip(vs, ts, weights)]
         mix = [g1 * t for t, (_, _, g1) in zip(ts, weights)]
@@ -296,7 +294,6 @@
         f0, v0, t, g0 = f0s[0][:rows], vs[0][:rows], ts[0][:rows], g0[:rows]
         terms = products([f0, v0 + dt0 * f0], [(0, 0), (1, 1)]) + products([t, g0], all_pairs(2))
         terms += products([(rho * kappa) * v0 + dt1 * t, rho * f0 + dt1 * g0], all_pairs(2))
-        terms += products(forces, EARLY) + products(kicked, EARLY)
         totals = gathered(totals, terms)
     sums[...] = lanes_of(totals, 0)
 
@@ -305,19 +302,21 @@
     op = stencil_of(ids, nstrips, fe, fo, mk, tails)
     rows = known.shape[1]
     dt0, dt1, dt2 = dts[0], dts[1], dts[2]
-    weights = weights_of(marks)
+    (_, k_even, g_even), (_, k_odd, g_odd) = weights_of(marks)[1:]
     totals = None
     for c in range(2):
-        even = op.even(side_ring(ge, rows, c, 1))[:rows]
-        odd = op.odd(side_ring(go, rows, c, 1))[:rows]
-        scale = dt1 * dt0
-        mu = scale * dt1 * (weights[1][1] * even + weights[2][1] * odd)
-        both = scale * (weights[1][2] * even + weights[2][2] * odd)
-        forces = [known[4 * c], known[4 * c + 1] + mu, known[4 * c + 2], known[4 * c + 3] + both]
-        kicked = [w2[4 * c], w2[4 * c + 1] + dt2 * mu, w2[4 * c + 2], w2[4 * c + 3] + dt2 * both]
-        f2[2 * c] = forces[1]
-        f2[2 * c + 1] = forces[3]
-        totals = gathered(totals, products(forces, LATE) + products(kicked, LATE))
+        keeps, mixes = [], []
+        for at, scale in ((2 + c, dt1 * dt0 * (1.0 - gamma())), (c, dt1 * dt0)):
+            even = op.even(side_ring(ge, rows, at, 1))[:rows]
+            odd = op.odd(side_ring(go, rows, at, 1))[:rows]
+            keeps.append((scale * dt1) * (k_even * even + k_odd * odd))
+            mixes.append(scale * (g_even * even + g_odd * odd))
+        more = keeps + mixes
+        forces = [known[4 * c + i] + x for i, x in enumerate(more)]
+        kicked = [w2[4 * c + i] + dt2 * x for i, x in enumerate(more)]
+        for i, force in enumerate(forces):
+            f2[4 * c + i] = force
+        totals = gathered(totals, products(forces, all_pairs(4)) + products(kicked, all_pairs(4)))
     sums[...] = early[...] + lanes_of(totals, N_EARLY)
 
 
@@ -336,7 +335,7 @@
     return jnp.sqrt(kicked / (force + 1e-06))
 
 
-def last_kernel(dts, marks, parts, start, f, h, g, known, f2, pos, vel, done, sems):
+def last_kernel(dts, marks, parts, start, f, g, f2, pos, vel, done, sems):
     rows = pos.shape[1]
     copies = []
     sums = jnp.sum(parts[...], axis=0)
@@ -352,9 +351,8 @@
     one = ((), (mu,))
     c1 = ratio(form(take(all_pairs(2), 5), one), form(take(all_pairs(2), 2), one))
     two = ((), (mu,), (c1,), (mu, c1))
-    force_sq = take(EARLY, 8) | take(LATE, N_EARLY)
-    kicked_sq = take(EARLY, 8 + len(EARLY)) | take(LATE, N_EARLY + len(LATE))
-    c2 = ratio(form(kicked_sq, two), form(force_sq, two))
+    pairs = all_pairs(4)
+    c2 = ratio(form(take(pairs, N_EARLY + len(pairs)), two), form(take(pairs, N_EARLY), two))
     rho, k1, g1 = weights_of(marks)[0]
     alpha = factors(marks[1], factors(marks[0], jnp.float32(0.1))[0])[0]
     _, k2, g2 = factors(marks[2], alpha)
@@ -362,10 +360,10 @@
         f0 = part(f, rows, c)
         speed = rho * (kappa * part(start, rows, 2 + c) + mu * f0)
         field = part(start, rows, c) + dt0 * speed
-        force = f0 + (dt0 * kappa) * part(h, rows, c) + (mu * dt0) * part(g, rows, c)
+        force = f0 + (dt0 * kappa) * part(g, rows, 2 + c) + (mu * dt0) * part(g, rows, c)
         speed = k1 * (speed + dt1 * force) + (g1 * c1) * force
         field = field + dt1 * speed
-        force = known[4 * c] + mu * f2[2 * c] + c1 * (known[4 * c + 2] + mu * f2[2 * c + 1])
+        force = f2[4 * c] + mu * f2[4 * c + 1] + c1 * (f2[4 * c + 2] + mu * f2[4 * c + 3])
         speed = k2 * (speed + dt2 * force) + (g2 * c2) * force
         done[0, c] = field + dt2 * speed
         done[1, c] = speed
@@ -436,29 +434,28 @@
     pe, po = swap(f, GZ, nz * nx)
     h, htails, inner = call(
         lambda *refs: beside_kernel(nstrips, *refs),
-        (packet, f32(16, cols), f32(comps, rows + 8, cols)),
+        (f32(2 * rows, cols), f32(16, cols), f32(comps, rows + 8, cols)),
         [SMEM] * 2 + [VMEM] * 9,
         ids, marks, *ends, f, ftails, *statics, tails,
         cost_estimate=side_by_side,
     )
-    he, ho = swap(h, GZ, nz * nx)
     g, gtails = call(
         lambda *refs: second_kernel(nstrips, *refs),
-        (packet, f32(16, cols)),
-        [SMEM] * 2 + [VMEM] * 7,
-        ids, marks, inner, pe, po, *statics, tails,
+        (f32(4 * rows + 8, cols), f32(16, cols)),
+        [SMEM] * 2 + [VMEM] * 9,
+        ids, marks, inner, pe, po, h, htails, *statics, tails,
     )
     ge, go = swap(g, GZ, nz * nx)
     known, w2, early = call(
         lambda *refs: third_kernel(nstrips, *refs),
         (f32(4 * comps, rows, cols), f32(4 * comps, rows, cols), f32(1, 128)),
-        [SMEM] * 3 + [VMEM] * 17,
-        ids, dts, marks, *ends, f, ftails, pe, po, h, htails, he, ho, g, gtails, *statics, tails,
+        [SMEM] * 3 + [VMEM] * 15,
+        ids, dts, marks, *ends, f, ftails, pe, po, h, htails, g, gtails, *statics, tails,
         cost_estimate=side_by_side,
     )
     f2, sums = call(
         lambda *refs: fourth_kernel(nstrips, *refs),
-        (f32(2 * comps, rows, cols), f32(1, 128)),
+        (f32(4 * comps, rows, cols), f32(1, 128)),
         [SMEM] * 3 + [VMEM] * 9,
         ids, dts, marks, known, w2, early, ge, go, *statics, tails,
     )
@@ -469,8 +466,8 @@
     pos, vel = call(
         last_kernel,
         (core, core),
-        [SMEM] * 2 + [VMEM] * 7,
-        dts, marks, sums, start, f, h, g, known, f2,
+        [SMEM] * 2 + [VMEM] * 5,
+        dts, marks, sums, start, f, g, f2,
         out_specs=(ANY, ANY),
         scratch_shapes=[pltpu.VMEM((2, comps, rows, cols), jnp.float32), pltpu.SemaphoreType.DMA((2, comps))],
     )

time: 96.9 us -> 98.2 us (1.013)
  waiting for transfers between devices: 6.98 us -> 14.1 us
  starting transfers between devices: 34.7 us -> 29.3 us
    ppermute x5 -> x4, waiting for transfers between devices: 6.48 us -> 13.6 us  [swap(): lax.ppermute(values[0], axes, first)]
    ppermute x5 -> x4, starting transfers between devices: 25.2 us -> 20.5 us  [swap(): lax.ppermute(values[0], axes, first)]
    ppermute x5 -> x4, starting transfers between devices: 9.48 us -> 8.81 us  [swap(): lax.ppermute(values[1], axes, second)]
  transfers between devices with their start and end apart: 10 -> 8, of which waited for: 4 -> 5; matrix products, arithmetic and copies ran while one was open for 1% -> 1% of each run, Pallas kernels for 4% -> 3%
where the time goes in v6:
time: 98.2 us; the launch traced here: 97.8 us
  blocking collectives  42 us (43%)
  starting transfers between devices  29.3 us (30%)
  waiting for transfers between devices  14.1 us (14%)
  Pallas kernels  9.96 us (10%)
  local copies, waits for them, and re-layouts  1.23 us (1%)
    all_to_all x1, blocking collectives, local(): sums = lax.all_to_all(jnp.broadcast_to(sums, (nz, 1, 128)), 'z', 0, 0)  26.1 us
    ppermute x4, starting transfers between devices, swap(): lax.ppermute(values[0], axes, first)  20.5 us
    all_to_all x1, blocking collectives, local(): lax.all_to_all(jnp.broadcast_to(sums, (near, 1, 128)), ('x', 'strip'), 0, 0)  15.9 us
    ppermute x4, waiting for transfers between devices, swap(): lax.ppermute(values[0], axes, first)  13.6 us
    pallas_call x8, Pallas kernels, call(): pl.pallas_call(kernel, out_shape=out_shape, in_specs=specs, out_specs=out...  9.96 us
    ppermute x4, starting transfers between devices, swap(): lax.ppermute(values[1], axes, second)  8.81 us
  transfers between devices with their start and end apart: 8, of which 5 were waited for; matrix products, arithmetic and copies ran while one was open for 1% of the time, Pallas kernels for 3%

profile of v6, /device:TPU:1, one launch (start us, length us, event | category | flops | bytes accessed | tf_op | source)
XLA Modules:
  0.0 97.8 jit_solution(4867358139379721966)
XLA Ops:
  0.6 1.8 %shard_map.86.start.refs_1_.refs_2_.refs_3_ = f32[136,640]{1,0:T(8,128)} custom-call(s32[3]{0:T(128)} %bitcast.23, f32[64,640]{1,0:T(8,128)} %bitcast.20, f32[64,640]{1,0:T(8,128)} %bitcast.21), custom_call_target="tpu_custom_call" | custom-call | tf_op jit(solution)/shard_map/pallas_call | solution.py:378
  2.4 0.7 collective-permute-start.1
  3.1 6.4 %collective-permute-start = (f32[136,640]{1,0:T(8,128)}, f32[136,640]{1,0:T(8,128)S(1)}, u32[]{:S(2)}, u32[]{:S(2)}) collective-permute-start(f32[136,640]{1,0:T(8,128)} %shard_map.86.start.refs_1_.refs_2_.refs_3_), channel_id=1, source_target_pairs={{0,8},{8,0},{16,24},{24,16},{32,40},{40,32},{48,56},{56,48},{64,72... | collective-permute-start | bytes 1044488 | tf_op jit(solution)/shard_map/ppermute | solution.py:20
  9.8 0.9 copy-done.2
  10.7 4.4 %collective-permute-done.even.refs_2_.refs_3_.refs_4_ = f32[136,640]{1,0:T(8,128)S(1)} collective-permute-done((f32[136,640]{1,0:T(8,128)}, f32[136,640]{1,0:T(8,128)S(1)}, u32[]{:S(2)}, u32[]{:S(2)}) %collective-permute-start) | collective-permute-done | bytes 348192 | tf_op jit(solution)/shard_map/ppermute | solution.py:20
  15.2 6.8 %collective-permute-start.2 = (f32[48,640]{1,0:T(8,128)S(1)}, f32[48,640]{1,0:T(8,128)S(1)}, u32[]{:S(2)}, u32[]{:S(2)}) collective-permute-start(f32[48,640]{1,0:T(8,128)S(1)} %get-tuple-element.19), channel_id=1, source_target_pairs={{1,2},{2,1},{3,4},{4,3},{5,6},{6,5},{9,10},{10,9},{11,12},{12,11},... | collective-permute-start | bytes 368648 | tf_op jit(solution)/shard_map/ppermute | solution.py:20
  22.0 1.9 %collective-permute-start.3 = (f32[48,640]{1,0:T(8,128)S(1)}, f32[48,640]{1,0:T(8,128)S(1)}, u32[]{:S(2)}, u32[]{:S(2)}) collective-permute-start(f32[48,640]{1,0:T(8,128)S(1)} %get-tuple-element.20), channel_id=1, source_target_pairs={{0,1},{1,0},{2,3},{3,2},{4,5},{5,4},{6,7},{7,6},{8,9},{9,8},{10,11... | collective-permute-start | bytes 368648 | tf_op jit(solution)/shard_map/ppermute | solution.py:20
  24.0 0.1 slice_reduce_fusion
  24.1 0.5 collective-permute-done.2.refs_7_
  24.6 0.7 collective-permute-done.3.refs_8_
  25.2 0.6 shard_map.88
  25.9 0.7 collective-permute-start.5
  26.5 5.6 %collective-permute-start.4 = (f32[72,640]{1,0:T(8,128)S(1)}, f32[72,640]{1,0:T(8,128)S(1)}, u32[]{:S(2)}, u32[]{:S(2)}) collective-permute-start(f32[72,640]{1,0:T(8,128)S(1)} %get-tuple-element.21.refs_5_.refs_6_.f), channel_id=1, source_target_pairs={{0,8},{8,0},{16,24},{24,16},{32,40},{40,32},{48,56},{56,48},{64,72... | collective-permute-start | bytes 552968 | tf_op jit(solution)/shard_map/ppermute | solution.py:20
  32.4 1.1 %shard_map.89 = (f32[64,640]{1,0:T(8,128)S(1)}, f32[16,640]{1,0:T(8,128)S(1)}, f32[2,40,640]{2,1,0:T(8,128)S(1)}) custom-call(s32[1]{0:T(128)} %bitcast.3.ids.refs_0_, f32[9]{0:T(128)S(1)} %pad_maximum_fusion.refs_1_.refs_2_.marks, f32[136,640]{1,0:T(8,128)S(1)} %copy-done, f32[136,640]{1,0:T(8,128)S(1)} %collective-permute-done.even.refs_2_.refs_3_.refs_4_, ...), custom_call_target="tpu_custom_call" | custom-call | flops 4000000 | bytes 3000000 | tf_op jit(solution)/shard_map/pallas_call | solution.py:378
  33.5 3.3 %collective-permute-done.4.refs_3_.refs_8_ = f32[72,640]{1,0:T(8,128)S(1)} collective-permute-done((f32[72,640]{1,0:T(8,128)S(1)}, f32[72,640]{1,0:T(8,128)S(1)}, u32[]{:S(2)}, u32[]{:S(2)}) %collective-permute-start.4) | collective-permute-done | bytes 184352 | tf_op jit(solution)/shard_map/ppermute | solution.py:20
  36.8 0.9 shard_map.90
  37.7 0.7 collective-permute-start.7
  38.4 6.6 %collective-permute-start.6 = (f32[136,640]{1,0:T(8,128)S(1)}, f32[136,640]{1,0:T(8,128)S(1)}, u32[]{:S(2)}, u32[]{:S(2)}) collective-permute-start(f32[136,640]{1,0:T(8,128)S(1)} %get-tuple-element.27.refs_12_.g), channel_id=1, source_target_pairs={{0,8},{8,0},{16,24},{24,16},{32,40},{40,32},{48,56},{56,48},{64,72... | collective-permute-start | bytes 1044488 | tf_op jit(solution)/shard_map/ppermute | solution.py:20
  45.0 2.0 %shard_map.91 = (f32[8,32,640]{2,1,0:T(8,128)S(1)}, f32[8,32,640]{2,1,0:T(8,128)S(1)}, f32[1,128]{1,0:T(1,128)S(1)}) custom-call(s32[1]{0:T(128)} %bitcast.3.ids.refs_0_, f32[3]{0:T(128)S(1)} %power_multiply_fusion.refs_1_.dts, f32[9]{0:T(128)S(1)} %pad_maximum_fusion.refs_1_.refs_2_.marks, f32[136,640]{1,0:T(8,128)S(1)} %copy-done, ...), custom_call_target="tpu_custom_call" | custom-call | flops 4000000 | bytes 3000000 | tf_op jit(solution)/shard_map/pallas_call | solution.py:378
  47.0 5.2 %collective-permute-done.6.refs_6_ = f32[136,640]{1,0:T(8,128)S(1)} collective-permute-done((f32[136,640]{1,0:T(8,128)S(1)}, f32[136,640]{1,0:T(8,128)S(1)}, u32[]{:S(2)}, u32[]{:S(2)}) %collective-permute-start.6) | collective-permute-done | bytes 348192 | tf_op jit(solution)/shard_map/ppermute | solution.py:20
  52.2 1.5 %shard_map.92 = (f32[8,32,640]{2,1,0:T(8,128)S(1)}, f32[1,128]{1,0:T(1,128)S(1)}) custom-call(s32[1]{0:T(128)} %bitcast.3.ids.refs_0_, f32[3]{0:T(128)S(1)} %power_multiply_fusion.refs_1_.dts, f32[9]{0:T(128)S(1)} %pad_maximum_fusion.refs_1_.refs_2_.marks, f32[8,32,640]{2,1,0:T(8,128)S(1)} %get-tuple-element.29.refs_3_, ...), custom_call_target="tpu_custom_call" | custom-call | tf_op jit(solution)/shard_map/pallas_call | solution.py:378
  53.7 15.9 %all_to_all.10 = f32[32,1,128]{2,1,0:T(1,128)S(1)} all-to-all(f32[32,1,128]{2,1,0:T(1,128)S(1)} %broadcast_in_dim.13), channel_id=1, replica_groups=mesh['z'=16,'x'=4,'strip'=8] {'x','strip'}, dimensions={0} | all-to-all | bytes 32768 | tf_op jit(solution)/shard_map/all_to_all | solution.py:463
  69.7 26.1 %all_to_all.11.parts = f32[16,1,128]{2,1,0:T(1,128)S(1)} all-to-all(f32[16,1,128]{2,1,0:T(1,128)S(1)} %broadcast_in_dim.14), channel_id=1, replica_groups=mesh['z'=16,'x'=4,'strip'=8] {'z'}, dimensions={0} | all-to-all | bytes 16384 | tf_op jit(solution)/shard_map/all_to_all | solution.py:465
  95.8 2.0 %shard_map.93 = (f32[2,32,640]{2,1,0:T(8,128)}, f32[2,32,640]{2,1,0:T(8,128)}) custom-call(f32[3]{0:T(128)S(1)} %power_multiply_fusion.refs_1_.dts, f32[9]{0:T(128)S(1)} %pad_maximum_fusion.refs_1_.refs_2_.marks, f32[16,1,128]{2,1,0:T(1,128)S(1)} %all_to_all.11.parts, f32[136,640]{1,0:T(8,128)S(1)} %copy-done, ...), custom_call_target="tpu_custom_call" | custom-call | tf_op jit(solution)/shard_map/pallas_call | solution.py:378
  (26 shorter events, 0.7 us)
Async XLA Ops:
  0.6 9.0 %copy-start.1 = (s32[2,1,32,640]{3,2,1,0:T(8,128)S(1)}, s32[2,1,32,640]{3,2,1,0:T(8,128)}, u32[]{:S(2)}) copy-start(s32[2,1,32,640]{3,2,1,0:T(8,128)} %param.11) | copy-start | bytes 491524
  2.4 8.3 %collective-permute-start.1 = (f32[136,640]{1,0:T(8,128)}, f32[136,640]{1,0:T(8,128)S(1)}, u32[]{:S(2)}, u32[]{:S(2)}) collective-permute-start(f32[136,640]{1,0:T(8,128)} %shard_map.86.start.refs_1_.refs_2_.refs_3_), channel_id=1, source_target_pairs={{8,16},{16,8},{24,32},{32,24},{40,48},{48,40},{56,64},{64,56},{72,... | collective-permute-start | bytes 1044488 | tf_op jit(solution)/shard_map/ppermute | solution.py:20
  3.1 12.0 %collective-permute-start = (f32[136,640]{1,0:T(8,128)}, f32[136,640]{1,0:T(8,128)S(1)}, u32[]{:S(2)}, u32[]{:S(2)}) collective-permute-start(f32[136,640]{1,0:T(8,128)} %shard_map.86.start.refs_1_.refs_2_.refs_3_), channel_id=1, source_target_pairs={{0,8},{8,0},{16,24},{24,16},{32,40},{40,32},{48,56},{56,48},{64,72... | collective-permute-start | bytes 1044488 | tf_op jit(solution)/shard_map/ppermute | solution.py:20
  9.7 0.9 copy-start.2
  9.7 1.0 %copy-start.3 = (f32[1,2,32,640]{3,2,1,0:T(8,128)S(1)}, f32[1,2,32,640]{3,2,1,0:T(8,128)}, u32[]{:S(2)}) copy-start(f32[1,2,32,640]{3,2,1,0:T(8,128)} %param.9) | copy-start | bytes 491524
  9.8 5.4 %copy-start = (f32[136,640]{1,0:T(8,128)S(1)}, f32[136,640]{1,0:T(8,128)}, u32[]{:S(2)}) copy-start(f32[136,640]{1,0:T(8,128)} %shard_map.86.start.refs_1_.refs_2_.refs_3_) | copy-start | bytes 1044484
  15.2 8.7 %copy-start.4 = (s32[3,1]{0,1:T(1,128)S(1)}, s32[3,1]{0,1:T(1,128)}, u32[]{:S(2)}) copy-start(s32[3,1]{0,1:T(1,128)} %param.12) | copy-start | bytes 40
  15.2 9.3 %collective-permute-start.2 = (f32[48,640]{1,0:T(8,128)S(1)}, f32[48,640]{1,0:T(8,128)S(1)}, u32[]{:S(2)}, u32[]{:S(2)}) collective-permute-start(f32[48,640]{1,0:T(8,128)S(1)} %get-tuple-element.19), channel_id=1, source_target_pairs={{1,2},{2,1},{3,4},{4,3},{5,6},{6,5},{9,10},{10,9},{11,12},{12,11},... | collective-permute-start | bytes 368648 | tf_op jit(solution)/shard_map/ppermute | solution.py:20
  22.0 3.2 %collective-permute-start.3 = (f32[48,640]{1,0:T(8,128)S(1)}, f32[48,640]{1,0:T(8,128)S(1)}, u32[]{:S(2)}, u32[]{:S(2)}) collective-permute-start(f32[48,640]{1,0:T(8,128)S(1)} %get-tuple-element.20), channel_id=1, source_target_pairs={{0,1},{1,0},{2,3},{3,2},{4,5},{5,4},{6,7},{7,6},{8,9},{9,8},{10,11... | collective-permute-start | bytes 368648 | tf_op jit(solution)/shard_map/ppermute | solution.py:20
  25.9 7.6 %collective-permute-start.5 = (f32[72,640]{1,0:T(8,128)S(1)}, f32[72,640]{1,0:T(8,128)S(1)}, u32[]{:S(2)}, u32[]{:S(2)}) collective-permute-start(f32[72,640]{1,0:T(8,128)S(1)} %get-tuple-element.21.refs_5_.refs_6_.f), channel_id=1, source_target_pairs={{8,16},{16,8},{24,32},{32,24},{40,48},{48,40},{56,64},{64,56},{72,... | collective-permute-start | bytes 552968 | tf_op jit(solution)/shard_map/ppermute | solution.py:20
  26.5 10.2 %collective-permute-start.4 = (f32[72,640]{1,0:T(8,128)S(1)}, f32[72,640]{1,0:T(8,128)S(1)}, u32[]{:S(2)}, u32[]{:S(2)}) collective-permute-start(f32[72,640]{1,0:T(8,128)S(1)} %get-tuple-element.21.refs_5_.refs_6_.f), channel_id=1, source_target_pairs={{0,8},{8,0},{16,24},{24,16},{32,40},{40,32},{48,56},{56,48},{64,72... | collective-permute-start | bytes 552968 | tf_op jit(solution)/shard_map/ppermute | solution.py:20
  37.7 7.3 %copy-start.5 = (s32[3]{0:T(128)S(1)}, s32[3]{0:T(128)}, u32[]{:S(2)}) copy-start(s32[3]{0:T(128)} %param.13) | copy-start | bytes 40
  37.7 9.3 %collective-permute-start.7 = (f32[136,640]{1,0:T(8,128)S(1)}, f32[136,640]{1,0:T(8,128)S(1)}, u32[]{:S(2)}, u32[]{:S(2)}) collective-permute-start(f32[136,640]{1,0:T(8,128)S(1)} %get-tuple-element.27.refs_12_.g), channel_id=1, source_target_pairs={{8,16},{16,8},{24,32},{32,24},{40,48},{48,40},{56,64},{64,56},{72,... | collective-permute-start | bytes 1044488 | tf_op jit(solution)/shard_map/ppermute | solution.py:20
  38.4 13.8 %collective-permute-start.6 = (f32[136,640]{1,0:T(8,128)S(1)}, f32[136,640]{1,0:T(8,128)S(1)}, u32[]{:S(2)}, u32[]{:S(2)}) collective-permute-start(f32[136,640]{1,0:T(8,128)S(1)} %get-tuple-element.27.refs_12_.g), channel_id=1, source_target_pairs={{0,8},{8,0},{16,24},{24,16},{32,40},{40,32},{48,56},{56,48},{64,72... | collective-permute-start | bytes 1044488 | tf_op jit(solution)/shard_map/ppermute | solution.py:20

commit v7 on v5

--- a/solution.py
+++ b/solution.py
@@ -111,26 +111,26 @@
     return weights
 
 
-def start_kernel(resets, pos, vel, out, rs, sems):
-    rows = pos.shape[0]
-    moves = ((resets, rs), (pos, out.at[pl.ds(0, rows)]), (vel, out.at[pl.ds(rows, rows)]))
+def start_kernel(resets, vel, out, rs, sems):
+    rows = vel.shape[0]
+    moves = ((resets, rs), (vel, out.at[pl.ds(0, rows)]))
     copies = [pltpu.make_async_copy(src, dst, sems.at[i]) for i, (src, dst) in enumerate(moves)]
     for copy in copies:
         copy.start()
-    out[2 * rows :] = jnp.zeros((8, out.shape[1]), jnp.float32)
+    out[rows:] = jnp.zeros((8, out.shape[1]), jnp.float32)
     copies[0].wait()
     for i in range(3):
         mark = jnp.where(rs[i] == 1, jnp.float32(1.0), jnp.float32(0.0))
-        out[2 * rows + i : 2 * rows + i + 1] = jnp.full((1, out.shape[1]), mark, jnp.float32)
+        out[rows + i : rows + i + 1] = jnp.full((1, out.shape[1]), mark, jnp.float32)
     for copy in copies[1:]:
         copy.wait()
 
 
-def rims_kernel(ids, start, fe, fo, mk, even, odd, first, second):
+def rims_kernel(ids, u, v, fe, fo, mk, ue, ve, uo, vo, first, second):
     rows = fe.shape[1]
-    comps = [(start, rows * at) for at in range(4)]
+    comps = [(x, rows * c) for x in (u, v) for c in range(2)]
     comps += [(x.at[c], 0) for x in (fe, fo, mk) for c in range(2)]
-    comps += [(x, rows * at) for x in (even, odd) for at in range(4)]
+    comps += [(x, rows * c) for x in (ue, ve, uo, vo) for c in range(2)]
 
     def fill(upper, lower):
         at = 0
@@ -185,7 +185,7 @@
 
 
 def velocities(start, even, odd, tails, rows, c):
-    return [ring(part(x, rows, 2 + c), tails, i, c) for x, i in ((start, V), (even, VE), (odd, VO))]
+    return [ring(part(x, rows, c), tails, i, c) for x, i in ((start, V), (even, VE), (odd, VO))]
 
 
 def beside_kernel(nstrips, ids, marks, start, even, odd, f, ftails, fe, fo, mk, tails, packet, htails, inner):
@@ -336,7 +336,7 @@
     return jnp.sqrt(kicked / (force + 1e-06))
 
 
-def last_kernel(dts, marks, parts, start, f, h, g, known, f2, pos, vel, done, sems):
+def last_kernel(dts, marks, parts, u, v, f, h, g, known, f2, pos, vel, done, sems):
     rows = pos.shape[1]
     copies = []
     sums = jnp.sum(parts[...], axis=0)
@@ -360,8 +360,8 @@
     _, k2, g2 = factors(marks[2], alpha)
     for c in range(2):
         f0 = part(f, rows, c)
-        speed = rho * (kappa * part(start, rows, 2 + c) + mu * f0)
-        field = part(start, rows, c) + dt0 * speed
+        speed = rho * (kappa * part(v, rows, c) + mu * f0)
+        field = part(u, rows, c) + dt0 * speed
         force = f0 + (dt0 * kappa) * part(h, rows, c) + (mu * dt0) * part(g, rows, c)
         speed = k1 * (speed + dt1 * force) + (g1 * c1) * force
         field = field + dt1 * speed
@@ -397,16 +397,18 @@
     _, comps, rows, cols = positions.shape
     core = f32(comps, rows, cols)
     marks = (resets[:, 0] == 1).astype(jnp.float32)
-    start = call(
+    u = positions.reshape(-1, cols)
+    ue, uo = swap(u, GZ, nz * nx)
+    v = call(
         start_kernel,
-        f32(4 * rows + 8, cols),
-        [ANY] * 3,
-        resets[:, 0], positions.reshape(-1, cols), velocity.reshape(-1, cols),
+        f32(2 * rows + 8, cols),
+        [ANY] * 2,
+        resets[:, 0], velocity.reshape(-1, cols),
         room=None,
-        scratch_shapes=[pltpu.SMEM((3,), jnp.int32), pltpu.SemaphoreType.DMA((3,))],
-    )
-    even, odd = swap(start, GZ, nz * nx)
-    marks = jnp.concatenate([marks] + [x[4 * rows : 4 * rows + 3, 0] for x in (even, odd)])
+        scratch_shapes=[pltpu.SMEM((3,), jnp.int32), pltpu.SemaphoreType.DMA((2,))],
+    )
+    ve, vo = swap(v, GZ, nz * nx)
+    marks = jnp.concatenate([marks] + [x[2 * rows : 2 * rows + 3, 0] for x in (ve, vo)])
     dts = 0.1 * jnp.power(jnp.float32(1.25), dt_index.astype(jnp.float32))
     ids = jnp.reshape(strip, (1,))
     is_odd = section % 2 == 1
@@ -419,26 +421,26 @@
     rims = call(
         rims_kernel,
         (f32(size, cols), f32(size, cols)),
-        [SMEM] + [VMEM] * 6,
-        ids, start, flow_even, flow_odd, masks, even, odd,
+        [SMEM] + [VMEM] * 9,
+        ids, u, v, flow_even, flow_odd, masks, ue, ve, uo, vo,
     )
     first, second = swap(tuple(rims), "strip", nstrips)
     statics = (flow_even, flow_odd, masks)
     side_by_side = pl.CostEstimate(flops=4_000_000, bytes_accessed=3_000_000, transcendentals=0)
     packet = f32(2 * rows + 8, cols)
-    ends = (start, even, odd)
+    speeds = (v, ve, vo)
     f, ftails, tails = call(
         lambda *refs: first_kernel(nstrips, *refs),
         (packet, f32(16, cols), f32(16 * len(DEEP), cols)),
         [SMEM] + [VMEM] * 8,
-        ids, *ends, *statics, second, first,
+        ids, u, ue, uo, *statics, second, first,
     )
     pe, po = swap(f, GZ, nz * nx)
     h, htails, inner = call(
         lambda *refs: beside_kernel(nstrips, *refs),
         (packet, f32(16, cols), f32(comps, rows + 8, cols)),
         [SMEM] * 2 + [VMEM] * 9,
-        ids, marks, *ends, f, ftails, *statics, tails,
+        ids, marks, *speeds, f, ftails, *statics, tails,
         cost_estimate=side_by_side,
     )
     he, ho = swap(h, GZ, nz * nx)
@@ -453,7 +455,7 @@
         lambda *refs: third_kernel(nstrips, *refs),
         (f32(4 * comps, rows, cols), f32(4 * comps, rows, cols), f32(1, 128)),
         [SMEM] * 3 + [VMEM] * 17,
-        ids, dts, marks, *ends, f, ftails, pe, po, h, htails, he, ho, g, gtails, *statics, tails,
+        ids, dts, marks, *speeds, f, ftails, pe, po, h, htails, he, ho, g, gtails, *statics, tails,
         cost_estimate=side_by_side,
     )
     f2, sums = call(
@@ -469,8 +471,8 @@
     pos, vel = call(
         last_kernel,
         (core, core),
-        [SMEM] * 2 + [VMEM] * 7,
-        dts, marks, sums, start, f, h, g, known, f2,
+        [SMEM] * 2 + [VMEM] * 8,
+        dts, marks, sums, u, v, f, h, g, known, f2,
         out_specs=(ANY, ANY),
         scratch_shapes=[pltpu.VMEM((2, comps, rows, cols), jnp.float32), pltpu.SemaphoreType.DMA((2, comps))],
     )

time: 96.9 us -> 99.2 us (1.024)
  starting transfers between devices: 34.7 us -> 39.6 us
  waiting for transfers between devices: 6.98 us -> 4.9 us
    ppermute x5 -> x6, starting transfers between devices: 25.2 us -> 30.8 us  [swap(): lax.ppermute(values[0], axes, first)]
    ppermute x5 -> x6, waiting for transfers between devices: 6.48 us -> 4.41 us  [swap(): lax.ppermute(values[0], axes, first)]
    ppermute x5 -> x6, starting transfers between devices: 9.48 us -> 8.76 us  [swap(): lax.ppermute(values[1], axes, second)]
  transfers between devices with their start and end apart: 10 -> 12, of which waited for: 4 -> 4; matrix products, arithmetic and copies ran while one was open for 1% -> 1% of each run, Pallas kernels for 4% -> 6%
where the time goes in v7:
time: 99.2 us; the launch traced here: 98.6 us
  blocking collectives  42.3 us (43%)
  starting transfers between devices  39.6 us (40%)
  Pallas kernels  9.44 us (10%)
  waiting for transfers between devices  4.9 us (5%)
  local copies, waits for them, and re-layouts  1.21 us (1%)
    ppermute x6, starting transfers between devices, swap(): lax.ppermute(values[0], axes, first)  30.8 us
    all_to_all x1, blocking collectives, local(): sums = lax.all_to_all(jnp.broadcast_to(sums, (nz, 1, 128)), 'z', 0, 0)  26.3 us
    all_to_all x1, blocking collectives, local(): lax.all_to_all(jnp.broadcast_to(sums, (near, 1, 128)), ('x', 'strip'), 0, 0)  16 us
    pallas_call x8, Pallas kernels, call(): pl.pallas_call(kernel, out_shape=out_shape, in_specs=specs, out_specs=out...  9.44 us
    ppermute x6, starting transfers between devices, swap(): lax.ppermute(values[1], axes, second)  8.76 us
    ppermute x6, waiting for transfers between devices, swap(): lax.ppermute(values[0], axes, first)  4.41 us
  transfers between devices with their start and end apart: 12, of which 4 were waited for; matrix products, arithmetic and copies ran while one was open for 1% of the time, Pallas kernels for 6%

profile of v7, /device:TPU:1, one launch (start us, length us, event | category | flops | bytes accessed | tf_op | source)
XLA Modules:
  0.0 98.6 jit_solution(5586924362381327432)
XLA Ops:
  0.6 0.7 collective-permute-start.3
  1.3 6.4 %collective-permute-start.2 = (f32[64,640]{1,0:T(8,128)}, f32[64,640]{1,0:T(8,128)S(1)}, u32[]{:S(2)}, u32[]{:S(2)}) collective-permute-start(f32[64,640]{1,0:T(8,128)} %bitcast.20), channel_id=1, source_target_pairs={{0,8},{8,0},{16,24},{24,16},{32,40},{40,32},{48,56},{56,48},{64,72... | collective-permute-start | bytes 491528 | tf_op jit(solution)/shard_map/ppermute | solution.py:20
  7.7 1.7 %shard_map.86.v.refs_2_.refs_3_ = f32[72,640]{1,0:T(8,128)} custom-call(s32[3]{0:T(128)} %bitcast.27, f32[64,640]{1,0:T(8,128)} %bitcast.25), custom_call_target="tpu_custom_call" | custom-call | tf_op jit(solution)/shard_map/pallas_call | solution.py:380
  9.4 0.7 collective-permute-start.1
  10.1 5.6 %collective-permute-start = (f32[72,640]{1,0:T(8,128)}, f32[72,640]{1,0:T(8,128)S(1)}, u32[]{:S(2)}, u32[]{:S(2)}) collective-permute-start(f32[72,640]{1,0:T(8,128)} %shard_map.86.v.refs_2_.refs_3_), channel_id=1, source_target_pairs={{0,8},{8,0},{16,24},{24,16},{32,40},{40,32},{48,56},{56,48},{64,72... | collective-permute-start | bytes 552968 | tf_op jit(solution)/shard_map/ppermute | solution.py:20
  15.9 0.8 copy-done.3
  16.9 2.3 %collective-permute-done.ve.refs_3_.refs_4_ = f32[72,640]{1,0:T(8,128)S(1)} collective-permute-done((f32[72,640]{1,0:T(8,128)}, f32[72,640]{1,0:T(8,128)S(1)}, u32[]{:S(2)}, u32[]{:S(2)}) %collective-permute-start) | collective-permute-done | bytes 184352 | tf_op jit(solution)/shard_map/ppermute | solution.py:20
  19.3 5.4 %collective-permute-start.4 = (f32[48,640]{1,0:T(8,128)S(1)}, f32[48,640]{1,0:T(8,128)S(1)}, u32[]{:S(2)}, u32[]{:S(2)}) collective-permute-start(f32[48,640]{1,0:T(8,128)S(1)} %get-tuple-element.19), channel_id=1, source_target_pairs={{1,2},{2,1},{3,4},{4,3},{5,6},{6,5},{9,10},{10,9},{11,12},{12,11},... | collective-permute-start | bytes 368648 | tf_op jit(solution)/shard_map/ppermute | solution.py:20
  24.7 1.9 %collective-permute-start.5 = (f32[48,640]{1,0:T(8,128)S(1)}, f32[48,640]{1,0:T(8,128)S(1)}, u32[]{:S(2)}, u32[]{:S(2)}) collective-permute-start(f32[48,640]{1,0:T(8,128)S(1)} %get-tuple-element.20), channel_id=1, source_target_pairs={{0,1},{1,0},{2,3},{3,2},{4,5},{5,4},{6,7},{7,6},{8,9},{9,8},{10,11... | collective-permute-start | bytes 368648 | tf_op jit(solution)/shard_map/ppermute | solution.py:20
  27.2 0.7 collective-permute-done.5.refs_8_
  28.5 0.7 collective-permute-start.7
  29.2 5.6 %collective-permute-start.6 = (f32[72,640]{1,0:T(8,128)S(1)}, f32[72,640]{1,0:T(8,128)S(1)}, u32[]{:S(2)}, u32[]{:S(2)}) collective-permute-start(f32[72,640]{1,0:T(8,128)S(1)} %get-tuple-element.21.refs_5_.refs_6_.f), channel_id=1, source_target_pairs={{0,8},{8,0},{16,24},{24,16},{32,40},{40,32},{48,56},{56,48},{64,72... | collective-permute-start | bytes 552968 | tf_op jit(solution)/shard_map/ppermute | solution.py:20
  34.9 1.1 %shard_map.89 = (f32[72,640]{1,0:T(8,128)S(1)}, f32[16,640]{1,0:T(8,128)S(1)}, f32[2,40,640]{2,1,0:T(8,128)S(1)}) custom-call(s32[1]{0:T(128)} %bitcast.2.ids.refs_0_, f32[9]{0:T(128)S(1)} %pad_maximum_fusion.refs_1_.refs_2_.marks, f32[72,640]{1,0:T(8,128)S(1)} %copy-done, f32[72,640]{1,0:T(8,128)S(1)} %collective-permute-done.ve.refs_3_.refs_4_, ...), custom_call_target="tpu_custom_call" | custom-call | flops 4000000 | bytes 3000000 | tf_op jit(solution)/shard_map/pallas_call | solution.py:380
  36.0 0.7 collective-permute-start.9
  36.7 5.8 %collective-permute-start.8 = (f32[72,640]{1,0:T(8,128)S(1)}, f32[72,640]{1,0:T(8,128)S(1)}, u32[]{:S(2)}, u32[]{:S(2)}) collective-permute-start(f32[72,640]{1,0:T(8,128)S(1)} %get-tuple-element.24.refs_10_.h), channel_id=1, source_target_pairs={{0,8},{8,0},{16,24},{24,16},{32,40},{40,32},{48,56},{56,48},{64,72... | collective-permute-start | bytes 552968 | tf_op jit(solution)/shard_map/ppermute | solution.py:20
  42.5 0.9 shard_map.90
  43.4 0.7 collective-permute-start.11
  44.1 5.6 %collective-permute-start.10 = (f32[72,640]{1,0:T(8,128)S(1)}, f32[72,640]{1,0:T(8,128)S(1)}, u32[]{:S(2)}, u32[]{:S(2)}) collective-permute-start(f32[72,640]{1,0:T(8,128)S(1)} %get-tuple-element.27.refs_14_.g), channel_id=1, source_target_pairs={{0,8},{8,0},{16,24},{24,16},{32,40},{40,32},{48,56},{56,48},{64,72... | collective-permute-start | bytes 552968 | tf_op jit(solution)/shard_map/ppermute | solution.py:20
  49.7 2.0 %shard_map.91 = (f32[8,32,640]{2,1,0:T(8,128)S(1)}, f32[8,32,640]{2,1,0:T(8,128)S(1)}, f32[1,128]{1,0:T(1,128)S(1)}) custom-call(s32[1]{0:T(128)} %bitcast.2.ids.refs_0_, f32[3]{0:T(128)S(1)} %power_multiply_fusion.refs_1_.dts, f32[9]{0:T(128)S(1)} %pad_maximum_fusion.refs_1_.refs_2_.marks, f32[72,640]{1,0:T(8,128)S(1)} %copy-done, ...), custom_call_target="tpu_custom_call" | custom-call | flops 4000000 | bytes 3000000 | tf_op jit(solution)/shard_map/pallas_call | solution.py:380
  51.7 1.4 %collective-permute-done.10.refs_6_ = f32[72,640]{1,0:T(8,128)S(1)} collective-permute-done((f32[72,640]{1,0:T(8,128)S(1)}, f32[72,640]{1,0:T(8,128)S(1)}, u32[]{:S(2)}, u32[]{:S(2)}) %collective-permute-start.10) | collective-permute-done | bytes 184352 | tf_op jit(solution)/shard_map/ppermute | solution.py:20
  53.2 1.1 %shard_map.92 = (f32[4,32,640]{2,1,0:T(8,128)S(1)}, f32[1,128]{1,0:T(1,128)S(1)}) custom-call(s32[1]{0:T(128)} %bitcast.2.ids.refs_0_, f32[3]{0:T(128)S(1)} %power_multiply_fusion.refs_1_.dts, f32[9]{0:T(128)S(1)} %pad_maximum_fusion.refs_1_.refs_2_.marks, f32[8,32,640]{2,1,0:T(8,128)S(1)} %get-tuple-element.29.refs_3_.known, ...), custom_call_target="tpu_custom_call" | custom-call | tf_op jit(solution)/shard_map/pallas_call | solution.py:380
  54.3 16.0 %all_to_all.10 = f32[32,1,128]{2,1,0:T(1,128)S(1)} all-to-all(f32[32,1,128]{2,1,0:T(1,128)S(1)} %broadcast_in_dim.13), channel_id=1, replica_groups=mesh['z'=16,'x'=4,'strip'=8] {'x','strip'}, dimensions={0} | all-to-all | bytes 32768 | tf_op jit(solution)/shard_map/all_to_all | solution.py:468
  70.3 26.3 %all_to_all.11.parts = f32[16,1,128]{2,1,0:T(1,128)S(1)} all-to-all(f32[16,1,128]{2,1,0:T(1,128)S(1)} %broadcast_in_dim.14), channel_id=1, replica_groups=mesh['z'=16,'x'=4,'strip'=8] {'z'}, dimensions={0} | all-to-all | bytes 16384 | tf_op jit(solution)/shard_map/all_to_all | solution.py:470
  96.6 2.0 %shard_map.93 = (f32[2,32,640]{2,1,0:T(8,128)}, f32[2,32,640]{2,1,0:T(8,128)}) custom-call(f32[3]{0:T(128)S(1)} %power_multiply_fusion.refs_1_.dts, f32[9]{0:T(128)S(1)} %pad_maximum_fusion.refs_1_.refs_2_.marks, f32[16,1,128]{2,1,0:T(1,128)S(1)} %all_to_all.11.parts, f32[64,640]{1,0:T(8,128)S(1)} %bitcast.23, f32[72,640]{1,0:T(8,128)S(1)} %copy-done, ...), custom_call_target="tpu_custom_call" | custom-call | tf_op jit(solution)/shard_map/pallas_call | solution.py:380
  (36 shorter events, 1.8 us)
Async XLA Ops:
  0.6 16.2 %collective-permute-start.3 = (f32[64,640]{1,0:T(8,128)}, f32[64,640]{1,0:T(8,128)S(1)}, u32[]{:S(2)}, u32[]{:S(2)}) collective-permute-start(f32[64,640]{1,0:T(8,128)} %bitcast.19), channel_id=1, source_target_pairs={{8,16},{16,8},{24,32},{32,24},{40,48},{48,40},{56,64},{64,56},{72,... | collective-permute-start | bytes 491528 | tf_op jit(solution)/shard_map/ppermute | solution.py:20
  1.3 15.6 %collective-permute-start.2 = (f32[64,640]{1,0:T(8,128)}, f32[64,640]{1,0:T(8,128)S(1)}, u32[]{:S(2)}, u32[]{:S(2)}) collective-permute-start(f32[64,640]{1,0:T(8,128)} %bitcast.20), channel_id=1, source_target_pairs={{0,8},{8,0},{16,24},{24,16},{32,40},{40,32},{48,56},{56,48},{64,72... | collective-permute-start | bytes 491528 | tf_op jit(solution)/shard_map/ppermute | solution.py:20
  7.7 8.1 %copy-start.2 = (s32[2,1,32,640]{3,2,1,0:T(8,128)S(1)}, s32[2,1,32,640]{3,2,1,0:T(8,128)}, u32[]{:S(2)}) copy-start(s32[2,1,32,640]{3,2,1,0:T(8,128)} %param.11) | copy-start | bytes 491524
  9.4 7.5 %collective-permute-start.1 = (f32[72,640]{1,0:T(8,128)}, f32[72,640]{1,0:T(8,128)S(1)}, u32[]{:S(2)}, u32[]{:S(2)}) collective-permute-start(f32[72,640]{1,0:T(8,128)} %shard_map.86.v.refs_2_.refs_3_), channel_id=1, source_target_pairs={{8,16},{16,8},{24,32},{32,24},{40,48},{48,40},{56,64},{64,56},{72,... | collective-permute-start | bytes 552968 | tf_op jit(solution)/shard_map/ppermute | solution.py:20
  10.1 9.1 %collective-permute-start = (f32[72,640]{1,0:T(8,128)}, f32[72,640]{1,0:T(8,128)S(1)}, u32[]{:S(2)}, u32[]{:S(2)}) collective-permute-start(f32[72,640]{1,0:T(8,128)} %shard_map.86.v.refs_2_.refs_3_), channel_id=1, source_target_pairs={{0,8},{8,0},{16,24},{24,16},{32,40},{40,32},{48,56},{56,48},{64,72... | collective-permute-start | bytes 552968 | tf_op jit(solution)/shard_map/ppermute | solution.py:20
  15.8 0.9 copy-start.3
  15.8 1.0 %copy-start.4 = (f32[1,2,32,640]{3,2,1,0:T(8,128)S(1)}, f32[1,2,32,640]{3,2,1,0:T(8,128)}, u32[]{:S(2)}) copy-start(f32[1,2,32,640]{3,2,1,0:T(8,128)} %param.9) | copy-start | bytes 491524
  16.8 2.4 %copy-start.1 = (f32[1,2,32,640]{3,2,1,0:T(8,128)S(1)}, f32[1,2,32,640]{3,2,1,0:T(8,128)}, u32[]{:S(2)}) copy-start(f32[1,2,32,640]{3,2,1,0:T(8,128)} %param.7) | copy-start | bytes 491524
  16.8 2.4 %copy-start = (f32[72,640]{1,0:T(8,128)S(1)}, f32[72,640]{1,0:T(8,128)}, u32[]{:S(2)}) copy-start(f32[72,640]{1,0:T(8,128)} %shard_map.86.v.refs_2_.refs_3_) | copy-start | bytes 552964
  19.3 7.3 %copy-start.5 = (s32[3,1]{0,1:T(1,128)S(1)}, s32[3,1]{0,1:T(1,128)}, u32[]{:S(2)}) copy-start(s32[3,1]{0,1:T(1,128)} %param.12) | copy-start | bytes 40
  19.3 8.0 %collective-permute-start.4 = (f32[48,640]{1,0:T(8,128)S(1)}, f32[48,640]{1,0:T(8,128)S(1)}, u32[]{:S(2)}, u32[]{:S(2)}) collective-permute-start(f32[48,640]{1,0:T(8,128)S(1)} %get-tuple-element.19), channel_id=1, source_target_pairs={{1,2},{2,1},{3,4},{4,3},{5,6},{6,5},{9,10},{10,9},{11,12},{12,11},... | collective-permute-start | bytes 368648 | tf_op jit(solution)/shard_map/ppermute | solution.py:20
  24.7 3.2 %collective-permute-start.5 = (f32[48,640]{1,0:T(8,128)S(1)}, f32[48,640]{1,0:T(8,128)S(1)}, u32[]{:S(2)}, u32[]{:S(2)}) collective-permute-start(f32[48,640]{1,0:T(8,128)S(1)} %get-tuple-element.20), channel_id=1, source_target_pairs={{0,1},{1,0},{2,3},{3,2},{4,5},{5,4},{6,7},{7,6},{8,9},{9,8},{10,11... | collective-permute-start | bytes 368648 | tf_op jit(solution)/shard_map/ppermute | solution.py:20
  28.5 14.0 %collective-permute-start.7 = (f32[72,640]{1,0:T(8,128)S(1)}, f32[72,640]{1,0:T(8,128)S(1)}, u32[]{:S(2)}, u32[]{:S(2)}) collective-permute-start(f32[72,640]{1,0:T(8,128)S(1)} %get-tuple-element.21.refs_5_.refs_6_.f), channel_id=1, source_target_pairs={{8,16},{16,8},{24,32},{32,24},{40,48},{48,40},{56,64},{64,56},{72,... | collective-permute-start | bytes 552968 | tf_op jit(solution)/shard_map/ppermute | solution.py:20
  29.2 13.3 %collective-permute-start.6 = (f32[72,640]{1,0:T(8,128)S(1)}, f32[72,640]{1,0:T(8,128)S(1)}, u32[]{:S(2)}, u32[]{:S(2)}) collective-permute-start(f32[72,640]{1,0:T(8,128)S(1)} %get-tuple-element.21.refs_5_.refs_6_.f), channel_id=1, source_target_pairs={{0,8},{8,0},{16,24},{24,16},{32,40},{40,32},{48,56},{56,48},{64,72... | collective-permute-start | bytes 552968 | tf_op jit(solution)/shard_map/ppermute | solution.py:20
  36.0 13.6 %collective-permute-start.9 = (f32[72,640]{1,0:T(8,128)S(1)}, f32[72,640]{1,0:T(8,128)S(1)}, u32[]{:S(2)}, u32[]{:S(2)}) collective-permute-start(f32[72,640]{1,0:T(8,128)S(1)} %get-tuple-element.24.refs_10_.h), channel_id=1, source_target_pairs={{8,16},{16,8},{24,32},{32,24},{40,48},{48,40},{56,64},{64,56},{72,... | collective-permute-start | bytes 552968 | tf_op jit(solution)/shard_map/ppermute | solution.py:20
  36.7 13.0 %collective-permute-start.8 = (f32[72,640]{1,0:T(8,128)S(1)}, f32[72,640]{1,0:T(8,128)S(1)}, u32[]{:S(2)}, u32[]{:S(2)}) collective-permute-start(f32[72,640]{1,0:T(8,128)S(1)} %get-tuple-element.24.refs_10_.h), channel_id=1, source_target_pairs={{0,8},{8,0},{16,24},{24,16},{32,40},{40,32},{48,56},{56,48},{64,72... | collective-permute-start | bytes 552968 | tf_op jit(solution)/shard_map/ppermute | solution.py:20
  43.4 6.3 %copy-start.6 = (s32[3]{0:T(128)S(1)}, s32[3]{0:T(128)}, u32[]{:S(2)}) copy-start(s32[3]{0:T(128)} %param.13) | copy-start | bytes 40
  43.4 8.3 %collective-permute-start.11 = (f32[72,640]{1,0:T(8,128)S(1)}, f32[72,640]{1,0:T(8,128)S(1)}, u32[]{:S(2)}, u32[]{:S(2)}) collective-permute-start(f32[72,640]{1,0:T(8,128)S(1)} %get-tuple-element.27.refs_14_.g), channel_id=1, source_target_pairs={{8,16},{16,8},{24,32},{32,24},{40,48},{48,40},{56,64},{64,56},{72,... | collective-permute-start | bytes 552968 | tf_op jit(solution)/shard_map/ppermute | solution.py:20
  44.1 9.1 %collective-permute-start.10 = (f32[72,640]{1,0:T(8,128)S(1)}, f32[72,640]{1,0:T(8,128)S(1)}, u32[]{:S(2)}, u32[]{:S(2)}) collective-permute-start(f32[72,640]{1,0:T(8,128)S(1)} %get-tuple-element.27.refs_14_.g), channel_id=1, source_target_pairs={{0,8},{8,0},{16,24},{24,16},{32,40},{40,32},{48,56},{56,48},{64,72... | collective-permute-start | bytes 552968 | tf_op jit(solution)/shard_map/ppermute | solution.py:20

commit v8 on v5

--- a/solution.py
+++ b/solution.py
@@ -462,10 +462,10 @@
         [SMEM] * 3 + [VMEM] * 9,
         ids, dts, marks, known, w2, early, ge, go, *statics, tails,
     )
+    sums = lax.all_to_all(jnp.broadcast_to(sums, (nz, 1, 128)), "z", 0, 0)
+    sums = jnp.sum(sums, axis=0)
     near = nx * nstrips
     sums = lax.all_to_all(jnp.broadcast_to(sums, (near, 1, 128)), ("x", "strip"), 0, 0)
-    sums = jnp.sum(sums, axis=0)
-    sums = lax.all_to_all(jnp.broadcast_to(sums, (nz, 1, 128)), "z", 0, 0)
     pos, vel = call(
         last_kernel,
         (core, core),

time: 96.9 us -> 98.3 us (1.014)
  blocking collectives: 42.6 us -> 44 us
    all_to_all x1, blocking collectives: 25.8 us -> 28.7 us  [local(): sums = lax.all_to_all(jnp.broadcast_to(sums, (nz, 1, 128)), 'z', 0, 0)]
    all_to_all x1, blocking collectives: 16.8 us -> 15.3 us  [local(): lax.all_to_all(jnp.broadcast_to(sums, (near, 1, 128)), ('x', 'strip'), 0, 0)]
where the time goes in v8:
time: 98.3 us; the launch traced here: 97.8 us
  blocking collectives  44 us (45%)
  starting transfers between devices  34.7 us (35%)
  Pallas kernels  9.68 us (10%)
  waiting for transfers between devices  6.98 us (7%)
  local copies, waits for them, and re-layouts  1.23 us (1%)
    all_to_all x1, blocking collectives, local(): sums = lax.all_to_all(jnp.broadcast_to(sums, (nz, 1, 128)), 'z', 0, 0)  28.7 us
    ppermute x5, starting transfers between devices, swap(): lax.ppermute(values[0], axes, first)  25.2 us
    all_to_all x1, blocking collectives, local(): lax.all_to_all(jnp.broadcast_to(sums, (near, 1, 128)), ('x', 'strip'), 0, 0)  15.3 us
    pallas_call x8, Pallas kernels, call(): pl.pallas_call(kernel, out_shape=out_shape, in_specs=specs, out_specs=out...  9.68 us
    ppermute x5, starting transfers between devices, swap(): lax.ppermute(values[1], axes, second)  9.48 us
    ppermute x5, waiting for transfers between devices, swap(): lax.ppermute(values[0], axes, first)  6.48 us
  transfers between devices with their start and end apart: 10, of which 4 were waited for; matrix products, arithmetic and copies ran while one was open for 1% of the time, Pallas kernels for 4%

profile of v8, /device:TPU:1, one launch (start us, length us, event | category | flops | bytes accessed | tf_op | source)
XLA Modules:
  0.0 97.8 jit_solution(13142363349809546062)
XLA Ops:
  0.6 1.8 %shard_map.86.start.refs_1_.refs_2_.refs_3_ = f32[136,640]{1,0:T(8,128)} custom-call(s32[3]{0:T(128)} %bitcast.23, f32[64,640]{1,0:T(8,128)} %bitcast.20, f32[64,640]{1,0:T(8,128)} %bitcast.21), custom_call_target="tpu_custom_call" | custom-call | tf_op jit(solution)/shard_map/pallas_call | solution.py:380
  2.4 0.7 collective-permute-start.1
  3.1 6.4 %collective-permute-start = (f32[136,640]{1,0:T(8,128)}, f32[136,640]{1,0:T(8,128)S(1)}, u32[]{:S(2)}, u32[]{:S(2)}) collective-permute-start(f32[136,640]{1,0:T(8,128)} %shard_map.86.start.refs_1_.refs_2_.refs_3_), channel_id=1, source_target_pairs={{0,8},{8,0},{16,24},{24,16},{32,40},{40,32},{48,56},{56,48},{64,72... | collective-permute-start | bytes 1044488 | tf_op jit(solution)/shard_map/ppermute | solution.py:20
  9.8 0.9 copy-done.2
  10.7 4.4 %collective-permute-done.even.refs_2_.refs_3_.refs_4_ = f32[136,640]{1,0:T(8,128)S(1)} collective-permute-done((f32[136,640]{1,0:T(8,128)}, f32[136,640]{1,0:T(8,128)S(1)}, u32[]{:S(2)}, u32[]{:S(2)}) %collective-permute-start) | collective-permute-done | bytes 348192 | tf_op jit(solution)/shard_map/ppermute | solution.py:20
  15.2 6.8 %collective-permute-start.2 = (f32[48,640]{1,0:T(8,128)S(1)}, f32[48,640]{1,0:T(8,128)S(1)}, u32[]{:S(2)}, u32[]{:S(2)}) collective-permute-start(f32[48,640]{1,0:T(8,128)S(1)} %get-tuple-element.19), channel_id=1, source_target_pairs={{1,2},{2,1},{3,4},{4,3},{5,6},{6,5},{9,10},{10,9},{11,12},{12,11},... | collective-permute-start | bytes 368648 | tf_op jit(solution)/shard_map/ppermute | solution.py:20
  22.0 1.9 %collective-permute-start.3 = (f32[48,640]{1,0:T(8,128)S(1)}, f32[48,640]{1,0:T(8,128)S(1)}, u32[]{:S(2)}, u32[]{:S(2)}) collective-permute-start(f32[48,640]{1,0:T(8,128)S(1)} %get-tuple-element.20), channel_id=1, source_target_pairs={{0,1},{1,0},{2,3},{3,2},{4,5},{5,4},{6,7},{7,6},{8,9},{9,8},{10,11... | collective-permute-start | bytes 368648 | tf_op jit(solution)/shard_map/ppermute | solution.py:20
  24.1 0.5 collective-permute-done.2.refs_7_
  24.6 0.7 collective-permute-done.3.refs_8_
  25.2 0.6 shard_map.88
  25.9 0.7 collective-permute-start.5
  26.5 5.6 %collective-permute-start.4 = (f32[72,640]{1,0:T(8,128)S(1)}, f32[72,640]{1,0:T(8,128)S(1)}, u32[]{:S(2)}, u32[]{:S(2)}) collective-permute-start(f32[72,640]{1,0:T(8,128)S(1)} %get-tuple-element.21.refs_5_.refs_6_.f), channel_id=1, source_target_pairs={{0,8},{8,0},{16,24},{24,16},{32,40},{40,32},{48,56},{56,48},{64,72... | collective-permute-start | bytes 552968 | tf_op jit(solution)/shard_map/ppermute | solution.py:20
  32.4 1.1 %shard_map.89 = (f32[72,640]{1,0:T(8,128)S(1)}, f32[16,640]{1,0:T(8,128)S(1)}, f32[2,40,640]{2,1,0:T(8,128)S(1)}) custom-call(s32[1]{0:T(128)} %bitcast.3.ids.refs_0_, f32[9]{0:T(128)S(1)} %pad_maximum_fusion.refs_1_.refs_2_.marks, f32[136,640]{1,0:T(8,128)S(1)} %copy-done, f32[136,640]{1,0:T(8,128)S(1)} %collective-permute-done.even.refs_2_.refs_3_.refs_4_, ...), custom_call_target="tpu_custom_call" | custom-call | flops 4000000 | bytes 3000000 | tf_op jit(solution)/shard_map/pallas_call | solution.py:380
  33.5 0.7 collective-permute-start.7
  34.2 6.6 %collective-permute-start.6 = (f32[72,640]{1,0:T(8,128)S(1)}, f32[72,640]{1,0:T(8,128)S(1)}, u32[]{:S(2)}, u32[]{:S(2)}) collective-permute-start(f32[72,640]{1,0:T(8,128)S(1)} %get-tuple-element.24.refs_10_.h), channel_id=1, source_target_pairs={{0,8},{8,0},{16,24},{24,16},{32,40},{40,32},{48,56},{56,48},{64,72... | collective-permute-start | bytes 552968 | tf_op jit(solution)/shard_map/ppermute | solution.py:20
  40.8 0.9 shard_map.90
  41.7 0.7 collective-permute-start.9
  42.4 4.7 %collective-permute-start.8 = (f32[72,640]{1,0:T(8,128)S(1)}, f32[72,640]{1,0:T(8,128)S(1)}, u32[]{:S(2)}, u32[]{:S(2)}) collective-permute-start(f32[72,640]{1,0:T(8,128)S(1)} %get-tuple-element.27.refs_14_.g), channel_id=1, source_target_pairs={{0,8},{8,0},{16,24},{24,16},{32,40},{40,32},{48,56},{56,48},{64,72... | collective-permute-start | bytes 552968 | tf_op jit(solution)/shard_map/ppermute | solution.py:20
  47.1 2.1 %shard_map.91 = (f32[8,32,640]{2,1,0:T(8,128)S(1)}, f32[8,32,640]{2,1,0:T(8,128)S(1)}, f32[1,128]{1,0:T(1,128)S(1)}) custom-call(s32[1]{0:T(128)} %bitcast.3.ids.refs_0_, f32[3]{0:T(128)S(1)} %power_multiply_fusion.refs_1_.dts, f32[9]{0:T(128)S(1)} %pad_maximum_fusion.refs_1_.refs_2_.marks, f32[136,640]{1,0:T(8,128)S(1)} %copy-done, ...), custom_call_target="tpu_custom_call" | custom-call | flops 4000000 | bytes 3000000 | tf_op jit(solution)/shard_map/pallas_call | solution.py:380
  49.2 1.4 %collective-permute-done.8.refs_6_ = f32[72,640]{1,0:T(8,128)S(1)} collective-permute-done((f32[72,640]{1,0:T(8,128)S(1)}, f32[72,640]{1,0:T(8,128)S(1)}, u32[]{:S(2)}, u32[]{:S(2)}) %collective-permute-start.8) | collective-permute-done | bytes 184352 | tf_op jit(solution)/shard_map/ppermute | solution.py:20
  50.6 1.1 %shard_map.92 = (f32[4,32,640]{2,1,0:T(8,128)S(1)}, f32[1,128]{1,0:T(1,128)S(1)}) custom-call(s32[1]{0:T(128)} %bitcast.3.ids.refs_0_, f32[3]{0:T(128)S(1)} %power_multiply_fusion.refs_1_.dts, f32[9]{0:T(128)S(1)} %pad_maximum_fusion.refs_1_.refs_2_.marks, f32[8,32,640]{2,1,0:T(8,128)S(1)} %get-tuple-element.29.refs_3_.known, ...), custom_call_target="tpu_custom_call" | custom-call | tf_op jit(solution)/shard_map/pallas_call | solution.py:380
  51.8 28.7 %all_to_all.10 = f32[16,1,128]{2,1,0:T(1,128)S(1)} all-to-all(f32[16,1,128]{2,1,0:T(1,128)S(1)} %broadcast_in_dim.13), channel_id=1, replica_groups=mesh['z'=16,'x'=4,'strip'=8] {'z'}, dimensions={0} | all-to-all | bytes 16384 | tf_op jit(solution)/shard_map/all_to_all | solution.py:465
  80.5 15.3 %all_to_all.11.parts = f32[32,1,128]{2,1,0:T(1,128)S(1)} all-to-all(f32[32,1,128]{2,1,0:T(1,128)S(1)} %broadcast_in_dim.14), channel_id=1, replica_groups=mesh['z'=16,'x'=4,'strip'=8] {'x','strip'}, dimensions={0} | all-to-all | bytes 32768 | tf_op jit(solution)/shard_map/all_to_all | solution.py:468
  95.8 2.0 %shard_map.93 = (f32[2,32,640]{2,1,0:T(8,128)}, f32[2,32,640]{2,1,0:T(8,128)}) custom-call(f32[3]{0:T(128)S(1)} %power_multiply_fusion.refs_1_.dts, f32[9]{0:T(128)S(1)} %pad_maximum_fusion.refs_1_.refs_2_.marks, f32[32,1,128]{2,1,0:T(1,128)S(1)} %all_to_all.11.parts, f32[136,640]{1,0:T(8,128)S(1)} %copy-done, ...), custom_call_target="tpu_custom_call" | custom-call | tf_op jit(solution)/shard_map/pallas_call | solution.py:380
  (30 shorter events, 0.8 us)
Async XLA Ops:
  0.6 9.0 %copy-start.1 = (s32[2,1,32,640]{3,2,1,0:T(8,128)S(1)}, s32[2,1,32,640]{3,2,1,0:T(8,128)}, u32[]{:S(2)}) copy-start(s32[2,1,32,640]{3,2,1,0:T(8,128)} %param.11) | copy-start | bytes 491524
  2.4 8.3 %collective-permute-start.1 = (f32[136,640]{1,0:T(8,128)}, f32[136,640]{1,0:T(8,128)S(1)}, u32[]{:S(2)}, u32[]{:S(2)}) collective-permute-start(f32[136,640]{1,0:T(8,128)} %shard_map.86.start.refs_1_.refs_2_.refs_3_), channel_id=1, source_target_pairs={{8,16},{16,8},{24,32},{32,24},{40,48},{48,40},{56,64},{64,56},{72,... | collective-permute-start | bytes 1044488 | tf_op jit(solution)/shard_map/ppermute | solution.py:20
  3.1 12.0 %collective-permute-start = (f32[136,640]{1,0:T(8,128)}, f32[136,640]{1,0:T(8,128)S(1)}, u32[]{:S(2)}, u32[]{:S(2)}) collective-permute-start(f32[136,640]{1,0:T(8,128)} %shard_map.86.start.refs_1_.refs_2_.refs_3_), channel_id=1, source_target_pairs={{0,8},{8,0},{16,24},{24,16},{32,40},{40,32},{48,56},{56,48},{64,72... | collective-permute-start | bytes 1044488 | tf_op jit(solution)/shard_map/ppermute | solution.py:20
  9.7 0.9 copy-start.2
  9.7 1.0 %copy-start.3 = (f32[1,2,32,640]{3,2,1,0:T(8,128)S(1)}, f32[1,2,32,640]{3,2,1,0:T(8,128)}, u32[]{:S(2)}) copy-start(f32[1,2,32,640]{3,2,1,0:T(8,128)} %param.9) | copy-start | bytes 491524
  9.7 5.4 %copy-start = (f32[136,640]{1,0:T(8,128)S(1)}, f32[136,640]{1,0:T(8,128)}, u32[]{:S(2)}) copy-start(f32[136,640]{1,0:T(8,128)} %shard_map.86.start.refs_1_.refs_2_.refs_3_) | copy-start | bytes 1044484
  15.2 8.7 %copy-start.4 = (s32[3,1]{0,1:T(1,128)S(1)}, s32[3,1]{0,1:T(1,128)}, u32[]{:S(2)}) copy-start(s32[3,1]{0,1:T(1,128)} %param.12) | copy-start | bytes 40
  15.2 9.3 %collective-permute-start.2 = (f32[48,640]{1,0:T(8,128)S(1)}, f32[48,640]{1,0:T(8,128)S(1)}, u32[]{:S(2)}, u32[]{:S(2)}) collective-permute-start(f32[48,640]{1,0:T(8,128)S(1)} %get-tuple-element.19), channel_id=1, source_target_pairs={{1,2},{2,1},{3,4},{4,3},{5,6},{6,5},{9,10},{10,9},{11,12},{12,11},... | collective-permute-start | bytes 368648 | tf_op jit(solution)/shard_map/ppermute | solution.py:20
  22.0 3.2 %collective-permute-start.3 = (f32[48,640]{1,0:T(8,128)S(1)}, f32[48,640]{1,0:T(8,128)S(1)}, u32[]{:S(2)}, u32[]{:S(2)}) collective-permute-start(f32[48,640]{1,0:T(8,128)S(1)} %get-tuple-element.20), channel_id=1, source_target_pairs={{0,1},{1,0},{2,3},{3,2},{4,5},{5,4},{6,7},{7,6},{8,9},{9,8},{10,11... | collective-permute-start | bytes 368648 | tf_op jit(solution)/shard_map/ppermute | solution.py:20
  25.9 14.9 %collective-permute-start.5 = (f32[72,640]{1,0:T(8,128)S(1)}, f32[72,640]{1,0:T(8,128)S(1)}, u32[]{:S(2)}, u32[]{:S(2)}) collective-permute-start(f32[72,640]{1,0:T(8,128)S(1)} %get-tuple-element.21.refs_5_.refs_6_.f), channel_id=1, source_target_pairs={{8,16},{16,8},{24,32},{32,24},{40,48},{48,40},{56,64},{64,56},{72,... | collective-permute-start | bytes 552968 | tf_op jit(solution)/shard_map/ppermute | solution.py:20
  26.5 14.3 %collective-permute-start.4 = (f32[72,640]{1,0:T(8,128)S(1)}, f32[72,640]{1,0:T(8,128)S(1)}, u32[]{:S(2)}, u32[]{:S(2)}) collective-permute-start(f32[72,640]{1,0:T(8,128)S(1)} %get-tuple-element.21.refs_5_.refs_6_.f), channel_id=1, source_target_pairs={{0,8},{8,0},{16,24},{24,16},{32,40},{40,32},{48,56},{56,48},{64,72... | collective-permute-start | bytes 552968 | tf_op jit(solution)/shard_map/ppermute | solution.py:20
  33.5 13.6 %collective-permute-start.7 = (f32[72,640]{1,0:T(8,128)S(1)}, f32[72,640]{1,0:T(8,128)S(1)}, u32[]{:S(2)}, u32[]{:S(2)}) collective-permute-start(f32[72,640]{1,0:T(8,128)S(1)} %get-tuple-element.24.refs_10_.h), channel_id=1, source_target_pairs={{8,16},{16,8},{24,32},{32,24},{40,48},{48,40},{56,64},{64,56},{72,... | collective-permute-start | bytes 552968 | tf_op jit(solution)/shard_map/ppermute | solution.py:20
  34.2 13.0 %collective-permute-start.6 = (f32[72,640]{1,0:T(8,128)S(1)}, f32[72,640]{1,0:T(8,128)S(1)}, u32[]{:S(2)}, u32[]{:S(2)}) collective-permute-start(f32[72,640]{1,0:T(8,128)S(1)} %get-tuple-element.24.refs_10_.h), channel_id=1, source_target_pairs={{0,8},{8,0},{16,24},{24,16},{32,40},{40,32},{48,56},{56,48},{64,72... | collective-permute-start | bytes 552968 | tf_op jit(solution)/shard_map/ppermute | solution.py:20
  41.7 5.4 %copy-start.5 = (s32[3]{0:T(128)S(1)}, s32[3]{0:T(128)}, u32[]{:S(2)}) copy-start(s32[3]{0:T(128)} %param.13) | copy-start | bytes 40
  41.7 7.5 %collective-permute-start.9 = (f32[72,640]{1,0:T(8,128)S(1)}, f32[72,640]{1,0:T(8,128)S(1)}, u32[]{:S(2)}, u32[]{:S(2)}) collective-permute-start(f32[72,640]{1,0:T(8,128)S(1)} %get-tuple-element.27.refs_14_.g), channel_id=1, source_target_pairs={{8,16},{16,8},{24,32},{32,24},{40,48},{48,40},{56,64},{64,56},{72,... | collective-permute-start | bytes 552968 | tf_op jit(solution)/shard_map/ppermute | solution.py:20
  42.4 8.2 %collective-permute-start.8 = (f32[72,640]{1,0:T(8,128)S(1)}, f32[72,640]{1,0:T(8,128)S(1)}, u32[]{:S(2)}, u32[]{:S(2)}) collective-permute-start(f32[72,640]{1,0:T(8,128)S(1)} %get-tuple-element.27.refs_14_.g), channel_id=1, source_target_pairs={{0,8},{8,0},{16,24},{24,16},{32,40},{40,32},{48,56},{56,48},{64,72... | collective-permute-start | bytes 552968 | tf_op jit(solution)/shard_map/ppermute | solution.py:20
